TPU v7x, 512 devices: a whole 4x4x16 slice. The times are simulated.
512 devices in a mesh: dp: 8 (over x, y_hi), ctx: 64 (over z, y_lo, core).
Axes of the slice: x: 4, y: 4 (y_hi: 2, y_lo: 2; y = y_hi * 2 + y_lo), z: 16, core: 2. Of those that a mesh axis runs over, the one named last changes fastest.
Arguments:
- query_proj: bfloat16 [8, 8192, 512], P('dp', 'ctx'), may hold values from -6 to 6
- key_proj: bfloat16 [8, 8192, 512], P('dp', 'ctx'), may hold values from -6 to 6
- value_proj: bfloat16 [8, 8192, 512], P('dp', 'ctx'), may hold values from -6 to 6
- long_filter: float32 [8192, 512], P(None, 'ctx'), may hold values from -2 to 2
- grad_output: bfloat16 [8, 8192, 512], P('dp', 'ctx'), may hold values from -6 to 6
Outputs:
- gated_output: bfloat16 [8, 8192, 512], P('dp', 'ctx')
- grad_query: bfloat16 [8, 8192, 512], P('dp', 'ctx')
- grad_key: bfloat16 [8, 8192, 512], P('dp', 'ctx')
- grad_value: bfloat16 [8, 8192, 512], P('dp', 'ctx')
- grad_filter: float32 [8192, 512], P(None, 'ctx')
All inputs are finite; a program needn't handle non-finite values.
Results may differ from a plain program's by a relative error of at most 0.0057.
Values may be sent and summed in bfloat16 or wider, within the bound.
No kernel may reach another device: no remote copies, remote signals or barrier semaphores. Data moves between devices by JAX's collectives and lax.ppermute only.
A program may use at most 64 MiB of HBM per device.

v0:
```python
import math

import jax
import jax.numpy as jnp
from jax import lax
from jax.sharding import PartitionSpec as P

FACTOR = 128


HIGHEST = lax.Precision.HIGHEST


def dft_tables(length):
    index = jnp.arange(length, dtype=jnp.int32)
    product = index[:, None] * index[None, :] % length
    angle = 2.0 * math.pi / length * product.astype(jnp.float32)
    return (jnp.cos(angle), jnp.sin(angle))


def twiddle_tables(first, second):
    total = first * second
    rows = jnp.arange(first, dtype=jnp.int32)[:, None]
    cols = jnp.arange(second, dtype=jnp.int32)[None, :]
    angle = 2.0 * math.pi / total * (rows * cols % total).astype(jnp.float32)
    return (jnp.cos(angle), jnp.sin(angle))


def forward_transform(signal, tables):
    cos_one, sin_one, cos_two, sin_two, cos_turn, sin_turn = tables
    half = signal.shape[1]
    part_re = jnp.einsum("kn,cnm->ckm", cos_one[:, :half], signal, precision=HIGHEST)
    part_im = -jnp.einsum("kn,cnm->ckm", sin_one[:, :half], signal, precision=HIGHEST)
    turned_re = part_re * cos_turn + part_im * sin_turn
    turned_im = part_im * cos_turn - part_re * sin_turn
    spec_re = jnp.einsum("ckn,jn->ckj", turned_re, cos_two, precision=HIGHEST) + jnp.einsum(
        "ckn,jn->ckj", turned_im, sin_two, precision=HIGHEST
    )
    spec_im = jnp.einsum("ckn,jn->ckj", turned_im, cos_two, precision=HIGHEST) - jnp.einsum(
        "ckn,jn->ckj", turned_re, sin_two, precision=HIGHEST
    )
    return (spec_re, spec_im)


def inverse_transform(spec_re, spec_im, tables):
    cos_one, sin_one, cos_two, sin_two, cos_turn, sin_turn = tables
    first = cos_one.shape[0]
    second = cos_two.shape[0]
    half = first // 2
    back_re = jnp.einsum("ckj,nj->ckn", spec_re, cos_two, precision=HIGHEST) - jnp.einsum(
        "ckj,nj->ckn", spec_im, sin_two, precision=HIGHEST
    )
    back_im = jnp.einsum("ckj,nj->ckn", spec_im, cos_two, precision=HIGHEST) + jnp.einsum(
        "ckj,nj->ckn", spec_re, sin_two, precision=HIGHEST
    )
    turned_re = back_re * cos_turn - back_im * sin_turn
    turned_im = back_im * cos_turn + back_re * sin_turn
    signal = jnp.einsum("nk,ckm->cnm", cos_one[:half], turned_re, precision=HIGHEST) - jnp.einsum(
        "nk,ckm->cnm", sin_one[:half], turned_im, precision=HIGHEST
    )
    return signal * (1.0 / (first * second))


def on_device(query_proj, key_proj, value_proj, long_filter, grad_output):
    tok_count = query_proj.shape[1]
    width = query_proj.shape[2]
    groups = lax.axis_size("ctx")
    seqs = lax.axis_size("dp")
    seq_len = tok_count * groups
    share = width // groups
    first = FACTOR
    second = 2 * seq_len // first
    half = first // 2
    cos_one, sin_one = dft_tables(first)
    cos_two, sin_two = dft_tables(second)
    cos_turn, sin_turn = twiddle_tables(first, second)
    tables = (cos_one, sin_one, cos_two, sin_two, cos_turn, sin_turn)

    wide = jnp.float32
    mixed = (key_proj.astype(wide) * value_proj.astype(wide)).astype(jnp.bfloat16)[0]
    grad_mix = (grad_output.astype(wide) * query_proj.astype(wide)).astype(jnp.bfloat16)[0]
    both = jnp.stack([mixed.T.reshape(groups, share, tok_count), grad_mix.T.reshape(groups, share, tok_count)], axis=1)
    both = lax.all_to_all(both, "ctx", 0, 0)
    signal = both.transpose(1, 2, 0, 3).reshape(2 * share, half, second).astype(wide)

    filt_re, filt_im = forward_transform(long_filter.T.reshape(share, half, second), tables)
    spec_re, spec_im = forward_transform(signal, tables)
    mix_re, cot_re = spec_re[:share], spec_re[share:]
    mix_im, cot_im = spec_im[:share], spec_im[share:]
    factor = 1.0 / math.sqrt(seq_len * seqs)
    taps = inverse_transform(mix_re * cot_re + mix_im * cot_im, mix_re * cot_im - mix_im * cot_re, tables)
    taps = lax.all_to_all(taps.astype(jnp.bfloat16), "dp", 0, 0)

    prod_re = jnp.concatenate([filt_re * mix_re - filt_im * mix_im, filt_re * cot_re + filt_im * cot_im])
    prod_im = jnp.concatenate([filt_re * mix_im + filt_im * mix_re, filt_re * cot_im - filt_im * cot_re])
    out = inverse_transform(prod_re, prod_im, tables).astype(jnp.bfloat16)
    out = out.reshape(2, share, groups, tok_count).transpose(2, 0, 1, 3)
    out = lax.all_to_all(out, "ctx", 0, 0)

    summed = (jnp.sum(taps.astype(wide), axis=0) * factor).astype(jnp.bfloat16)
    grad_filter = lax.all_to_all(jnp.broadcast_to(summed[None], (seqs,) + summed.shape), "dp", 0, 0)
    grad_filter = grad_filter.astype(wide).reshape(share, seq_len).T

    conv_wide = out[:, 0].reshape(width, tok_count).T[None].astype(wide)
    back_wide = out[:, 1].reshape(width, tok_count).T[None].astype(wide)
    gated_output = (query_proj.astype(wide) * conv_wide).astype(jnp.bfloat16)
    grad_query = (grad_output.astype(wide) * conv_wide).astype(jnp.bfloat16)
    grad_key = (back_wide * value_proj.astype(wide)).astype(jnp.bfloat16)
    grad_value = (back_wide * key_proj.astype(wide)).astype(jnp.bfloat16)
    return (gated_output, grad_query, grad_key, grad_value, grad_filter)


def solution(mesh):
    in_specs = (
        P("dp", "ctx", None),
        P("dp", "ctx", None),
        P("dp", "ctx", None),
        P(None, "ctx"),
        P("dp", "ctx", None),
    )
    out_specs = (
        P("dp", "ctx", None),
        P("dp", "ctx", None),
        P("dp", "ctx", None),
        P("dp", "ctx", None),
        P(None, "ctx"),
    )
    return jax.shard_map(
        on_device, mesh=mesh, in_specs=in_specs, out_specs=out_specs, check_vma=False
    )
```

profile of v0, /device:TPU:1, one launch (start us, length us, event | category | flops | bytes accessed | tf_op | source)
XLA Modules:
  0.0 122.5 jit_solution(17611708877053468753)
XLA Ops:
  0.7 1.1 copy.96
  1.9 0.8 copy-done.22
  2.9 0.8 copy-done.23
  5.3 18.2 %all-to-all-start = ((bf16[64,2,8,128]{3,2,1,0:T(8,128)(2,1)}), bf16[64,2,8,128]{3,2,1,0:T(8,128)(2,1)S(1)}, u32[]{:S(2)}, u32[]{:S(2)}) async-start(bf16[64,2,8,128]{3,2,1,0:T(8,128)(2,1)} %copy.106), calls=%async_computation | async-start | bytes 524288 | tf_op jit(solution)/shard_map/all_to_all | solution.py:83
  25.7 1.6 %fusion.15 = f32[8,128,128]{2,1,0:T(8,128)} fusion(f32[128,8,128]{2,0,1:T(8,128)S(1)} %fusion.45, f32[128,8,128]{2,0,1:T(8,128)S(1)} %convolution_negate_fusion.1, f32[128,128]{1,0:T(8,128)S(1)} %copy.100, f32[128,128]{1,0:T(8,128)S(1)} %copy.98), kind=kOutput, calls=%fused_computation.32 | convolution fusion | flops 201949184 | bytes 1703936 | tf_op jit(solution)/shard_map/ckn,jn->ckj/dot_general | solution.py:39
  27.3 0.8 fusion.19
  28.2 1.6 %convolution_add_fusion.3 = f32[8,128,128]{2,1,0:T(8,128)} fusion(f32[8,128,128]{2,1,0:T(8,128)S(1)} %fusion.19, f32[128,8,128]{2,0,1:T(8,128)S(1)} %fusion.45, f32[128,8,128]{2,0,1:T(8,128)S(1)} %convolution_negate_fusion.1, f32[128,128]{1,0:T(8,128)S(1)} %copy.100, f32[128,128]{1,0:T(8,128)S(1)} %copy.98), kind=kOutput, calls=%fused_computation.13 | convolution fusion | flops 202080256 | bytes 2228224 | tf_op jit(solution)/shard_map/ckn,jn->ckj/dot_general | solution.py:36
  29.8 15.9 %all-to-all-done = bf16[64,2,8,128]{3,2,1,0:T(8,128)(2,1)S(1)} async-done(((bf16[64,2,8,128]{3,2,1,0:T(8,128)(2,1)}), bf16[64,2,8,128]{3,2,1,0:T(8,128)(2,1)S(1)}, u32[]{:S(2)}, u32[]{:S(2)}) %all-to-all-start) | async-done | bytes 262176 | tf_op jit(solution)/shard_map/all_to_all | solution.py:83
  47.2 2.0 %fusion.33 = f32[16,128,128]{2,1,0:T(8,128)S(1)} fusion(f32[16,128,128]{1,2,0:T(8,128)S(1)} %convolution_bitcast_fusion, f32[16,128,128]{1,2,0:T(8,128)S(1)} %fusion, f32[128,128]{0,1:T(8,128)S(1)} %get-tuple-element.31, f32[128,128]{0,1:T(8,128)S(1)} %get-tuple-element.32), kind=kOutput, calls=%fused_computation.64 | convolution fusion | flops 403668992 | bytes 3276800 | tf_op jit(solution)/shard_map/ckn,jn->ckj/dot_general | solution.py:39
  49.2 2.0 %fusion.32 = f32[16,128,128]{2,1,0:T(8,128)S(1)} fusion(f32[16,128,128]{1,2,0:T(8,128)S(1)} %fusion, f32[16,128,128]{1,2,0:T(8,128)S(1)} %convolution_bitcast_fusion, f32[128,128]{0,1:T(8,128)S(1)} %get-tuple-element.31, f32[128,128]{0,1:T(8,128)S(1)} %get-tuple-element.32), kind=kOutput, calls=%fused_computation.63 | convolution fusion | flops 403668992 | bytes 3276800 | tf_op jit(solution)/shard_map/ckn,jn->ckj/dot_general | solution.py:36
  51.2 2.0 %convolution_subtract_fusion.1 = f32[16,128,128]{2,1,0:T(8,128)S(1)} fusion(f32[16,128,128]{2,1,0:T(8,128)S(1)} %fusion.33, f32[16,128,128]{1,2,0:T(8,128)S(1)} %fusion, f32[16,128,128]{1,2,0:T(8,128)S(1)} %convolution_bitcast_fusion, f32[128,128]{0,1:T(8,128)S(1)} %get-tuple-element.31, f32[128,128]{0,1:T(8,128)S(1)} %get-tuple-element.32), kind=kOutput, calls=%fused_computation.2 | convolution fusion | flops 403931136 | bytes 4325376 | tf_op jit(solution)/shard_map/ckn,jn->ckj/dot_general | solution.py:39
  53.3 2.2 %convolution_add_fusion.1 = f32[16,128,128]{2,1,0:T(8,128)S(1)} fusion(f32[16,128,128]{2,1,0:T(8,128)S(1)} %fusion.32, f32[16,128,128]{1,2,0:T(8,128)S(1)} %convolution_bitcast_fusion, f32[16,128,128]{1,2,0:T(8,128)S(1)} %fusion, f32[128,128]{0,1:T(8,128)S(1)} %get-tuple-element.31, f32[128,128]{0,1:T(8,128)S(1)} %get-tuple-element.32), kind=kOutput, calls=%fused_computation.3 | convolution fusion | flops 403931136 | bytes 4325376 | tf_op jit(solution)/shard_map/ckn,jn->ckj/dot_general | solution.py:36
  55.6 1.1 multiply_add_fusion.1
  56.7 0.8 fusion.63
  57.5 0.8 fusion.61
  58.3 0.8 convolution_subtract_fusion.3
  59.2 0.8 convolution_add_fusion.2
  60.8 1.1 fusion.5
  62.0 6.4 %all-to-all-start.2 = ((bf16[8,64,128]{2,1,0:T(8,128)(2,1)}), bf16[8,64,128]{2,1,0:T(8,128)(2,1)}, u32[]{:S(2)}, u32[]{:S(2)}) async-start(bf16[8,64,128]{2,1,0:T(8,128)(2,1)} %fusion.5), calls=%async_computation.2 | async-start | bytes 262144 | tf_op jit(solution)/shard_map/all_to_all | solution.py:92
  68.3 1.3 %fusion.14 = f32[16,128,128]{1,2,0:T(8,128)S(1)} fusion(f32[8,128,128]{2,1,0:T(8,128)S(1)} %get-tuple-element.21, f32[8,128,128]{2,1,0:T(8,128)S(1)} %get-tuple-element.24), kind=kOutput, calls=%fused_computation.31 | convolution fusion | flops 403144704 | bytes 2097152 | tf_op jit(solution)/shard_map/ckj,nj->ckn/dot_general | solution.py:50
  69.7 1.3 %fusion.13 = f32[16,128,128]{1,2,0:T(8,128)S(1)} fusion(f32[8,128,128]{2,1,0:T(8,128)S(1)} %get-tuple-element.23, f32[8,128,128]{2,1,0:T(8,128)S(1)} %get-tuple-element.22), kind=kOutput, calls=%fused_computation.30 | convolution fusion | flops 403144704 | bytes 2097152 | tf_op jit(solution)/shard_map/ckj,nj->ckn/dot_general | solution.py:53
  71.0 1.3 %convolution_subtract_fusion = f32[16,128,128]{1,2,0:T(8,128)S(1)} fusion(f32[16,128,128]{1,2,0:T(8,128)S(1)} %fusion.14, f32[8,128,128]{2,1,0:T(8,128)S(1)} %get-tuple-element.23, f32[8,128,128]{2,1,0:T(8,128)S(1)} %get-tuple-element.22), kind=kOutput, calls=%fused_computation.1 | convolution fusion | flops 403406848 | bytes 3145728 | tf_op jit(solution)/shard_map/ckj,nj->ckn/dot_general | solution.py:50
  72.4 1.3 %convolution_add_fusion = f32[16,128,128]{1,2,0:T(8,128)S(1)} fusion(f32[16,128,128]{1,2,0:T(8,128)S(1)} %fusion.13, f32[8,128,128]{2,1,0:T(8,128)S(1)} %get-tuple-element.21, f32[8,128,128]{2,1,0:T(8,128)S(1)} %get-tuple-element.24), kind=kOutput, calls=%fused_computation | convolution fusion | flops 403406848 | bytes 3145728 | tf_op jit(solution)/shard_map/ckj,nj->ckn/dot_general | solution.py:53
  73.7 1.4 %fusion.9 = f32[16,128,64]{1,2,0:T(8,128)S(1)} fusion(f32[16,128,128]{1,2,0:T(8,128)S(1)} %convolution_add_fusion, f32[16,128,128]{1,2,0:T(8,128)S(1)} %convolution_subtract_fusion, f32[128,128]{0,1:T(8,128)S(1)} %get-tuple-element.31, f32[128,128]{0,1:T(8,128)S(1)} %get-tuple-element.32, f32[128,128]{0,1:T(8,128)S(1)} %copy-done.20), kind=kOutput, calls=%fused_computation.24 | convolution fusion | flops 202113024 | bytes 2818048 | tf_op jit(solution)/shard_map/nk,ckm->cnm/dot_general | solution.py:58
  75.2 0.9 convert_reduce_fusion
  76.8 6.7 %all-to-all-start.3 = ((bf16[8,64,128]{2,1,0:T(8,128)(2,1)}), bf16[8,64,128]{2,1,0:T(8,128)(2,1)S(1)}, u32[]{:S(2)}, u32[]{:S(2)}) async-start(bf16[8,64,128]{2,1,0:T(8,128)(2,1)} %broadcast_in_dim.2), calls=%async_computation.3 | async-start | bytes 262144 | tf_op jit(solution)/shard_map/all_to_all | solution.py:101
  83.5 1.4 %fusion.2 = bf16[16,128,64]{1,2,0:T(8,128)(2,1)S(1)} fusion(f32[16,128,64]{1,2,0:T(8,128)S(1)} %fusion.9, f32[16,128,128]{1,2,0:T(8,128)S(1)} %convolution_subtract_fusion, f32[16,128,128]{1,2,0:T(8,128)S(1)} %convolution_add_fusion, f32[128,128]{0,1:T(8,128)S(1)} %get-tuple-element.31, f32[128,128]{0,1:T(8,128)S(1)} %get-tuple-element.32, ...), kind=kOutput, calls=%fused_computation.14 | convolution fusion | flops 202506240 | bytes 3080192 | tf_op jit(solution)/shard_map/nk,ckm->cnm/dot_general | solution.py:58
  84.9 0.9 copy.205
  85.7 4.5 %all-to-all-done.3 = bf16[8,64,128]{2,1,0:T(8,128)(2,1)S(1)} async-done(((bf16[8,64,128]{2,1,0:T(8,128)(2,1)}), bf16[8,64,128]{2,1,0:T(8,128)(2,1)S(1)}, u32[]{:S(2)}, u32[]{:S(2)}) %all-to-all-start.3) | async-done | bytes 131104 | tf_op jit(solution)/shard_map/all_to_all | solution.py:101
  90.3 6.7 %all-to-all-start.1 = ((bf16[64,2,8,128]{3,2,1,0:T(8,128)(2,1)}), bf16[64,2,8,128]{3,2,1,0:T(8,128)(2,1)S(1)}, u32[]{:S(2)}, u32[]{:S(2)}) async-start(bf16[64,2,8,128]{3,2,1,0:T(8,128)(2,1)} %bitcast.150), calls=%async_computation.1 | async-start | bytes 524288 | tf_op jit(solution)/shard_map/all_to_all | solution.py:98
  97.0 0.9 copy.204
  97.9 21.4 %all-to-all-done.1 = bf16[64,2,8,128]{3,2,1,0:T(8,128)(2,1)S(1)} async-done(((bf16[64,2,8,128]{3,2,1,0:T(8,128)(2,1)}), bf16[64,2,8,128]{3,2,1,0:T(8,128)(2,1)S(1)}, u32[]{:S(2)}, u32[]{:S(2)}) %all-to-all-start.1) | async-done | bytes 262176 | tf_op jit(solution)/shard_map/all_to_all | solution.py:98
  (72 shorter events, 10.4 us)
Async XLA Ops:
  0.6 23.8 %copy-start = (f32[8192,8]{0,1:T(8,128)S(1)}, f32[8192,8]{0,1:T(8,128)}, u32[]{:S(2)}) copy-start(f32[8192,8]{0,1:T(8,128)} %param.8) | copy-start | bytes 786436
  0.6 1.1 copy-start.21
  1.8 2.0 %copy-start.7 = (bf16[1,128,512]{1,2,0:T(8,128)(2,1)}, bf16[1,128,512]{1,2,0:T(8,128)(2,1)S(1)}, u32[]{:S(2)}) copy-start(bf16[1,128,512]{1,2,0:T(8,128)(2,1)S(1)} %copy.96) | copy-start | bytes 393220
  1.8 1.0 copy-start.22
  2.7 1.1 copy-start.9
  2.7 1.0 copy-start.23
  3.7 0.7 copy-start.11
  3.8 0.7 copy-start.13
  5.3 40.5 %all-to-all-start = ((bf16[64,2,8,128]{3,2,1,0:T(8,128)(2,1)}), bf16[64,2,8,128]{3,2,1,0:T(8,128)(2,1)S(1)}, u32[]{:S(2)}, u32[]{:S(2)}) async-start(bf16[64,2,8,128]{3,2,1,0:T(8,128)(2,1)} %copy.106), calls=%async_computation | async-start | bytes 524288 | tf_op jit(solution)/shard_map/all_to_all | solution.py:83
  23.7 22.8 %copy-start.18 = (f32[128,128]{0,1:T(8,128)}, f32[128,128]{0,1:T(8,128)S(1)}, u32[]{:S(2)}) copy-start(f32[128,128]{0,1:T(8,128)S(1)} %fusion.81) | copy-start | bytes 196612
  24.0 21.8 %copy-start.15 = (f32[128,128]{0,1:T(8,128)}, f32[128,128]{0,1:T(8,128)S(1)}, u32[]{:S(2)}) copy-start(f32[128,128]{0,1:T(8,128)S(1)} %fusion.80) | copy-start | bytes 196612
  24.4 3.8 %copy-start.1 = (f32[128,128]{1,0:T(8,128)}, f32[128,128]{1,0:T(8,128)S(1)}, u32[]{:S(2)}) copy-start(f32[128,128]{1,0:T(8,128)S(1)} %copy.100) | copy-start | bytes 196612
  24.5 3.7 %copy-start.3 = (f32[128,128]{1,0:T(8,128)}, f32[128,128]{1,0:T(8,128)S(1)}, u32[]{:S(2)}) copy-start(f32[128,128]{1,0:T(8,128)S(1)} %copy.98) | copy-start | bytes 196612
  53.3 2.3 %copy-start.2 = (f32[128,128]{1,0:T(8,128)S(1)}, f32[128,128]{1,0:T(8,128)}, u32[]{:S(2)}) copy-start(f32[128,128]{1,0:T(8,128)} %copy-done.1) | copy-start | bytes 196612
  53.3 2.3 %copy-start.4 = (f32[128,128]{1,0:T(8,128)S(1)}, f32[128,128]{1,0:T(8,128)}, u32[]{:S(2)}) copy-start(f32[128,128]{1,0:T(8,128)} %copy-done.3) | copy-start | bytes 196612
  53.3 2.3 %copy-start.5 = (f32[8,128,128]{2,1,0:T(8,128)S(1)}, f32[8,128,128]{2,1,0:T(8,128)}, u32[]{:S(2)}) copy-start(f32[8,128,128]{2,1,0:T(8,128)} %convolution_add_fusion.3) | copy-start | bytes 1572868
  53.3 2.3 %copy-start.6 = (f32[8,128,128]{2,1,0:T(8,128)S(1)}, f32[8,128,128]{2,1,0:T(8,128)}, u32[]{:S(2)}) copy-start(f32[8,128,128]{2,1,0:T(8,128)} %fusion.15) | copy-start | bytes 1572868
  59.2 0.8 copy-start.19
  60.0 0.8 copy-start.16
  62.0 13.2 %all-to-all-start.2 = ((bf16[8,64,128]{2,1,0:T(8,128)(2,1)}), bf16[8,64,128]{2,1,0:T(8,128)(2,1)}, u32[]{:S(2)}, u32[]{:S(2)}) async-start(bf16[8,64,128]{2,1,0:T(8,128)(2,1)} %fusion.5), calls=%async_computation.2 | async-start | bytes 262144 | tf_op jit(solution)/shard_map/all_to_all | solution.py:92
  72.4 1.4 %copy-start.20 = (f32[128,128]{0,1:T(8,128)S(1)}, f32[128,128]{0,1:T(8,128)}, u32[]{:S(2)}) copy-start(f32[128,128]{0,1:T(8,128)} %copy-done.18) | copy-start | bytes 196612
  76.8 6.7 %copy-start.17 = (f32[128,128]{0,1:T(8,128)S(1)}, f32[128,128]{0,1:T(8,128)}, u32[]{:S(2)}) copy-start(f32[128,128]{0,1:T(8,128)} %copy-done.15) | copy-start | bytes 196612
  76.8 13.4 %all-to-all-start.3 = ((bf16[8,64,128]{2,1,0:T(8,128)(2,1)}), bf16[8,64,128]{2,1,0:T(8,128)(2,1)S(1)}, u32[]{:S(2)}, u32[]{:S(2)}) async-start(bf16[8,64,128]{2,1,0:T(8,128)(2,1)} %broadcast_in_dim.2), calls=%async_computation.3 | async-start | bytes 262144 | tf_op jit(solution)/shard_map/all_to_all | solution.py:101
  90.3 29.0 %all-to-all-start.1 = ((bf16[64,2,8,128]{3,2,1,0:T(8,128)(2,1)}), bf16[64,2,8,128]{3,2,1,0:T(8,128)(2,1)S(1)}, u32[]{:S(2)}, u32[]{:S(2)}) async-start(bf16[64,2,8,128]{3,2,1,0:T(8,128)(2,1)} %bitcast.150), calls=%async_computation.1 | async-start | bytes 524288 | tf_op jit(solution)/shard_map/all_to_all | solution.py:98
  97.0 22.3 %copy-start.8 = (bf16[1,128,512]{1,2,0:T(8,128)(2,1)S(1)}, bf16[1,128,512]{1,2,0:T(8,128)(2,1)}, u32[]{:S(2)}) copy-start(bf16[1,128,512]{1,2,0:T(8,128)(2,1)} %copy-done.7) | copy-start | bytes 393220
  97.0 22.3 %copy-start.10 = (bf16[1,128,512]{1,2,0:T(8,128)(2,1)S(1)}, bf16[1,128,512]{1,2,0:T(8,128)(2,1)}, u32[]{:S(2)}) copy-start(bf16[1,128,512]{1,2,0:T(8,128)(2,1)} %copy-done.9) | copy-start | bytes 393220
  97.0 22.3 %copy-start.12 = (bf16[1,128,512]{1,2,0:T(8,128)(2,1)S(1)}, bf16[1,128,512]{1,2,0:T(8,128)(2,1)}, u32[]{:S(2)}) copy-start(bf16[1,128,512]{1,2,0:T(8,128)(2,1)} %copy-done.11) | copy-start | bytes 393220
  97.0 22.3 %copy-start.14 = (bf16[1,128,512]{1,2,0:T(8,128)(2,1)S(1)}, bf16[1,128,512]{1,2,0:T(8,128)(2,1)}, u32[]{:S(2)}) copy-start(bf16[1,128,512]{1,2,0:T(8,128)(2,1)} %copy-done.13) | copy-start | bytes 393220
where the time goes:
time: 123 us; the launch traced here: 122 us
  waiting for transfers between devices  41.9 us (34%)
  starting transfers between devices  37.8 us (31%)
  matrix products  29 us (24%)
  local copies, waits for them, and re-layouts  10.6 us (9%)
  other arithmetic  1.97 us (2%)
    all_to_all x1, waiting for transfers between devices, on_device(): out = lax.all_to_all(out, 'ctx', 0, 0)  21.4 us
    all_to_all x1, starting transfers between devices, on_device(): both = lax.all_to_all(both, 'ctx', 0, 0)  18.2 us
    all_to_all x1, waiting for transfers between devices, on_device(): both = lax.all_to_all(both, 'ctx', 0, 0)  15.9 us
    unnamed x57, local copies, waits for them, and re-layouts  8.03 us
    all_to_all x1, starting transfers between devices, on_device(): lax.all_to_all(jnp.broadcast_to(summed[None], (seqs,) + summed.shape), 'd...  6.66 us
    all_to_all x1, starting transfers between devices, on_device(): out = lax.all_to_all(out, 'ctx', 0, 0)  6.66 us
    all_to_all x1, starting transfers between devices, on_device(): taps = lax.all_to_all(taps.astype(jnp.bfloat16), 'dp', 0, 0)  6.35 us
    all_to_all x1, waiting for transfers between devices, on_device(): lax.all_to_all(jnp.broadcast_to(summed[None], (seqs,) + summed.shape), 'd...  4.51 us
  transfers between devices with their start and end apart: 4, of which 4 were waited for; matrix products, arithmetic and copies ran while one was open for 13% of the time, Pallas kernels for 0%

commit v1 on v0

v1 whole, which is shorter than its diff:
```python
import math

import jax
import jax.numpy as jnp
import ml_dtypes
import numpy as np
from jax import lax
from jax.experimental import pallas as pl
from jax.experimental.pallas import tpu as pltpu
from jax.sharding import PartitionSpec as P

BF = jnp.bfloat16
F32 = jnp.float32


def halves(table):
    high = table.astype(np.float32).astype(ml_dtypes.bfloat16)
    low = (table - high.astype(np.float64)).astype(np.float32).astype(ml_dtypes.bfloat16)
    return high, low


def make_tables(blocks, lanes):
    period = 2 * blocks
    total = period * lanes
    n = np.arange(blocks)
    odd = 2 * np.arange(blocks) + 1
    angle = math.pi / period * (n[None, :] * odd[:, None] % (2 * period))
    first = np.concatenate([np.cos(angle), -np.sin(angle)])
    m = np.arange(lanes)
    turn = math.pi / total * (odd[:, None] * m[None, :] % (2 * total))
    angle = 2 * math.pi / lanes * (m[:, None] * m[None, :] % lanes)
    cos, sin = np.cos(angle), np.sin(angle)
    second = np.block([[cos, -sin], [sin, cos]])
    a_high, a_low = halves(first)
    b_high, b_low = halves(first.T)
    g_high, g_low = halves(second)
    return dict(
        into=np.concatenate([a_high, a_low], axis=1),
        into3=np.concatenate([a_high, a_high, a_low], axis=1),
        out=np.block([[b_high, b_high], [b_low, np.zeros_like(b_low)]]),
        turn_cos=np.cos(turn).astype(np.float32),
        turn_sin=np.sin(turn).astype(np.float32),
        g_high=g_high,
        g_low=g_low,
    )


def dot(a, b):
    return jnp.dot(a, b, preferred_element_type=F32)


def split(x):
    high = x.astype(BF)
    return high, (x - high.astype(F32)).astype(BF)


def across(z_high, z_low, g_high, g_low):
    return dot(z_high, g_high) + dot(z_low, g_high) + dot(z_high, g_low)


def turned(part, blocks, cos, sin):
    re, im = part[:blocks], part[blocks:]
    return jnp.concatenate([re * cos + im * sin, im * cos - re * sin], axis=1)


def back_to_positions(spec, out_ref, cos, sin, blocks, lanes):
    count = spec.shape[0] // blocks
    result = []
    for pair in range(count // 2):
        rows = []
        for one in range(2):
            c = 2 * pair + one
            block = spec[c * blocks:(c + 1) * blocks]
            im, re = block[:, :lanes], block[:, lanes:]
            rows.append(jnp.concatenate([re * cos - im * sin, im * cos + re * sin], axis=0))
        both = jnp.concatenate(rows, axis=1)
        high, low = split(both)
        y = dot(out_ref[...], jnp.concatenate([high, low], axis=0))
        y = y[:blocks] + y[blocks:]
        result += [y[:, :lanes], y[:, lanes:]]
    return result


def filter_kernel(scale, f_ref, into3_ref, cos_ref, sin_ref, gh_ref, gl_ref, spec_ref):
    share, blocks, lanes = f_ref.shape
    cos, sin = cos_ref[...], sin_ref[...]
    rows = []
    for pair in range(share // 2):
        x = jnp.concatenate([f_ref[2 * pair], f_ref[2 * pair + 1]], axis=1)
        high, low = split(x)
        part = dot(into3_ref[...], jnp.concatenate([high, low, high], axis=0))
        rows.append(turned(part[:, :lanes], blocks, cos, sin))
        rows.append(turned(part[:, lanes:], blocks, cos, sin))
    high, low = split(jnp.concatenate(rows, axis=0))
    spec_ref[...] = across(high, low, gh_ref[...], gl_ref[...]) * scale


def conv_kernel(x_ref, filt_ref, into_ref, out_tab_ref, cos_ref, sin_ref, gh_ref, gl_ref, y_ref, spec_ref, wide_ref):
    blocks, fields, lanes = x_ref.shape
    share = fields // 2
    cos, sin = cos_ref[...], sin_ref[...]
    wide_ref[...] = x_ref[...].astype(F32).reshape(blocks * fields, lanes)
    rows = []
    for pair in range(fields // 2):
        x = jnp.concatenate(
            [wide_ref[pl.ds(2 * pair + one, blocks, stride=fields), :] for one in range(2)], axis=1
        ).astype(BF)
        part = dot(into_ref[...], jnp.concatenate([x, x], axis=0))
        rows.append(turned(part[:, :lanes], blocks, cos, sin))
        rows.append(turned(part[:, lanes:], blocks, cos, sin))
    high, low = split(jnp.concatenate(rows, axis=0))
    spec_ref[...] = across(high, low, gh_ref[...], gl_ref[...])
    half = share * blocks
    fr, fi = filt_ref[:, :lanes], filt_ref[:, lanes:]
    xr, xi = spec_ref[:half, :lanes], spec_ref[:half, lanes:]
    gr, gi = spec_ref[half:, :lanes], spec_ref[half:, lanes:]
    conv = jnp.concatenate([fr * xi + fi * xr, fr * xr - fi * xi], axis=1)
    back = jnp.concatenate([fr * gi - fi * gr, fr * gr + fi * gi], axis=1)
    high, low = split(jnp.concatenate([conv, back], axis=0))
    inner = across(high, low, gh_ref[...], gl_ref[...])
    ys = back_to_positions(inner, out_tab_ref, cos, sin, blocks, lanes)
    for f, y in enumerate(ys):
        wide_ref[pl.ds(f, blocks, stride=fields), :] = y
    y_ref[...] = wide_ref[...].reshape(blocks, fields, lanes).astype(BF)


def taps_kernel(scale, spec_ref, out_tab_ref, cos_ref, sin_ref, gh_ref, gl_ref, taps_ref, wide_ref):
    blocks, lanes = cos_ref.shape
    half = spec_ref.shape[0] // 2
    share = half // blocks
    cos, sin = cos_ref[...], sin_ref[...]
    xr, xi = spec_ref[:half, :lanes], spec_ref[:half, lanes:]
    gr, gi = spec_ref[half:, :lanes], spec_ref[half:, lanes:]
    prod = jnp.concatenate([xr * gi - xi * gr, xr * gr + xi * gi], axis=1)
    high, low = split(prod * scale)
    inner = across(high, low, gh_ref[...], gl_ref[...])
    for c, y in enumerate(back_to_positions(inner, out_tab_ref, cos, sin, blocks, lanes)):
        wide_ref[pl.ds(c, blocks, stride=share), :] = y
    taps_ref[...] = wide_ref[...].astype(BF)


def mix_kernel(q_ref, k_ref, v_ref, g_ref, out_ref):
    groups, fields, lanes = out_ref.shape
    share = fields // 2

    def turn(a, b):
        prod = (a[0].astype(F32) * b[0].astype(F32)).astype(BF).astype(F32)
        return prod.T.reshape(groups, share, lanes)

    both = jnp.concatenate([turn(k_ref, v_ref), turn(g_ref, q_ref)], axis=1)
    out_ref[...] = both.astype(BF)


def gate_kernel(y_ref, q_ref, k_ref, v_ref, g_ref, go_ref, gq_ref, gk_ref, gv_ref):
    groups, fields, lanes = y_ref.shape
    share = fields // 2
    both = y_ref[...].astype(F32)
    conv = both[:, :share].reshape(groups * share, lanes).T
    back = both[:, share:].reshape(groups * share, lanes).T
    go_ref[0] = (q_ref[0].astype(F32) * conv).astype(BF)
    gq_ref[0] = (g_ref[0].astype(F32) * conv).astype(BF)
    gk_ref[0] = (back * v_ref[0].astype(F32)).astype(BF)
    gv_ref[0] = (back * k_ref[0].astype(F32)).astype(BF)


PARAMS = pltpu.CompilerParams(vmem_limit_bytes=32 * 1024 * 1024)


def on_device(query_proj, key_proj, value_proj, long_filter, grad_output):
    tok_count = query_proj.shape[1]
    width = query_proj.shape[2]
    groups = lax.axis_size("ctx")
    seqs = lax.axis_size("dp")
    seq_len = tok_count * groups
    share = width // groups
    t = make_tables(groups, tok_count)
    spec_rows = share * groups

    both = pl.pallas_call(
        mix_kernel,
        out_shape=jax.ShapeDtypeStruct((groups, 2 * share, tok_count), BF),
        compiler_params=PARAMS,
    )(query_proj, key_proj, value_proj, grad_output)
    both = lax.all_to_all(both, "ctx", 0, 0)

    filt_spec = pl.pallas_call(
        lambda *refs: filter_kernel(2.0 / (2 * seq_len), *refs),
        out_shape=jax.ShapeDtypeStruct((spec_rows, 2 * tok_count), F32),
        compiler_params=PARAMS,
    )(long_filter.T.reshape(share, groups, tok_count), t["into3"], t["turn_cos"], t["turn_sin"], t["g_high"], t["g_low"])

    out, spec = pl.pallas_call(
        conv_kernel,
        out_shape=(
            jax.ShapeDtypeStruct((groups, 2 * share, tok_count), BF),
            jax.ShapeDtypeStruct((2 * spec_rows, 2 * tok_count), F32),
        ),
        scratch_shapes=[pltpu.VMEM((2 * spec_rows, tok_count), F32)],
        compiler_params=PARAMS,
    )(both, filt_spec, t["into"], t["out"], t["turn_cos"], t["turn_sin"], t["g_high"], t["g_low"])
    out = lax.all_to_all(out, "ctx", 0, 0)

    factor = 1.0 / math.sqrt(seq_len * seqs)
    taps = pl.pallas_call(
        lambda *refs: taps_kernel(factor * 2.0 / (2 * seq_len), *refs),
        out_shape=jax.ShapeDtypeStruct((spec_rows, tok_count), BF),
        scratch_shapes=[pltpu.VMEM((spec_rows, tok_count), F32)],
        compiler_params=PARAMS,
    )(spec, t["out"], t["turn_cos"], t["turn_sin"], t["g_high"], t["g_low"])
    for flip in (1, 2, 6):
        taps = taps.astype(BF)
        other = lax.ppermute(taps, "dp", [(i, i ^ flip) for i in range(seqs)])
        taps = taps.astype(F32) + other.astype(F32)
    grad_filter = taps.reshape(groups, share, tok_count).transpose(0, 2, 1).reshape(seq_len, share)

    grads = pl.pallas_call(
        gate_kernel,
        out_shape=[jax.ShapeDtypeStruct(query_proj.shape, BF)] * 4,
        compiler_params=PARAMS,
    )(out, query_proj, key_proj, value_proj, grad_output)
    return (*grads, grad_filter)


def solution(mesh):
    tokens = P("dp", "ctx", None)
    taps = P(None, "ctx")
    return jax.shard_map(
        on_device,
        mesh=mesh,
        in_specs=(tokens, tokens, tokens, taps, tokens),
        out_specs=(tokens, tokens, tokens, tokens, taps),
        check_vma=False,
    )
```

time: 123 us -> 97.8 us (0.80)
  the two profiles are of different devices: /device:TPU:1 before, /device:TPU:24 now
where the time goes in v1:
time: 97.8 us; the launch traced here: 96.4 us
  waiting for transfers between devices  51.1 us (52%)
  starting transfers between devices  33.4 us (34%)
  Pallas kernels  5.69 us (6%)
  local copies, waits for them, and re-layouts  4.6 us (5%)
    all_to_all x1, waiting for transfers between devices, on_device(): out = lax.all_to_all(out, 'ctx', 0, 0)  21.7 us
    all_to_all x1, waiting for transfers between devices, on_device(): both = lax.all_to_all(both, 'ctx', 0, 0)  20.8 us
    all_to_all x1, starting transfers between devices, on_device(): both = lax.all_to_all(both, 'ctx', 0, 0)  17.2 us
    ppermute x3, starting transfers between devices, on_device(): other = lax.ppermute(taps, 'dp', [(i, i ^ flip) for i in range(seqs)])  11.2 us
    ppermute x3, waiting for transfers between devices, on_device(): other = lax.ppermute(taps, 'dp', [(i, i ^ flip) for i in range(seqs)])  8.67 us
    all_to_all x1, starting transfers between devices, on_device(): out = lax.all_to_all(out, 'ctx', 0, 0)  4.98 us
    unnamed x33, local copies, waits for them, and re-layouts  4.6 us
    pallas_call x1, Pallas kernels, on_device(): pl.pallas_call(conv_kernel, out_shape=(jax.ShapeDtypeStruct((groups, 2 *...  2.78 us
  transfers between devices with their start and end apart: 5, of which 4 were waited for; matrix products, arithmetic and copies ran while one was open for 1% of the time, Pallas kernels for 1%

profile of v1, /device:TPU:24, one launch (start us, length us, event | category | flops | bytes accessed | tf_op | source)
XLA Modules:
  0.0 96.4 jit_solution(11629186591796194657)
XLA Ops:
  0.6 0.0 copy-start.2
  0.6 0.9 copy-done.2
  1.5 0.9 copy-done.4
  2.4 0.9 copy-done.6
  3.3 0.9 copy-done.8
  4.3 0.8 shard_map.155
  5.1 17.2 %all-to-all-start = ((bf16[64,16,128]{2,1,0:T(8,128)(2,1)}), bf16[64,16,128]{2,1,0:T(8,128)(2,1)S(1)}, u32[]{:S(2)}, u32[]{:S(2)}) async-start(bf16[64,16,128]{2,1,0:T(8,128)(2,1)} %shard_map.155), calls=%async_computation | async-start | bytes 524288 | tf_op jit(solution)/shard_map/all_to_all | solution.py:184
  22.4 0.0 copy-start
  22.4 0.0 copy-start.1
  22.4 0.0 copy-start.10
  22.4 0.0 copy-start.11
  22.4 0.0 copy-start.13
  22.4 0.1 copy.19
  22.5 0.8 copy-done
  23.3 0.1 copy-done.1
  23.3 0.0 copy-done.13
  23.4 0.5 shard_map.156.filt_ref
  23.9 20.8 %all-to-all-done.x_ref = bf16[64,16,128]{2,1,0:T(8,128)(2,1)S(1)} async-done(((bf16[64,16,128]{2,1,0:T(8,128)(2,1)}), bf16[64,16,128]{2,1,0:T(8,128)(2,1)S(1)}, u32[]{:S(2)}, u32[]{:S(2)}) %all-to-all-start) | async-done | bytes 262176 | tf_op jit(solution)/shard_map/all_to_all | solution.py:184
  44.7 2.8 %shard_map.157 = (bf16[64,16,128]{2,1,0:T(8,128)(2,1)}, f32[1024,256]{1,0:T(8,128)S(1)}) custom-call(bf16[64,16,128]{2,1,0:T(8,128)(2,1)S(1)} %all-to-all-done.x_ref, f32[512,256]{1,0:T(8,128)S(1)} %shard_map.156.filt_ref, bf16[128,128]{1,0:T(8,128)(2,1)S(1)} %copy-done.14, bf16[128,256]{1,0:T(8,128)(2,1)S(1)} %copy-done.12, f32[64,128]{1,0:T(8,128)S(1)} %copy-done.11, ...), custom_call_target="tpu_custom_call" | custom-call | tf_op jit(solution)/shard_map/pallas_call | solution.py:192
  47.5 0.6 shard_map.159
  48.1 3.1 %collective-permute-start = (bf16[512,128]{1,0:T(8,128)(2,1)S(1)}, bf16[512,128]{1,0:T(8,128)(2,1)S(1)}, u32[]{:S(2)}, u32[]{:S(2)}) collective-permute-start(bf16[512,128]{1,0:T(8,128)(2,1)S(1)} %shard_map.159), channel_id=1, source_target_pairs={{0,64},{64,0},{128,192},{192,128},{256,320},{320,256},{384,448},{4... | collective-permute-start | bytes 393224 | tf_op jit(solution)/shard_map/ppermute | solution.py:212
  51.2 5.2 %collective-permute-done = bf16[512,128]{1,0:T(8,128)(2,1)S(1)} collective-permute-done((bf16[512,128]{1,0:T(8,128)(2,1)S(1)}, bf16[512,128]{1,0:T(8,128)(2,1)S(1)}, u32[]{:S(2)}, u32[]{:S(2)}) %collective-permute-start) | collective-permute-done | bytes 131104 | tf_op jit(solution)/shard_map/ppermute | solution.py:212
  56.5 3.4 %collective-permute-start.1 = (bf16[512,128]{1,0:T(8,128)(2,1)S(1)}, bf16[512,128]{1,0:T(8,128)(2,1)S(1)}, u32[]{:S(2)}, u32[]{:S(2)}) collective-permute-start(bf16[512,128]{1,0:T(8,128)(2,1)S(1)} %add_convert_fusion.1), channel_id=1, source_target_pairs={{0,128},{64,192},{128,0},{192,64},{256,384},{320,448},{384,256},{4... | collective-permute-start | bytes 393224 | tf_op jit(solution)/shard_map/ppermute | solution.py:212
  59.9 3.5 %collective-permute-done.1 = bf16[512,128]{1,0:T(8,128)(2,1)S(1)} collective-permute-done((bf16[512,128]{1,0:T(8,128)(2,1)S(1)}, bf16[512,128]{1,0:T(8,128)(2,1)S(1)}, u32[]{:S(2)}, u32[]{:S(2)}) %collective-permute-start.1) | collective-permute-done | bytes 131104 | tf_op jit(solution)/shard_map/ppermute | solution.py:212
  63.4 4.7 %collective-permute-start.2 = (bf16[512,128]{1,0:T(8,128)(2,1)S(1)}, bf16[512,128]{1,0:T(8,128)(2,1)S(1)}, u32[]{:S(2)}, u32[]{:S(2)}) collective-permute-start(bf16[512,128]{1,0:T(8,128)(2,1)S(1)} %add_convert_fusion), channel_id=1, source_target_pairs={{0,384},{64,448},{128,256},{192,320},{256,128},{320,192},{384,0},{... | collective-permute-start | bytes 393224 | tf_op jit(solution)/shard_map/ppermute | solution.py:212
  68.1 5.0 %all-to-all-start.1 = ((bf16[64,16,128]{2,1,0:T(8,128)(2,1)}), bf16[64,16,128]{2,1,0:T(8,128)(2,1)S(1)}, u32[]{:S(2)}, u32[]{:S(2)}) async-start(bf16[64,16,128]{2,1,0:T(8,128)(2,1)} %get-tuple-element.11), calls=%async_computation.1 | async-start | bytes 524288 | tf_op jit(solution)/shard_map/all_to_all | solution.py:201
  73.0 0.0 copy-start.3
  73.1 0.0 copy-start.7
  73.1 0.0 copy-start.9
  73.1 0.7 add_bitcast_fusion
  73.8 21.7 %all-to-all-done.1.y_ref = bf16[64,16,128]{2,1,0:T(8,128)(2,1)S(1)} async-done(((bf16[64,16,128]{2,1,0:T(8,128)(2,1)}), bf16[64,16,128]{2,1,0:T(8,128)(2,1)S(1)}, u32[]{:S(2)}, u32[]{:S(2)}) %all-to-all-start.1) | async-done | bytes 262176 | tf_op jit(solution)/shard_map/all_to_all | solution.py:201
  95.5 0.9 shard_map.158
  (19 shorter events, 0.1 us)
Async XLA Ops:
  0.6 0.9 copy-start.2
  1.5 0.9 copy-start.4
  2.4 0.9 copy-start.6
  3.3 0.9 copy-start.8
  5.1 17.3 %copy-start.15 = (f32[8192,8]{0,1:T(8,128)S(1)}, f32[8192,8]{0,1:T(8,128)}, u32[]{:S(2)}) copy-start(f32[8192,8]{0,1:T(8,128)} %param.15) | copy-start | bytes 786436
  5.1 39.6 %all-to-all-start = ((bf16[64,16,128]{2,1,0:T(8,128)(2,1)}), bf16[64,16,128]{2,1,0:T(8,128)(2,1)S(1)}, u32[]{:S(2)}, u32[]{:S(2)}) async-start(bf16[64,16,128]{2,1,0:T(8,128)(2,1)} %shard_map.155), calls=%async_computation | async-start | bytes 524288 | tf_op jit(solution)/shard_map/all_to_all | solution.py:184
  22.4 0.9 copy-start
  22.4 1.0 copy-start.1
  22.4 1.0 copy-start.10
  22.4 0.9 copy-start.11
  22.4 1.0 copy-start.13
  23.4 21.3 %copy-start.12 = (bf16[128,256]{1,0:T(8,128)(2,1)S(1)}, bf16[128,256]{1,0:T(8,128)(2,1)}, u32[]{:S(2)}) copy-start(bf16[128,256]{1,0:T(8,128)(2,1)} %constant.20.clone.out_tab_ref.refs_1_) | copy-start | bytes 196612
  23.4 21.3 %copy-start.14 = (bf16[128,128]{1,0:T(8,128)(2,1)S(1)}, bf16[128,128]{1,0:T(8,128)(2,1)}, u32[]{:S(2)}) copy-start(bf16[128,128]{1,0:T(8,128)(2,1)} %constant.19.clone.into_ref) | copy-start | bytes 98308
  48.1 8.4 %collective-permute-start = (bf16[512,128]{1,0:T(8,128)(2,1)S(1)}, bf16[512,128]{1,0:T(8,128)(2,1)S(1)}, u32[]{:S(2)}, u32[]{:S(2)}) collective-permute-start(bf16[512,128]{1,0:T(8,128)(2,1)S(1)} %shard_map.159), channel_id=1, source_target_pairs={{0,64},{64,0},{128,192},{192,128},{256,320},{320,256},{384,448},{4... | collective-permute-start | bytes 393224 | tf_op jit(solution)/shard_map/ppermute | solution.py:212
  56.5 6.9 %collective-permute-start.1 = (bf16[512,128]{1,0:T(8,128)(2,1)S(1)}, bf16[512,128]{1,0:T(8,128)(2,1)S(1)}, u32[]{:S(2)}, u32[]{:S(2)}) collective-permute-start(bf16[512,128]{1,0:T(8,128)(2,1)S(1)} %add_convert_fusion.1), channel_id=1, source_target_pairs={{0,128},{64,192},{128,0},{192,64},{256,384},{320,448},{384,256},{4... | collective-permute-start | bytes 393224 | tf_op jit(solution)/shard_map/ppermute | solution.py:212
  63.4 9.7 %collective-permute-start.2 = (bf16[512,128]{1,0:T(8,128)(2,1)S(1)}, bf16[512,128]{1,0:T(8,128)(2,1)S(1)}, u32[]{:S(2)}, u32[]{:S(2)}) collective-permute-start(bf16[512,128]{1,0:T(8,128)(2,1)S(1)} %add_convert_fusion), channel_id=1, source_target_pairs={{0,384},{64,448},{128,256},{192,320},{256,128},{320,192},{384,0},{... | collective-permute-start | bytes 393224 | tf_op jit(solution)/shard_map/ppermute | solution.py:212
  68.1 27.4 %all-to-all-start.1 = ((bf16[64,16,128]{2,1,0:T(8,128)(2,1)}), bf16[64,16,128]{2,1,0:T(8,128)(2,1)S(1)}, u32[]{:S(2)}, u32[]{:S(2)}) async-start(bf16[64,16,128]{2,1,0:T(8,128)(2,1)} %get-tuple-element.11), calls=%async_computation.1 | async-start | bytes 524288 | tf_op jit(solution)/shard_map/all_to_all | solution.py:201
  73.0 22.4 %copy-start.3 = (bf16[1,128,512]{2,1,0:T(8,128)(2,1)S(1)}, bf16[1,128,512]{2,1,0:T(8,128)(2,1)}, u32[]{:S(2)}) copy-start(bf16[1,128,512]{2,1,0:T(8,128)(2,1)} %q_ref.3) | copy-start | bytes 393220
  73.1 22.4 %copy-start.5 = (bf16[1,128,512]{2,1,0:T(8,128)(2,1)S(1)}, bf16[1,128,512]{2,1,0:T(8,128)(2,1)}, u32[]{:S(2)}) copy-start(bf16[1,128,512]{2,1,0:T(8,128)(2,1)} %k_ref.3) | copy-start | bytes 393220
  73.1 22.4 %copy-start.7 = (bf16[1,128,512]{2,1,0:T(8,128)(2,1)S(1)}, bf16[1,128,512]{2,1,0:T(8,128)(2,1)}, u32[]{:S(2)}) copy-start(bf16[1,128,512]{2,1,0:T(8,128)(2,1)} %v_ref.3) | copy-start | bytes 393220
  73.1 22.4 %copy-start.9 = (bf16[1,128,512]{2,1,0:T(8,128)(2,1)S(1)}, bf16[1,128,512]{2,1,0:T(8,128)(2,1)}, u32[]{:S(2)}) copy-start(bf16[1,128,512]{2,1,0:T(8,128)(2,1)} %g_ref.3) | copy-start | bytes 393220

commit v2 on v1

--- a/solution.py
+++ b/solution.py
@@ -139,16 +139,28 @@
     taps_ref[...] = wide_ref[...].astype(BF)
 
 
-def mix_kernel(q_ref, k_ref, v_ref, g_ref, out_ref):
+def mix_kernel(q_hbm, k_hbm, v_hbm, g_hbm, out_ref, q_ref, k_ref, v_ref, g_ref, sems):
     groups, fields, lanes = out_ref.shape
     share = fields // 2
+    copies = [
+        pltpu.make_async_copy(source, target, sems.at[i])
+        for i, (source, target) in enumerate(
+            [(k_hbm, k_ref), (v_hbm, v_ref), (g_hbm, g_ref), (q_hbm, q_ref)]
+        )
+    ]
+    for copy in copies:
+        copy.start()
 
     def turn(a, b):
         prod = (a[0].astype(F32) * b[0].astype(F32)).astype(BF).astype(F32)
         return prod.T.reshape(groups, share, lanes)
 
-    both = jnp.concatenate([turn(k_ref, v_ref), turn(g_ref, q_ref)], axis=1)
-    out_ref[...] = both.astype(BF)
+    copies[0].wait()
+    copies[1].wait()
+    mixed = turn(k_ref, v_ref)
+    copies[2].wait()
+    copies[3].wait()
+    out_ref[...] = jnp.concatenate([mixed, turn(g_ref, q_ref)], axis=1).astype(BF)
 
 
 def gate_kernel(y_ref, q_ref, k_ref, v_ref, g_ref, go_ref, gq_ref, gk_ref, gv_ref):
@@ -179,7 +191,9 @@
     both = pl.pallas_call(
         mix_kernel,
         out_shape=jax.ShapeDtypeStruct((groups, 2 * share, tok_count), BF),
-        compiler_params=PARAMS,
+        in_specs=[pl.BlockSpec(memory_space=pltpu.HBM)] * 4,
+        scratch_shapes=[pltpu.VMEM(query_proj.shape, BF)] * 4 + [pltpu.SemaphoreType.DMA((4,))],
+        compiler_params=pltpu.CompilerParams(vmem_limit_bytes=60 * 1024 * 1024),
     )(query_proj, key_proj, value_proj, grad_output)
     both = lax.all_to_all(both, "ctx", 0, 0)
 
@@ -207,10 +221,15 @@
         scratch_shapes=[pltpu.VMEM((spec_rows, tok_count), F32)],
         compiler_params=PARAMS,
     )(spec, t["out"], t["turn_cos"], t["turn_sin"], t["g_high"], t["g_low"])
-    for flip in (1, 2, 6):
-        taps = taps.astype(BF)
-        other = lax.ppermute(taps, "dp", [(i, i ^ flip) for i in range(seqs)])
-        taps = taps.astype(F32) + other.astype(F32)
+    def exchanged(part):
+        for flip in (1, 2, 6):
+            part = part.astype(BF)
+            other = lax.ppermute(part, "dp", [(i, i ^ flip) for i in range(seqs)])
+            part = part.astype(F32) + other.astype(F32)
+        return part
+
+    cut = spec_rows * 3 // 8
+    taps = jnp.concatenate([exchanged(taps[:cut]), exchanged(taps[cut:])])
     grad_filter = taps.reshape(groups, share, tok_count).transpose(0, 2, 1).reshape(seq_len, share)
 
     grads = pl.pallas_call(

time: 97.8 us -> 81 us (0.83)
  the two profiles are of different devices: /device:TPU:24 before, /device:TPU:8 now
where the time goes in v2:
time: 81 us; the launch traced here: 80.5 us
  starting transfers between devices  43.1 us (53%)
  waiting for transfers between devices  27.5 us (34%)
  Pallas kernels  6.76 us (8%)
  local copies, waits for them, and re-layouts  1.42 us (2%)
  between operations  0.91 us (1%)
  other arithmetic  0.84 us (1%)
    all_to_all x1, waiting for transfers between devices, on_device(): both = lax.all_to_all(both, 'ctx', 0, 0)  20.8 us
    ppermute x6, starting transfers between devices, exchanged(): other = lax.ppermute(part, 'dp', [(i, i ^ flip) for i in range(seqs)])  20.6 us
    all_to_all x1, starting transfers between devices, on_device(): both = lax.all_to_all(both, 'ctx', 0, 0)  17.2 us
    ppermute x6, waiting for transfers between devices, exchanged(): other = lax.ppermute(part, 'dp', [(i, i ^ flip) for i in range(seqs)])  6.72 us
    all_to_all x1, starting transfers between devices, on_device(): out = lax.all_to_all(out, 'ctx', 0, 0)  5.26 us
    pallas_call x1, Pallas kernels, on_device(): pl.pallas_call(conv_kernel, out_shape=(jax.ShapeDtypeStruct((groups, 2 *...  2.76 us
    pallas_call x1, Pallas kernels, on_device(): pl.pallas_call(mix_kernel, out_shape=jax.ShapeDtypeStruct((groups, 2 * sh...  1.94 us
  transfers between devices with their start and end apart: 8, of which 3 were waited for; matrix products, arithmetic and copies ran while one was open for 1% of the time, Pallas kernels for 1%

profile of v2, /device:TPU:8, one launch (start us, length us, event | category | flops | bytes accessed | tf_op | source)
XLA Modules:
  0.0 80.5 jit_solution(4362905365798231210)
XLA Ops:
  0.6 1.9 %shard_map.155 = bf16[64,16,128]{2,1,0:T(8,128)(2,1)} custom-call(bf16[1,128,512]{2,1,0:T(8,128)(2,1)} %q_ref.1, bf16[1,128,512]{2,1,0:T(8,128)(2,1)} %k_ref.1, bf16[1,128,512]{2,1,0:T(8,128)(2,1)} %v_ref.1, bf16[1,128,512]{2,1,0:T(8,128)(2,1)} %g_ref.1), custom_call_target="tpu_custom_call" | custom-call | tf_op jit(solution)/shard_map/pallas_call | solution.py:191
  2.6 0.0 copy-start.11
  2.6 17.2 %all-to-all-start = ((bf16[64,16,128]{2,1,0:T(8,128)(2,1)}), bf16[64,16,128]{2,1,0:T(8,128)(2,1)S(1)}, u32[]{:S(2)}, u32[]{:S(2)}) async-start(bf16[64,16,128]{2,1,0:T(8,128)(2,1)} %shard_map.155), calls=%async_computation | async-start | bytes 524288 | tf_op jit(solution)/shard_map/all_to_all | solution.py:198
  19.9 0.0 copy-start
  19.9 0.0 copy-start.1
  19.9 0.0 copy-start.6
  19.9 0.0 copy-start.7
  19.9 0.0 copy-start.9
  19.9 0.1 copy.19
  20.0 0.8 copy-done
  20.8 0.1 copy-done.1
  20.8 0.0 copy-done.9
  20.9 0.5 shard_map.156.filt_ref
  21.4 20.8 %all-to-all-done.x_ref = bf16[64,16,128]{2,1,0:T(8,128)(2,1)S(1)} async-done(((bf16[64,16,128]{2,1,0:T(8,128)(2,1)}), bf16[64,16,128]{2,1,0:T(8,128)(2,1)S(1)}, u32[]{:S(2)}, u32[]{:S(2)}) %all-to-all-start) | async-done | bytes 262176 | tf_op jit(solution)/shard_map/all_to_all | solution.py:198
  42.2 2.8 %shard_map.157 = (bf16[64,16,128]{2,1,0:T(8,128)(2,1)}, f32[1024,256]{1,0:T(8,128)S(1)}) custom-call(bf16[64,16,128]{2,1,0:T(8,128)(2,1)S(1)} %all-to-all-done.x_ref, f32[512,256]{1,0:T(8,128)S(1)} %shard_map.156.filt_ref, bf16[128,128]{1,0:T(8,128)(2,1)S(1)} %copy-done.10, bf16[128,256]{1,0:T(8,128)(2,1)S(1)} %copy-done.8, f32[64,128]{1,0:T(8,128)S(1)} %copy-done.7, ...), custom_call_target="tpu_custom_call" | custom-call | tf_op jit(solution)/shard_map/pallas_call | solution.py:206
  44.9 0.6 shard_map.159
  45.6 4.2 %collective-permute-start = (bf16[192,128]{1,0:T(8,128)(2,1)S(1)}, bf16[192,128]{1,0:T(8,128)(2,1)S(1)}, u32[]{:S(2)}, u32[]{:S(2)}) collective-permute-start(bf16[192,128]{1,0:T(8,128)(2,1)S(1)} %slice.8), channel_id=1, source_target_pairs={{0,64},{64,0},{128,192},{192,128},{256,320},{320,256},{384,448},{4... | collective-permute-start | bytes 147464 | tf_op jit(solution)/shard_map/ppermute | solution.py:227
  49.8 5.3 %all-to-all-start.1 = ((bf16[64,16,128]{2,1,0:T(8,128)(2,1)}), bf16[64,16,128]{2,1,0:T(8,128)(2,1)S(1)}, u32[]{:S(2)}, u32[]{:S(2)}) async-start(bf16[64,16,128]{2,1,0:T(8,128)(2,1)} %get-tuple-element.11), calls=%async_computation.1 | async-start | bytes 524288 | tf_op jit(solution)/shard_map/all_to_all | solution.py:215
  55.1 2.1 %collective-permute-start.3 = (bf16[320,128]{1,0:T(8,128)(2,1)S(1)}, bf16[320,128]{1,0:T(8,128)(2,1)S(1)}, u32[]{:S(2)}, u32[]{:S(2)}) collective-permute-start(bf16[320,128]{1,0:T(8,128)(2,1)S(1)} %slice.9), channel_id=1, source_target_pairs={{0,64},{64,0},{128,192},{192,128},{256,320},{320,256},{384,448},{4... | collective-permute-start | bytes 245768 | tf_op jit(solution)/shard_map/ppermute | solution.py:227
  57.2 3.4 %collective-permute-start.1 = (bf16[192,128]{1,0:T(8,128)(2,1)S(1)}, bf16[192,128]{1,0:T(8,128)(2,1)S(1)}, u32[]{:S(2)}, u32[]{:S(2)}) collective-permute-start(bf16[192,128]{1,0:T(8,128)(2,1)S(1)} %add_convert_fusion.3), channel_id=1, source_target_pairs={{0,128},{64,192},{128,0},{192,64},{256,384},{320,448},{384,256},{4... | collective-permute-start | bytes 147464 | tf_op jit(solution)/shard_map/ppermute | solution.py:227
  60.6 2.7 %collective-permute-done.3 = bf16[320,128]{1,0:T(8,128)(2,1)S(1)} collective-permute-done((bf16[320,128]{1,0:T(8,128)(2,1)S(1)}, bf16[320,128]{1,0:T(8,128)(2,1)S(1)}, u32[]{:S(2)}, u32[]{:S(2)}) %collective-permute-start.3) | collective-permute-done | bytes 81952 | tf_op jit(solution)/shard_map/ppermute | solution.py:227
  63.4 3.4 %collective-permute-start.4 = (bf16[320,128]{1,0:T(8,128)(2,1)S(1)}, bf16[320,128]{1,0:T(8,128)(2,1)S(1)}, u32[]{:S(2)}, u32[]{:S(2)}) collective-permute-start(bf16[320,128]{1,0:T(8,128)(2,1)S(1)} %add_convert_fusion.1), channel_id=1, source_target_pairs={{0,128},{64,192},{128,0},{192,64},{256,384},{320,448},{384,256},{4... | collective-permute-start | bytes 245768 | tf_op jit(solution)/shard_map/ppermute | solution.py:227
  66.8 4.0 %collective-permute-start.2 = (bf16[192,128]{1,0:T(8,128)(2,1)S(1)}, bf16[192,128]{1,0:T(8,128)(2,1)S(1)}, u32[]{:S(2)}, u32[]{:S(2)}) collective-permute-start(bf16[192,128]{1,0:T(8,128)(2,1)S(1)} %add_convert_fusion.2), channel_id=1, source_target_pairs={{0,384},{64,448},{128,256},{192,320},{256,128},{320,192},{384,0},{... | collective-permute-start | bytes 147464 | tf_op jit(solution)/shard_map/ppermute | solution.py:227
  70.9 3.5 %collective-permute-start.5 = (bf16[320,128]{1,0:T(8,128)(2,1)S(1)}, bf16[320,128]{1,0:T(8,128)(2,1)S(1)}, u32[]{:S(2)}, u32[]{:S(2)}) collective-permute-start(bf16[320,128]{1,0:T(8,128)(2,1)S(1)} %add_convert_fusion), channel_id=1, source_target_pairs={{0,384},{64,448},{128,256},{192,320},{256,128},{320,192},{384,0},{... | collective-permute-start | bytes 245768 | tf_op jit(solution)/shard_map/ppermute | solution.py:227
  74.4 4.0 %collective-permute-done.5 = bf16[320,128]{1,0:T(8,128)(2,1)S(1)} collective-permute-done((bf16[320,128]{1,0:T(8,128)(2,1)S(1)}, bf16[320,128]{1,0:T(8,128)(2,1)S(1)}, u32[]{:S(2)}, u32[]{:S(2)}) %collective-permute-start.5) | collective-permute-done | bytes 81952 | tf_op jit(solution)/shard_map/ppermute | solution.py:227
  78.5 0.0 copy-start.4
  78.5 0.7 maximum_bitcast_fusion
  79.2 0.1 copy-done.2
  79.3 0.2 copy-done.3
  79.5 0.1 copy-done.4
  79.6 0.1 copy-done.5
  79.6 0.9 %shard_map.158 = (bf16[1,128,512]{2,1,0:T(8,128)(2,1)}, bf16[1,128,512]{2,1,0:T(8,128)(2,1)}, bf16[1,128,512]{2,1,0:T(8,128)(2,1)}, bf16[1,128,512]{2,1,0:T(8,128)(2,1)}) custom-call(bf16[64,16,128]{2,1,0:T(8,128)(2,1)S(1)} %all-to-all-done.1.y_ref, bf16[1,128,512]{2,1,0:T(8,128)(2,1)S(1)} %copy-done.2, bf16[1,128,512]{2,1,0:T(8,128)(2,1)S(1)} %copy-done.3, ...), custom_call_target="tpu_custom_call" | custom-call | tf_op jit(solution)/shard_map/pallas_call | solution.py:235
  (23 shorter events, 0.2 us)
Async XLA Ops:
  2.6 17.3 %copy-start.11 = (f32[8192,8]{0,1:T(8,128)S(1)}, f32[8192,8]{0,1:T(8,128)}, u32[]{:S(2)}) copy-start(f32[8192,8]{0,1:T(8,128)} %param.15) | copy-start | bytes 786436
  2.6 39.6 %all-to-all-start = ((bf16[64,16,128]{2,1,0:T(8,128)(2,1)}), bf16[64,16,128]{2,1,0:T(8,128)(2,1)S(1)}, u32[]{:S(2)}, u32[]{:S(2)}) async-start(bf16[64,16,128]{2,1,0:T(8,128)(2,1)} %shard_map.155), calls=%async_computation | async-start | bytes 524288 | tf_op jit(solution)/shard_map/all_to_all | solution.py:198
  19.9 0.9 %copy-start = (bf16[256,256]{1,0:T(8,128)(2,1)S(1)}, bf16[256,256]{1,0:T(8,128)(2,1)}, u32[]{:S(2)}) copy-start(bf16[256,256]{1,0:T(8,128)(2,1)} %constant.18.clone.refs_5_.gl_ref) | copy-start | bytes 393220
  19.9 1.0 %copy-start.1 = (bf16[256,256]{1,0:T(8,128)(2,1)S(1)}, bf16[256,256]{1,0:T(8,128)(2,1)}, u32[]{:S(2)}) copy-start(bf16[256,256]{1,0:T(8,128)(2,1)} %constant.17.clone.refs_4_.gh_ref) | copy-start | bytes 393220
  19.9 1.0 %copy-start.6 = (f32[64,128]{1,0:T(8,128)S(1)}, f32[64,128]{1,0:T(8,128)}, u32[]{:S(2)}) copy-start(f32[64,128]{1,0:T(8,128)} %constant.16.clone.refs_3_.sin_ref) | copy-start | bytes 98308
  19.9 0.9 %copy-start.7 = (f32[64,128]{1,0:T(8,128)S(1)}, f32[64,128]{1,0:T(8,128)}, u32[]{:S(2)}) copy-start(f32[64,128]{1,0:T(8,128)} %constant.15.clone.refs_2_.cos_ref) | copy-start | bytes 98308
  19.9 1.0 %copy-start.9 = (bf16[128,192]{1,0:T(8,128)(2,1)S(1)}, bf16[128,192]{1,0:T(8,128)(2,1)}, u32[]{:S(2)}) copy-start(bf16[128,192]{1,0:T(8,128)(2,1)} %constant.14.clone.refs_1_) | copy-start | bytes 147460
  20.9 21.3 %copy-start.8 = (bf16[128,256]{1,0:T(8,128)(2,1)S(1)}, bf16[128,256]{1,0:T(8,128)(2,1)}, u32[]{:S(2)}) copy-start(bf16[128,256]{1,0:T(8,128)(2,1)} %constant.20.clone.out_tab_ref.refs_1_) | copy-start | bytes 196612
  20.9 21.3 %copy-start.10 = (bf16[128,128]{1,0:T(8,128)(2,1)S(1)}, bf16[128,128]{1,0:T(8,128)(2,1)}, u32[]{:S(2)}) copy-start(bf16[128,128]{1,0:T(8,128)(2,1)} %constant.19.clone.into_ref) | copy-start | bytes 98308
  45.6 11.6 %collective-permute-start = (bf16[192,128]{1,0:T(8,128)(2,1)S(1)}, bf16[192,128]{1,0:T(8,128)(2,1)S(1)}, u32[]{:S(2)}, u32[]{:S(2)}) collective-permute-start(bf16[192,128]{1,0:T(8,128)(2,1)S(1)} %slice.8), channel_id=1, source_target_pairs={{0,64},{64,0},{128,192},{192,128},{256,320},{320,256},{384,448},{4... | collective-permute-start | bytes 147464 | tf_op jit(solution)/shard_map/ppermute | solution.py:227
  49.8 29.4 %all-to-all-start.1 = ((bf16[64,16,128]{2,1,0:T(8,128)(2,1)}), bf16[64,16,128]{2,1,0:T(8,128)(2,1)S(1)}, u32[]{:S(2)}, u32[]{:S(2)}) async-start(bf16[64,16,128]{2,1,0:T(8,128)(2,1)} %get-tuple-element.11), calls=%async_computation.1 | async-start | bytes 524288 | tf_op jit(solution)/shard_map/all_to_all | solution.py:215
  55.1 8.3 %collective-permute-start.3 = (bf16[320,128]{1,0:T(8,128)(2,1)S(1)}, bf16[320,128]{1,0:T(8,128)(2,1)S(1)}, u32[]{:S(2)}, u32[]{:S(2)}) collective-permute-start(bf16[320,128]{1,0:T(8,128)(2,1)S(1)} %slice.9), channel_id=1, source_target_pairs={{0,64},{64,0},{128,192},{192,128},{256,320},{320,256},{384,448},{4... | collective-permute-start | bytes 245768 | tf_op jit(solution)/shard_map/ppermute | solution.py:227
  57.2 9.6 %collective-permute-start.1 = (bf16[192,128]{1,0:T(8,128)(2,1)S(1)}, bf16[192,128]{1,0:T(8,128)(2,1)S(1)}, u32[]{:S(2)}, u32[]{:S(2)}) collective-permute-start(bf16[192,128]{1,0:T(8,128)(2,1)S(1)} %add_convert_fusion.3), channel_id=1, source_target_pairs={{0,128},{64,192},{128,0},{192,64},{256,384},{320,448},{384,256},{4... | collective-permute-start | bytes 147464 | tf_op jit(solution)/shard_map/ppermute | solution.py:227
  63.4 7.5 %collective-permute-start.4 = (bf16[320,128]{1,0:T(8,128)(2,1)S(1)}, bf16[320,128]{1,0:T(8,128)(2,1)S(1)}, u32[]{:S(2)}, u32[]{:S(2)}) collective-permute-start(bf16[320,128]{1,0:T(8,128)(2,1)S(1)} %add_convert_fusion.1), channel_id=1, source_target_pairs={{0,128},{64,192},{128,0},{192,64},{256,384},{320,448},{384,256},{4... | collective-permute-start | bytes 245768 | tf_op jit(solution)/shard_map/ppermute | solution.py:227
  66.8 7.6 %collective-permute-start.2 = (bf16[192,128]{1,0:T(8,128)(2,1)S(1)}, bf16[192,128]{1,0:T(8,128)(2,1)S(1)}, u32[]{:S(2)}, u32[]{:S(2)}) collective-permute-start(bf16[192,128]{1,0:T(8,128)(2,1)S(1)} %add_convert_fusion.2), channel_id=1, source_target_pairs={{0,384},{64,448},{128,256},{192,320},{256,128},{320,192},{384,0},{... | collective-permute-start | bytes 147464 | tf_op jit(solution)/shard_map/ppermute | solution.py:227
  70.9 7.5 %collective-permute-start.5 = (bf16[320,128]{1,0:T(8,128)(2,1)S(1)}, bf16[320,128]{1,0:T(8,128)(2,1)S(1)}, u32[]{:S(2)}, u32[]{:S(2)}) collective-permute-start(bf16[320,128]{1,0:T(8,128)(2,1)S(1)} %add_convert_fusion), channel_id=1, source_target_pairs={{0,384},{64,448},{128,256},{192,320},{256,128},{320,192},{384,0},{... | collective-permute-start | bytes 245768 | tf_op jit(solution)/shard_map/ppermute | solution.py:227
  78.4 0.9 %copy-start.2 = (bf16[1,128,512]{2,1,0:T(8,128)(2,1)S(1)}, bf16[1,128,512]{2,1,0:T(8,128)(2,1)}, u32[]{:S(2)}) copy-start(bf16[1,128,512]{2,1,0:T(8,128)(2,1)} %q_ref.1) | copy-start | bytes 393220
  78.4 1.1 %copy-start.3 = (bf16[1,128,512]{2,1,0:T(8,128)(2,1)S(1)}, bf16[1,128,512]{2,1,0:T(8,128)(2,1)}, u32[]{:S(2)}) copy-start(bf16[1,128,512]{2,1,0:T(8,128)(2,1)} %k_ref.1) | copy-start | bytes 393220
  78.5 1.1 %copy-start.4 = (bf16[1,128,512]{2,1,0:T(8,128)(2,1)S(1)}, bf16[1,128,512]{2,1,0:T(8,128)(2,1)}, u32[]{:S(2)}) copy-start(bf16[1,128,512]{2,1,0:T(8,128)(2,1)} %v_ref.1) | copy-start | bytes 393220
  78.5 1.2 %copy-start.5 = (bf16[1,128,512]{2,1,0:T(8,128)(2,1)S(1)}, bf16[1,128,512]{2,1,0:T(8,128)(2,1)}, u32[]{:S(2)}) copy-start(bf16[1,128,512]{2,1,0:T(8,128)(2,1)} %g_ref.1) | copy-start | bytes 393220

commit v3 on v2

--- a/solution.py
+++ b/solution.py
@@ -163,7 +163,8 @@
     out_ref[...] = jnp.concatenate([mixed, turn(g_ref, q_ref)], axis=1).astype(BF)
 
 
-def gate_kernel(y_ref, q_ref, k_ref, v_ref, g_ref, go_ref, gq_ref, gk_ref, gv_ref):
+def gate_kernel(y_ref, mine_ref, other_ref, q_ref, k_ref, v_ref, g_ref, go_ref, gq_ref, gk_ref, gv_ref, taps_ref):
+    taps_ref[...] = mine_ref[...].astype(F32) + other_ref[...].astype(F32)
     groups, fields, lanes = y_ref.shape
     share = fields // 2
     both = y_ref[...].astype(F32)
@@ -221,22 +222,22 @@
         scratch_shapes=[pltpu.VMEM((spec_rows, tok_count), F32)],
         compiler_params=PARAMS,
     )(spec, t["out"], t["turn_cos"], t["turn_sin"], t["g_high"], t["g_low"])
-    def exchanged(part):
-        for flip in (1, 2, 6):
-            part = part.astype(BF)
-            other = lax.ppermute(part, "dp", [(i, i ^ flip) for i in range(seqs)])
-            part = part.astype(F32) + other.astype(F32)
-        return part
-
-    cut = spec_rows * 3 // 8
-    taps = jnp.concatenate([exchanged(taps[:cut]), exchanged(taps[cut:])])
-    grad_filter = taps.reshape(groups, share, tok_count).transpose(0, 2, 1).reshape(seq_len, share)
-
-    grads = pl.pallas_call(
+    def swap(part, flip):
+        return lax.ppermute(part, "dp", [(i, i ^ flip) for i in range(seqs)])
+
+    def add(a, b):
+        return (a.astype(F32) + b.astype(F32)).astype(BF)
+
+    for flip in (1, 2):
+        taps = add(taps, swap(taps, flip))
+    other = swap(taps, 6)
+
+    *grads, grad_filter = pl.pallas_call(
         gate_kernel,
-        out_shape=[jax.ShapeDtypeStruct(query_proj.shape, BF)] * 4,
-        compiler_params=PARAMS,
-    )(out, query_proj, key_proj, value_proj, grad_output)
+        out_shape=[jax.ShapeDtypeStruct(query_proj.shape, BF)] * 4 + [jax.ShapeDtypeStruct(taps.shape, F32)],
+        compiler_params=PARAMS,
+    )(out, taps, other, query_proj, key_proj, value_proj, grad_output)
+    grad_filter = grad_filter.reshape(groups, share, tok_count).transpose(0, 2, 1).reshape(seq_len, share)
     return (*grads, grad_filter)
 
 

time: 81 us -> 76.5 us (0.944)
  the two profiles are of different devices: /device:TPU:8 before, /device:TPU:24 now
where the time goes in v3:
time: 76.5 us; the launch traced here: 76.2 us
  waiting for transfers between devices  34.2 us (45%)
  starting transfers between devices  33.2 us (43%)
  Pallas kernels  6.86 us (9%)
  local copies, waits for them, and re-layouts  0.99 us (1%)
  between operations  0.81 us (1%)
    all_to_all x1, waiting for transfers between devices, on_device(): both = lax.all_to_all(both, 'ctx', 0, 0)  20.8 us
    all_to_all x1, starting transfers between devices, on_device(): both = lax.all_to_all(both, 'ctx', 0, 0)  17.2 us
    ppermute x3, waiting for transfers between devices, swap(): return lax.ppermute(part, 'dp', [(i, i ^ flip) for i in range(seqs)])  13.4 us
    ppermute x3, starting transfers between devices, swap(): return lax.ppermute(part, 'dp', [(i, i ^ flip) for i in range(seqs)])  11.3 us
    all_to_all x1, starting transfers between devices, on_device(): out = lax.all_to_all(out, 'ctx', 0, 0)  4.66 us
    pallas_call x1, Pallas kernels, on_device(): pl.pallas_call(conv_kernel, out_shape=(jax.ShapeDtypeStruct((groups, 2 *...  2.77 us
    pallas_call x1, Pallas kernels, on_device(): pl.pallas_call(mix_kernel, out_shape=jax.ShapeDtypeStruct((groups, 2 * sh...  1.94 us
  transfers between devices with their start and end apart: 5, of which 4 were waited for; matrix products, arithmetic and copies ran while one was open for 0% of the time, Pallas kernels for 2%

profile of v3, /device:TPU:24, one launch (start us, length us, event | category | flops | bytes accessed | tf_op | source)
XLA Modules:
  0.0 76.2 jit_solution(9375040798904011573)
XLA Ops:
  0.6 1.9 %shard_map.155 = bf16[64,16,128]{2,1,0:T(8,128)(2,1)} custom-call(bf16[1,128,512]{2,1,0:T(8,128)(2,1)} %q_ref.1, bf16[1,128,512]{2,1,0:T(8,128)(2,1)} %k_ref.1, bf16[1,128,512]{2,1,0:T(8,128)(2,1)} %v_ref.1, bf16[1,128,512]{2,1,0:T(8,128)(2,1)} %g_ref.1), custom_call_target="tpu_custom_call" | custom-call | tf_op jit(solution)/shard_map/pallas_call | solution.py:192
  2.6 0.0 copy-start.11
  2.6 17.2 %all-to-all-start = ((bf16[64,16,128]{2,1,0:T(8,128)(2,1)}), bf16[64,16,128]{2,1,0:T(8,128)(2,1)S(1)}, u32[]{:S(2)}, u32[]{:S(2)}) async-start(bf16[64,16,128]{2,1,0:T(8,128)(2,1)} %shard_map.155), calls=%async_computation | async-start | bytes 524288 | tf_op jit(solution)/shard_map/all_to_all | solution.py:199
  19.8 0.0 copy-done.11
  19.9 0.0 copy-start
  19.9 0.0 copy-start.1
  19.9 0.0 copy-start.6
  19.9 0.0 copy-start.7
  19.9 0.0 copy-start.9
  19.9 0.1 copy.19
  20.0 0.8 %copy-done = bf16[256,256]{1,0:T(8,128)(2,1)S(1)} copy-done((bf16[256,256]{1,0:T(8,128)(2,1)S(1)}, bf16[256,256]{1,0:T(8,128)(2,1)}, u32[]{:S(2)}) %copy-start) | copy-done | bytes 131096
  20.8 0.1 copy-done.1
  20.8 0.0 copy-done.6
  20.8 0.0 copy-done.7
  20.8 0.0 copy-done.9
  20.9 0.5 shard_map.156.filt_ref
  21.4 20.8 %all-to-all-done.x_ref = bf16[64,16,128]{2,1,0:T(8,128)(2,1)S(1)} async-done(((bf16[64,16,128]{2,1,0:T(8,128)(2,1)}), bf16[64,16,128]{2,1,0:T(8,128)(2,1)S(1)}, u32[]{:S(2)}, u32[]{:S(2)}) %all-to-all-start) | async-done | bytes 262176 | tf_op jit(solution)/shard_map/all_to_all | solution.py:199
  42.2 0.0 copy-done.10
  42.2 2.8 %shard_map.157 = (bf16[64,16,128]{2,1,0:T(8,128)(2,1)}, f32[1024,256]{1,0:T(8,128)S(1)}) custom-call(bf16[64,16,128]{2,1,0:T(8,128)(2,1)S(1)} %all-to-all-done.x_ref, f32[512,256]{1,0:T(8,128)S(1)} %shard_map.156.filt_ref, bf16[128,128]{1,0:T(8,128)(2,1)S(1)} %copy-done.10, bf16[128,256]{1,0:T(8,128)(2,1)S(1)} %copy-done.8, f32[64,128]{1,0:T(8,128)S(1)} %copy-done.7, ...), custom_call_target="tpu_custom_call" | custom-call | tf_op jit(solution)/shard_map/pallas_call | solution.py:207
  44.9 4.7 %all-to-all-start.1 = ((bf16[64,16,128]{2,1,0:T(8,128)(2,1)}), bf16[64,16,128]{2,1,0:T(8,128)(2,1)S(1)}, u32[]{:S(2)}, u32[]{:S(2)}) async-start(bf16[64,16,128]{2,1,0:T(8,128)(2,1)} %get-tuple-element.12), calls=%async_computation.1 | async-start | bytes 524288 | tf_op jit(solution)/shard_map/all_to_all | solution.py:216
  49.6 0.6 shard_map.158
  50.2 3.1 %collective-permute-start = (bf16[512,128]{1,0:T(8,128)(2,1)S(1)}, bf16[512,128]{1,0:T(8,128)(2,1)S(1)}, u32[]{:S(2)}, u32[]{:S(2)}) collective-permute-start(bf16[512,128]{1,0:T(8,128)(2,1)S(1)} %shard_map.158), channel_id=1, source_target_pairs={{0,64},{64,0},{128,192},{192,128},{256,320},{320,256},{384,448},{4... | collective-permute-start | bytes 393224 | tf_op jit(solution)/shard_map/ppermute | solution.py:226
  53.4 6.6 %collective-permute-done = bf16[512,128]{1,0:T(8,128)(2,1)S(1)} collective-permute-done((bf16[512,128]{1,0:T(8,128)(2,1)S(1)}, bf16[512,128]{1,0:T(8,128)(2,1)S(1)}, u32[]{:S(2)}, u32[]{:S(2)}) %collective-permute-start) | collective-permute-done | bytes 131104 | tf_op jit(solution)/shard_map/ppermute | solution.py:226
  60.0 0.0 copy-start.2
  60.0 0.0 copy-start.3
  60.0 0.0 copy-start.4
  60.0 3.5 %collective-permute-start.1 = (bf16[512,128]{1,0:T(8,128)(2,1)S(1)}, bf16[512,128]{1,0:T(8,128)(2,1)S(1)}, u32[]{:S(2)}, u32[]{:S(2)}) collective-permute-start(bf16[512,128]{1,0:T(8,128)(2,1)S(1)} %add_convert_fusion.1), channel_id=1, source_target_pairs={{0,128},{64,192},{128,0},{192,64},{256,384},{320,448},{384,256},{4... | collective-permute-start | bytes 393224 | tf_op jit(solution)/shard_map/ppermute | solution.py:226
  63.6 3.5 %collective-permute-done.1 = bf16[512,128]{1,0:T(8,128)(2,1)S(1)} collective-permute-done((bf16[512,128]{1,0:T(8,128)(2,1)S(1)}, bf16[512,128]{1,0:T(8,128)(2,1)S(1)}, u32[]{:S(2)}, u32[]{:S(2)}) %collective-permute-start.1) | collective-permute-done | bytes 131104 | tf_op jit(solution)/shard_map/ppermute | solution.py:226
  67.0 4.7 %collective-permute-start.2 = (bf16[512,128]{1,0:T(8,128)(2,1)S(1)}, bf16[512,128]{1,0:T(8,128)(2,1)S(1)}, u32[]{:S(2)}, u32[]{:S(2)}) collective-permute-start(bf16[512,128]{1,0:T(8,128)(2,1)S(1)} %add_convert_fusion.mine_ref), channel_id=1, source_target_pairs={{0,384},{64,448},{128,256},{192,320},{256,128},{320,192},{384,0},{... | collective-permute-start | bytes 393224 | tf_op jit(solution)/shard_map/ppermute | solution.py:226
  71.7 3.4 %collective-permute-done.2.other_ref = bf16[512,128]{1,0:T(8,128)(2,1)S(1)} collective-permute-done((bf16[512,128]{1,0:T(8,128)(2,1)S(1)}, bf16[512,128]{1,0:T(8,128)(2,1)S(1)}, u32[]{:S(2)}, u32[]{:S(2)}) %collective-permute-start.2) | collective-permute-done | bytes 131104 | tf_op jit(solution)/shard_map/ppermute | solution.py:226
  75.1 0.0 all-to-all-done.1.y_ref
  75.2 1.0 %shard_map.159 = (bf16[1,128,512]{2,1,0:T(8,128)(2,1)}, bf16[1,128,512]{2,1,0:T(8,128)(2,1)}, bf16[1,128,512]{2,1,0:T(8,128)(2,1)}, bf16[1,128,512]{2,1,0:T(8,128)(2,1)}, f32[512,128]{1,0:T(8,128)}) custom-call(bf16[64,16,128]{2,1,0:T(8,128)(2,1)S(1)} %all-to-all-done.1.y_ref, bf16[512,128]{1,0:T(8,128)(2,1)S(1)} %add_convert_fusion.mine_ref, ...), custom_call_target="tpu_custom_call" | custom-call | tf_op jit(solution)/shard_map/pallas_call | solution.py:235
  (10 shorter events, 0.1 us)
Async XLA Ops:
  2.6 17.3 %copy-start.11 = (f32[8192,8]{0,1:T(8,128)S(1)}, f32[8192,8]{0,1:T(8,128)}, u32[]{:S(2)}) copy-start(f32[8192,8]{0,1:T(8,128)} %param.15) | copy-start | bytes 786436
  2.6 39.6 %all-to-all-start = ((bf16[64,16,128]{2,1,0:T(8,128)(2,1)}), bf16[64,16,128]{2,1,0:T(8,128)(2,1)S(1)}, u32[]{:S(2)}, u32[]{:S(2)}) async-start(bf16[64,16,128]{2,1,0:T(8,128)(2,1)} %shard_map.155), calls=%async_computation | async-start | bytes 524288 | tf_op jit(solution)/shard_map/all_to_all | solution.py:199
  19.9 0.9 %copy-start = (bf16[256,256]{1,0:T(8,128)(2,1)S(1)}, bf16[256,256]{1,0:T(8,128)(2,1)}, u32[]{:S(2)}) copy-start(bf16[256,256]{1,0:T(8,128)(2,1)} %constant.18.clone.refs_5_.gl_ref) | copy-start | bytes 393220
  19.9 1.0 %copy-start.1 = (bf16[256,256]{1,0:T(8,128)(2,1)S(1)}, bf16[256,256]{1,0:T(8,128)(2,1)}, u32[]{:S(2)}) copy-start(bf16[256,256]{1,0:T(8,128)(2,1)} %constant.17.clone.refs_4_.gh_ref) | copy-start | bytes 393220
  19.9 1.0 %copy-start.6 = (f32[64,128]{1,0:T(8,128)S(1)}, f32[64,128]{1,0:T(8,128)}, u32[]{:S(2)}) copy-start(f32[64,128]{1,0:T(8,128)} %constant.16.clone.refs_3_.sin_ref) | copy-start | bytes 98308
  19.9 0.9 %copy-start.7 = (f32[64,128]{1,0:T(8,128)S(1)}, f32[64,128]{1,0:T(8,128)}, u32[]{:S(2)}) copy-start(f32[64,128]{1,0:T(8,128)} %constant.15.clone.refs_2_.cos_ref) | copy-start | bytes 98308
  19.9 1.0 %copy-start.9 = (bf16[128,192]{1,0:T(8,128)(2,1)S(1)}, bf16[128,192]{1,0:T(8,128)(2,1)}, u32[]{:S(2)}) copy-start(bf16[128,192]{1,0:T(8,128)(2,1)} %constant.14.clone.refs_1_) | copy-start | bytes 147460
  20.9 21.3 %copy-start.8 = (bf16[128,256]{1,0:T(8,128)(2,1)S(1)}, bf16[128,256]{1,0:T(8,128)(2,1)}, u32[]{:S(2)}) copy-start(bf16[128,256]{1,0:T(8,128)(2,1)} %constant.20.clone.out_tab_ref.refs_1_) | copy-start | bytes 196612
  20.9 21.3 %copy-start.10 = (bf16[128,128]{1,0:T(8,128)(2,1)S(1)}, bf16[128,128]{1,0:T(8,128)(2,1)}, u32[]{:S(2)}) copy-start(bf16[128,128]{1,0:T(8,128)(2,1)} %constant.19.clone.into_ref) | copy-start | bytes 98308
  44.9 30.2 %all-to-all-start.1 = ((bf16[64,16,128]{2,1,0:T(8,128)(2,1)}), bf16[64,16,128]{2,1,0:T(8,128)(2,1)S(1)}, u32[]{:S(2)}, u32[]{:S(2)}) async-start(bf16[64,16,128]{2,1,0:T(8,128)(2,1)} %get-tuple-element.12), calls=%async_computation.1 | async-start | bytes 524288 | tf_op jit(solution)/shard_map/all_to_all | solution.py:216
  50.2 9.7 %collective-permute-start = (bf16[512,128]{1,0:T(8,128)(2,1)S(1)}, bf16[512,128]{1,0:T(8,128)(2,1)S(1)}, u32[]{:S(2)}, u32[]{:S(2)}) collective-permute-start(bf16[512,128]{1,0:T(8,128)(2,1)S(1)} %shard_map.158), channel_id=1, source_target_pairs={{0,64},{64,0},{128,192},{192,128},{256,320},{320,256},{384,448},{4... | collective-permute-start | bytes 393224 | tf_op jit(solution)/shard_map/ppermute | solution.py:226
  59.9 15.2 %copy-start.5 = (bf16[1,128,512]{2,1,0:T(8,128)(2,1)S(1)}, bf16[1,128,512]{2,1,0:T(8,128)(2,1)}, u32[]{:S(2)}) copy-start(bf16[1,128,512]{2,1,0:T(8,128)(2,1)} %g_ref.1) | copy-start | bytes 393220
  60.0 15.2 %copy-start.2 = (bf16[1,128,512]{2,1,0:T(8,128)(2,1)S(1)}, bf16[1,128,512]{2,1,0:T(8,128)(2,1)}, u32[]{:S(2)}) copy-start(bf16[1,128,512]{2,1,0:T(8,128)(2,1)} %q_ref.1) | copy-start | bytes 393220
  60.0 15.1 %copy-start.3 = (bf16[1,128,512]{2,1,0:T(8,128)(2,1)S(1)}, bf16[1,128,512]{2,1,0:T(8,128)(2,1)}, u32[]{:S(2)}) copy-start(bf16[1,128,512]{2,1,0:T(8,128)(2,1)} %k_ref.1) | copy-start | bytes 393220
  60.0 15.1 %copy-start.4 = (bf16[1,128,512]{2,1,0:T(8,128)(2,1)S(1)}, bf16[1,128,512]{2,1,0:T(8,128)(2,1)}, u32[]{:S(2)}) copy-start(bf16[1,128,512]{2,1,0:T(8,128)(2,1)} %v_ref.1) | copy-start | bytes 393220
  60.0 7.0 %collective-permute-start.1 = (bf16[512,128]{1,0:T(8,128)(2,1)S(1)}, bf16[512,128]{1,0:T(8,128)(2,1)S(1)}, u32[]{:S(2)}, u32[]{:S(2)}) collective-permute-start(bf16[512,128]{1,0:T(8,128)(2,1)S(1)} %add_convert_fusion.1), channel_id=1, source_target_pairs={{0,128},{64,192},{128,0},{192,64},{256,384},{320,448},{384,256},{4... | collective-permute-start | bytes 393224 | tf_op jit(solution)/shard_map/ppermute | solution.py:226
  67.0 8.1 %collective-permute-start.2 = (bf16[512,128]{1,0:T(8,128)(2,1)S(1)}, bf16[512,128]{1,0:T(8,128)(2,1)S(1)}, u32[]{:S(2)}, u32[]{:S(2)}) collective-permute-start(bf16[512,128]{1,0:T(8,128)(2,1)S(1)} %add_convert_fusion.mine_ref), channel_id=1, source_target_pairs={{0,384},{64,448},{128,256},{192,320},{256,128},{320,192},{384,0},{... | collective-permute-start | bytes 393224 | tf_op jit(solution)/shard_map/ppermute | solution.py:226

commit v4 on v3

--- a/solution.py
+++ b/solution.py
@@ -228,10 +228,10 @@
     def add(a, b):
         return (a.astype(F32) + b.astype(F32)).astype(BF)
 
-    for flip in (1, 2):
-        taps = add(taps, swap(taps, flip))
-    other = swap(taps, 6)
-
+    a, b, c = swap(taps, 2), swap(taps, 6), swap(taps, 4)
+    taps = (taps.astype(F32) + c.astype(F32)) + (a.astype(F32) + b.astype(F32))
+    taps = taps.astype(BF)
+    other = swap(taps, 1)
     *grads, grad_filter = pl.pallas_call(
         gate_kernel,
         out_shape=[jax.ShapeDtypeStruct(query_proj.shape, BF)] * 4 + [jax.ShapeDtypeStruct(taps.shape, F32)],

time: 76.5 us -> 75.9 us (level)
  waiting for transfers between devices: 34.2 us -> 30.8 us
  starting transfers between devices: 33.2 us -> 35.6 us
    ppermute x3 -> x4, waiting for transfers between devices: 13.4 us -> 10 us  [swap(): return lax.ppermute(part, 'dp', [(i, i ^ flip) for i in range(seqs)])]
    ppermute x3 -> x4, starting transfers between devices: 11.3 us -> 13.7 us  [swap(): return lax.ppermute(part, 'dp', [(i, i ^ flip) for i in range(seqs)])]
  transfers between devices with their start and end apart: 5 -> 6, of which waited for: 4 -> 4; matrix products, arithmetic and copies ran while one was open for 0% -> 0% of each run, Pallas kernels for 2% -> 2%
where the time goes in v4:
time: 75.9 us; the launch traced here: 75.2 us
  starting transfers between devices  35.6 us (47%)
  waiting for transfers between devices  30.8 us (41%)
  Pallas kernels  6.86 us (9%)
  local copies, waits for them, and re-layouts  0.99 us (1%)
  between operations  0.83 us (1%)
    all_to_all x1, waiting for transfers between devices, on_device(): both = lax.all_to_all(both, 'ctx', 0, 0)  20.8 us
    all_to_all x1, starting transfers between devices, on_device(): both = lax.all_to_all(both, 'ctx', 0, 0)  17.2 us
    ppermute x4, starting transfers between devices, swap(): return lax.ppermute(part, 'dp', [(i, i ^ flip) for i in range(seqs)])  13.7 us
    ppermute x4, waiting for transfers between devices, swap(): return lax.ppermute(part, 'dp', [(i, i ^ flip) for i in range(seqs)])  10 us
    all_to_all x1, starting transfers between devices, on_device(): out = lax.all_to_all(out, 'ctx', 0, 0)  4.66 us
    pallas_call x1, Pallas kernels, on_device(): pl.pallas_call(conv_kernel, out_shape=(jax.ShapeDtypeStruct((groups, 2 *...  2.77 us
    pallas_call x1, Pallas kernels, on_device(): pl.pallas_call(mix_kernel, out_shape=jax.ShapeDtypeStruct((groups, 2 * sh...  1.94 us
  transfers between devices with their start and end apart: 6, of which 4 were waited for; matrix products, arithmetic and copies ran while one was open for 0% of the time, Pallas kernels for 2%

profile of v4, /device:TPU:24, one launch (start us, length us, event | category | flops | bytes accessed | tf_op | source)
XLA Modules:
  0.0 75.2 jit_solution(6529812423858277743)
XLA Ops:
  0.6 1.9 %shard_map.155 = bf16[64,16,128]{2,1,0:T(8,128)(2,1)} custom-call(bf16[1,128,512]{2,1,0:T(8,128)(2,1)} %q_ref.1, bf16[1,128,512]{2,1,0:T(8,128)(2,1)} %k_ref.1, bf16[1,128,512]{2,1,0:T(8,128)(2,1)} %v_ref.1, bf16[1,128,512]{2,1,0:T(8,128)(2,1)} %g_ref.1), custom_call_target="tpu_custom_call" | custom-call | tf_op jit(solution)/shard_map/pallas_call | solution.py:192
  2.6 0.0 copy-start.11
  2.6 17.2 %all-to-all-start = ((bf16[64,16,128]{2,1,0:T(8,128)(2,1)}), bf16[64,16,128]{2,1,0:T(8,128)(2,1)S(1)}, u32[]{:S(2)}, u32[]{:S(2)}) async-start(bf16[64,16,128]{2,1,0:T(8,128)(2,1)} %shard_map.155), calls=%async_computation | async-start | bytes 524288 | tf_op jit(solution)/shard_map/all_to_all | solution.py:199
  19.9 0.0 copy-start
  19.9 0.0 copy-start.1
  19.9 0.0 copy-start.6
  19.9 0.0 copy-start.7
  19.9 0.0 copy-start.9
  19.9 0.1 copy.19
  20.0 0.8 %copy-done = bf16[256,256]{1,0:T(8,128)(2,1)S(1)} copy-done((bf16[256,256]{1,0:T(8,128)(2,1)S(1)}, bf16[256,256]{1,0:T(8,128)(2,1)}, u32[]{:S(2)}) %copy-start) | copy-done | bytes 131096
  20.8 0.1 copy-done.1
  20.8 0.0 copy-done.9
  20.9 0.5 shard_map.156.filt_ref
  21.4 20.8 %all-to-all-done.x_ref = bf16[64,16,128]{2,1,0:T(8,128)(2,1)S(1)} async-done(((bf16[64,16,128]{2,1,0:T(8,128)(2,1)}), bf16[64,16,128]{2,1,0:T(8,128)(2,1)S(1)}, u32[]{:S(2)}, u32[]{:S(2)}) %all-to-all-start) | async-done | bytes 262176 | tf_op jit(solution)/shard_map/all_to_all | solution.py:199
  42.2 2.8 %shard_map.157 = (bf16[64,16,128]{2,1,0:T(8,128)(2,1)}, f32[1024,256]{1,0:T(8,128)S(1)}) custom-call(bf16[64,16,128]{2,1,0:T(8,128)(2,1)S(1)} %all-to-all-done.x_ref, f32[512,256]{1,0:T(8,128)S(1)} %shard_map.156.filt_ref, bf16[128,128]{1,0:T(8,128)(2,1)S(1)} %copy-done.10, bf16[128,256]{1,0:T(8,128)(2,1)S(1)} %copy-done.8, f32[64,128]{1,0:T(8,128)S(1)} %copy-done.7, ...), custom_call_target="tpu_custom_call" | custom-call | tf_op jit(solution)/shard_map/pallas_call | solution.py:207
  44.9 4.7 %all-to-all-start.1 = ((bf16[64,16,128]{2,1,0:T(8,128)(2,1)}), bf16[64,16,128]{2,1,0:T(8,128)(2,1)S(1)}, u32[]{:S(2)}, u32[]{:S(2)}) async-start(bf16[64,16,128]{2,1,0:T(8,128)(2,1)} %get-tuple-element.12), calls=%async_computation.1 | async-start | bytes 524288 | tf_op jit(solution)/shard_map/all_to_all | solution.py:216
  49.6 0.6 shard_map.158
  50.2 0.0 copy-start.2
  50.2 0.0 copy-start.3
  50.3 0.0 copy-start.4
  50.3 0.0 copy-start.5
  50.3 4.8 %collective-permute-start.2 = (bf16[512,128]{1,0:T(8,128)(2,1)S(1)}, bf16[512,128]{1,0:T(8,128)(2,1)S(1)}, u32[]{:S(2)}, u32[]{:S(2)}) collective-permute-start(bf16[512,128]{1,0:T(8,128)(2,1)S(1)} %shard_map.158), channel_id=1, source_target_pairs={{0,384},{64,448},{128,256},{192,320},{256,128},{320,192},{384,0},{... | collective-permute-start | bytes 393224 | tf_op jit(solution)/shard_map/ppermute | solution.py:226
  55.1 2.1 %collective-permute-start.1 = (bf16[512,128]{1,0:T(8,128)(2,1)S(1)}, bf16[512,128]{1,0:T(8,128)(2,1)S(1)}, u32[]{:S(2)}, u32[]{:S(2)}) collective-permute-start(bf16[512,128]{1,0:T(8,128)(2,1)S(1)} %shard_map.158), channel_id=1, source_target_pairs={{0,128},{64,192},{128,0},{192,64},{256,384},{320,448},{384,256},{4... | collective-permute-start | bytes 393224 | tf_op jit(solution)/shard_map/ppermute | solution.py:226
  57.2 3.6 %collective-permute-start = (bf16[512,128]{1,0:T(8,128)(2,1)S(1)}, bf16[512,128]{1,0:T(8,128)(2,1)S(1)}, u32[]{:S(2)}, u32[]{:S(2)}) collective-permute-start(bf16[512,128]{1,0:T(8,128)(2,1)S(1)} %shard_map.158), channel_id=1, source_target_pairs={{0,256},{64,320},{128,384},{192,448},{256,0},{320,64},{384,128},{4... | collective-permute-start | bytes 393224 | tf_op jit(solution)/shard_map/ppermute | solution.py:226
  60.9 0.0 collective-permute-done.2
  60.9 2.3 %collective-permute-done.1 = bf16[512,128]{1,0:T(8,128)(2,1)S(1)} collective-permute-done((bf16[512,128]{1,0:T(8,128)(2,1)S(1)}, bf16[512,128]{1,0:T(8,128)(2,1)S(1)}, u32[]{:S(2)}, u32[]{:S(2)}) %collective-permute-start.1) | collective-permute-done | bytes 131104 | tf_op jit(solution)/shard_map/ppermute | solution.py:226
  63.2 2.5 %collective-permute-done = bf16[512,128]{1,0:T(8,128)(2,1)S(1)} collective-permute-done((bf16[512,128]{1,0:T(8,128)(2,1)S(1)}, bf16[512,128]{1,0:T(8,128)(2,1)S(1)}, u32[]{:S(2)}, u32[]{:S(2)}) %collective-permute-start) | collective-permute-done | bytes 131104 | tf_op jit(solution)/shard_map/ppermute | solution.py:226
  65.7 0.1 add_convert_fusion.mine_ref
  65.8 3.1 %collective-permute-start.3 = (bf16[512,128]{1,0:T(8,128)(2,1)S(1)}, bf16[512,128]{1,0:T(8,128)(2,1)S(1)}, u32[]{:S(2)}, u32[]{:S(2)}) collective-permute-start(bf16[512,128]{1,0:T(8,128)(2,1)S(1)} %add_convert_fusion.mine_ref), channel_id=1, source_target_pairs={{0,64},{64,0},{128,192},{192,128},{256,320},{320,256},{384,448},{4... | collective-permute-start | bytes 393224 | tf_op jit(solution)/shard_map/ppermute | solution.py:226
  68.9 5.2 %collective-permute-done.3.other_ref = bf16[512,128]{1,0:T(8,128)(2,1)S(1)} collective-permute-done((bf16[512,128]{1,0:T(8,128)(2,1)S(1)}, bf16[512,128]{1,0:T(8,128)(2,1)S(1)}, u32[]{:S(2)}, u32[]{:S(2)}) %collective-permute-start.3) | collective-permute-done | bytes 131104 | tf_op jit(solution)/shard_map/ppermute | solution.py:226
  74.1 0.0 all-to-all-done.1.y_ref
  74.2 1.0 %shard_map.159 = (bf16[1,128,512]{2,1,0:T(8,128)(2,1)}, bf16[1,128,512]{2,1,0:T(8,128)(2,1)}, bf16[1,128,512]{2,1,0:T(8,128)(2,1)}, bf16[1,128,512]{2,1,0:T(8,128)(2,1)}, f32[512,128]{1,0:T(8,128)}) custom-call(bf16[64,16,128]{2,1,0:T(8,128)(2,1)S(1)} %all-to-all-done.1.y_ref, bf16[512,128]{1,0:T(8,128)(2,1)S(1)} %add_convert_fusion.mine_ref, ...), custom_call_target="tpu_custom_call" | custom-call | tf_op jit(solution)/shard_map/pallas_call | solution.py:235
  (11 shorter events, 0.0 us)
Async XLA Ops:
  2.6 17.3 %copy-start.11 = (f32[8192,8]{0,1:T(8,128)S(1)}, f32[8192,8]{0,1:T(8,128)}, u32[]{:S(2)}) copy-start(f32[8192,8]{0,1:T(8,128)} %param.15) | copy-start | bytes 786436
  2.6 39.6 %all-to-all-start = ((bf16[64,16,128]{2,1,0:T(8,128)(2,1)}), bf16[64,16,128]{2,1,0:T(8,128)(2,1)S(1)}, u32[]{:S(2)}, u32[]{:S(2)}) async-start(bf16[64,16,128]{2,1,0:T(8,128)(2,1)} %shard_map.155), calls=%async_computation | async-start | bytes 524288 | tf_op jit(solution)/shard_map/all_to_all | solution.py:199
  19.9 0.9 %copy-start = (bf16[256,256]{1,0:T(8,128)(2,1)S(1)}, bf16[256,256]{1,0:T(8,128)(2,1)}, u32[]{:S(2)}) copy-start(bf16[256,256]{1,0:T(8,128)(2,1)} %constant.18.clone.refs_5_.gl_ref) | copy-start | bytes 393220
  19.9 1.0 %copy-start.1 = (bf16[256,256]{1,0:T(8,128)(2,1)S(1)}, bf16[256,256]{1,0:T(8,128)(2,1)}, u32[]{:S(2)}) copy-start(bf16[256,256]{1,0:T(8,128)(2,1)} %constant.17.clone.refs_4_.gh_ref) | copy-start | bytes 393220
  19.9 1.0 %copy-start.6 = (f32[64,128]{1,0:T(8,128)S(1)}, f32[64,128]{1,0:T(8,128)}, u32[]{:S(2)}) copy-start(f32[64,128]{1,0:T(8,128)} %constant.16.clone.refs_3_.sin_ref) | copy-start | bytes 98308
  19.9 0.9 %copy-start.7 = (f32[64,128]{1,0:T(8,128)S(1)}, f32[64,128]{1,0:T(8,128)}, u32[]{:S(2)}) copy-start(f32[64,128]{1,0:T(8,128)} %constant.15.clone.refs_2_.cos_ref) | copy-start | bytes 98308
  19.9 1.0 %copy-start.9 = (bf16[128,192]{1,0:T(8,128)(2,1)S(1)}, bf16[128,192]{1,0:T(8,128)(2,1)}, u32[]{:S(2)}) copy-start(bf16[128,192]{1,0:T(8,128)(2,1)} %constant.14.clone.refs_1_) | copy-start | bytes 147460
  20.9 21.3 %copy-start.8 = (bf16[128,256]{1,0:T(8,128)(2,1)S(1)}, bf16[128,256]{1,0:T(8,128)(2,1)}, u32[]{:S(2)}) copy-start(bf16[128,256]{1,0:T(8,128)(2,1)} %constant.20.clone.out_tab_ref.refs_1_) | copy-start | bytes 196612
  20.9 21.3 %copy-start.10 = (bf16[128,128]{1,0:T(8,128)(2,1)S(1)}, bf16[128,128]{1,0:T(8,128)(2,1)}, u32[]{:S(2)}) copy-start(bf16[128,128]{1,0:T(8,128)(2,1)} %constant.19.clone.into_ref) | copy-start | bytes 98308
  44.9 29.2 %all-to-all-start.1 = ((bf16[64,16,128]{2,1,0:T(8,128)(2,1)}), bf16[64,16,128]{2,1,0:T(8,128)(2,1)S(1)}, u32[]{:S(2)}, u32[]{:S(2)}) async-start(bf16[64,16,128]{2,1,0:T(8,128)(2,1)} %get-tuple-element.12), calls=%async_computation.1 | async-start | bytes 524288 | tf_op jit(solution)/shard_map/all_to_all | solution.py:216
  50.2 23.9 %copy-start.2 = (bf16[1,128,512]{2,1,0:T(8,128)(2,1)S(1)}, bf16[1,128,512]{2,1,0:T(8,128)(2,1)}, u32[]{:S(2)}) copy-start(bf16[1,128,512]{2,1,0:T(8,128)(2,1)} %q_ref.1) | copy-start | bytes 393220
  50.2 23.9 %copy-start.3 = (bf16[1,128,512]{2,1,0:T(8,128)(2,1)S(1)}, bf16[1,128,512]{2,1,0:T(8,128)(2,1)}, u32[]{:S(2)}) copy-start(bf16[1,128,512]{2,1,0:T(8,128)(2,1)} %k_ref.1) | copy-start | bytes 393220
  50.3 23.9 %copy-start.4 = (bf16[1,128,512]{2,1,0:T(8,128)(2,1)S(1)}, bf16[1,128,512]{2,1,0:T(8,128)(2,1)}, u32[]{:S(2)}) copy-start(bf16[1,128,512]{2,1,0:T(8,128)(2,1)} %v_ref.1) | copy-start | bytes 393220
  50.3 23.9 %copy-start.5 = (bf16[1,128,512]{2,1,0:T(8,128)(2,1)S(1)}, bf16[1,128,512]{2,1,0:T(8,128)(2,1)}, u32[]{:S(2)}) copy-start(bf16[1,128,512]{2,1,0:T(8,128)(2,1)} %g_ref.1) | copy-start | bytes 393220
  50.3 10.6 %collective-permute-start.2 = (bf16[512,128]{1,0:T(8,128)(2,1)S(1)}, bf16[512,128]{1,0:T(8,128)(2,1)S(1)}, u32[]{:S(2)}, u32[]{:S(2)}) collective-permute-start(bf16[512,128]{1,0:T(8,128)(2,1)S(1)} %shard_map.158), channel_id=1, source_target_pairs={{0,384},{64,448},{128,256},{192,320},{256,128},{320,192},{384,0},{... | collective-permute-start | bytes 393224 | tf_op jit(solution)/shard_map/ppermute | solution.py:226
  55.1 8.1 %collective-permute-start.1 = (bf16[512,128]{1,0:T(8,128)(2,1)S(1)}, bf16[512,128]{1,0:T(8,128)(2,1)S(1)}, u32[]{:S(2)}, u32[]{:S(2)}) collective-permute-start(bf16[512,128]{1,0:T(8,128)(2,1)S(1)} %shard_map.158), channel_id=1, source_target_pairs={{0,128},{64,192},{128,0},{192,64},{256,384},{320,448},{384,256},{4... | collective-permute-start | bytes 393224 | tf_op jit(solution)/shard_map/ppermute | solution.py:226
  57.2 8.5 %collective-permute-start = (bf16[512,128]{1,0:T(8,128)(2,1)S(1)}, bf16[512,128]{1,0:T(8,128)(2,1)S(1)}, u32[]{:S(2)}, u32[]{:S(2)}) collective-permute-start(bf16[512,128]{1,0:T(8,128)(2,1)S(1)} %shard_map.158), channel_id=1, source_target_pairs={{0,256},{64,320},{128,384},{192,448},{256,0},{320,64},{384,128},{4... | collective-permute-start | bytes 393224 | tf_op jit(solution)/shard_map/ppermute | solution.py:226
  65.8 8.4 %collective-permute-start.3 = (bf16[512,128]{1,0:T(8,128)(2,1)S(1)}, bf16[512,128]{1,0:T(8,128)(2,1)S(1)}, u32[]{:S(2)}, u32[]{:S(2)}) collective-permute-start(bf16[512,128]{1,0:T(8,128)(2,1)S(1)} %add_convert_fusion.mine_ref), channel_id=1, source_target_pairs={{0,64},{64,0},{128,192},{192,128},{256,320},{320,256},{384,448},{4... | collective-permute-start | bytes 393224 | tf_op jit(solution)/shard_map/ppermute | solution.py:226

commit v5 on v4

--- a/solution.py
+++ b/solution.py
@@ -11,6 +11,7 @@
 
 BF = jnp.bfloat16
 F32 = jnp.float32
+CHUNK = 256
 
 
 def halves(table):
@@ -95,48 +96,55 @@
     spec_ref[...] = across(high, low, gh_ref[...], gl_ref[...]) * scale
 
 
-def conv_kernel(x_ref, filt_ref, into_ref, out_tab_ref, cos_ref, sin_ref, gh_ref, gl_ref, y_ref, spec_ref, wide_ref):
+def conv_kernel(
+    scale, x_ref, filt_ref, into_ref, out_tab_ref, cos_ref, sin_ref, gh_ref, gl_ref,
+    y_ref, taps_ref, wide_ref, wide_taps_ref, high_ref, low_ref, spec_ref, inner_ref,
+):
     blocks, fields, lanes = x_ref.shape
     share = fields // 2
+    step = 2 * blocks
+    half = share // 2
     cos, sin = cos_ref[...], sin_ref[...]
     wide_ref[...] = x_ref[...].astype(F32).reshape(blocks * fields, lanes)
-    rows = []
-    for pair in range(fields // 2):
+
+    def put(i, parts):
+        high, low = split(jnp.concatenate(parts, axis=1))
+        high_ref[i * step:(i + 1) * step] = high
+        low_ref[i * step:(i + 1) * step] = low
+
+    def transform(count, out_ref):
+        for start in range(0, count * step, CHUNK):
+            rows = slice(start, min(start + CHUNK, count * step))
+            out_ref[rows] = across(high_ref[rows], low_ref[rows], gh_ref[...], gl_ref[...])
+
+    for i in range(share):
         x = jnp.concatenate(
-            [wide_ref[pl.ds(2 * pair + one, blocks, stride=fields), :] for one in range(2)], axis=1
+            [wide_ref[pl.ds(2 * i + one, blocks, stride=fields), :] for one in range(2)], axis=1
         ).astype(BF)
         part = dot(into_ref[...], jnp.concatenate([x, x], axis=0))
-        rows.append(turned(part[:, :lanes], blocks, cos, sin))
-        rows.append(turned(part[:, lanes:], blocks, cos, sin))
-    high, low = split(jnp.concatenate(rows, axis=0))
-    spec_ref[...] = across(high, low, gh_ref[...], gl_ref[...])
-    half = share * blocks
-    fr, fi = filt_ref[:, :lanes], filt_ref[:, lanes:]
-    xr, xi = spec_ref[:half, :lanes], spec_ref[:half, lanes:]
-    gr, gi = spec_ref[half:, :lanes], spec_ref[half:, lanes:]
-    conv = jnp.concatenate([fr * xi + fi * xr, fr * xr - fi * xi], axis=1)
-    back = jnp.concatenate([fr * gi - fi * gr, fr * gr + fi * gi], axis=1)
-    high, low = split(jnp.concatenate([conv, back], axis=0))
-    inner = across(high, low, gh_ref[...], gl_ref[...])
-    ys = back_to_positions(inner, out_tab_ref, cos, sin, blocks, lanes)
-    for f, y in enumerate(ys):
-        wide_ref[pl.ds(f, blocks, stride=fields), :] = y
+        turns = [turned(part[:, one * lanes:(one + 1) * lanes], blocks, cos, sin) for one in range(2)]
+        put(i, [jnp.concatenate(turns, axis=0)])
+    transform(share, spec_ref)
+    for i in range(half):
+        xs = spec_ref[i * step:(i + 1) * step]
+        gs = spec_ref[(half + i) * step:(half + i + 1) * step]
+        fs = filt_ref[i * step:(i + 1) * step]
+        xr, xi, gr, gi = xs[:, :lanes], xs[:, lanes:], gs[:, :lanes], gs[:, lanes:]
+        fr, fi = fs[:, :lanes], fs[:, lanes:]
+        put(i, [fr * xi + fi * xr, fr * xr - fi * xi])
+        put(half + i, [fr * gi - fi * gr, fr * gr + fi * gi])
+        put(share + i, [scale * (xr * gi - xi * gr), scale * (xr * gr + xi * gi)])
+    transform(share + half, inner_ref)
+    for i in range(share + half):
+        inner = inner_ref[i * step:(i + 1) * step]
+        for one, y in enumerate(back_to_positions(inner, out_tab_ref, cos, sin, blocks, lanes)):
+            field = 2 * i + one
+            if field < fields:
+                wide_ref[pl.ds(field, blocks, stride=fields), :] = y
+            else:
+                wide_taps_ref[pl.ds(field - fields, blocks, stride=share), :] = y
     y_ref[...] = wide_ref[...].reshape(blocks, fields, lanes).astype(BF)
-
-
-def taps_kernel(scale, spec_ref, out_tab_ref, cos_ref, sin_ref, gh_ref, gl_ref, taps_ref, wide_ref):
-    blocks, lanes = cos_ref.shape
-    half = spec_ref.shape[0] // 2
-    share = half // blocks
-    cos, sin = cos_ref[...], sin_ref[...]
-    xr, xi = spec_ref[:half, :lanes], spec_ref[:half, lanes:]
-    gr, gi = spec_ref[half:, :lanes], spec_ref[half:, lanes:]
-    prod = jnp.concatenate([xr * gi - xi * gr, xr * gr + xi * gi], axis=1)
-    high, low = split(prod * scale)
-    inner = across(high, low, gh_ref[...], gl_ref[...])
-    for c, y in enumerate(back_to_positions(inner, out_tab_ref, cos, sin, blocks, lanes)):
-        wide_ref[pl.ds(c, blocks, stride=share), :] = y
-    taps_ref[...] = wide_ref[...].astype(BF)
+    taps_ref[...] = wide_taps_ref[...].astype(BF)
 
 
 def mix_kernel(q_hbm, k_hbm, v_hbm, g_hbm, out_ref, q_ref, k_ref, v_ref, g_ref, sems):
@@ -204,24 +212,25 @@
         compiler_params=PARAMS,
     )(long_filter.T.reshape(share, groups, tok_count), t["into3"], t["turn_cos"], t["turn_sin"], t["g_high"], t["g_low"])
 
-    out, spec = pl.pallas_call(
-        conv_kernel,
+    factor = 1.0 / math.sqrt(seq_len * seqs)
+    out, taps = pl.pallas_call(
+        lambda *refs: conv_kernel(factor * 2.0 / (2 * seq_len), *refs),
         out_shape=(
             jax.ShapeDtypeStruct((groups, 2 * share, tok_count), BF),
-            jax.ShapeDtypeStruct((2 * spec_rows, 2 * tok_count), F32),
+            jax.ShapeDtypeStruct((spec_rows, tok_count), BF),
         ),
-        scratch_shapes=[pltpu.VMEM((2 * spec_rows, tok_count), F32)],
+        scratch_shapes=[
+            pltpu.VMEM((2 * spec_rows, tok_count), F32),
+            pltpu.VMEM((spec_rows, tok_count), F32),
+            pltpu.VMEM((3 * spec_rows, 2 * tok_count), BF),
+            pltpu.VMEM((3 * spec_rows, 2 * tok_count), BF),
+            pltpu.VMEM((2 * spec_rows, 2 * tok_count), F32),
+            pltpu.VMEM((3 * spec_rows, 2 * tok_count), F32),
+        ],
         compiler_params=PARAMS,
     )(both, filt_spec, t["into"], t["out"], t["turn_cos"], t["turn_sin"], t["g_high"], t["g_low"])
     out = lax.all_to_all(out, "ctx", 0, 0)
 
-    factor = 1.0 / math.sqrt(seq_len * seqs)
-    taps = pl.pallas_call(
-        lambda *refs: taps_kernel(factor * 2.0 / (2 * seq_len), *refs),
-        out_shape=jax.ShapeDtypeStruct((spec_rows, tok_count), BF),
-        scratch_shapes=[pltpu.VMEM((spec_rows, tok_count), F32)],
-        compiler_params=PARAMS,
-    )(spec, t["out"], t["turn_cos"], t["turn_sin"], t["g_high"], t["g_low"])
     def swap(part, flip):
         return lax.ppermute(part, "dp", [(i, i ^ flip) for i in range(seqs)])
 

time: 75.9 us -> 74.9 us (0.987)
  Pallas kernels: 6.86 us -> 5.87 us
    pallas_call x2 -> x1, Pallas kernels: 3.38 us -> 2.39 us  [on_device(): pl.pallas_call(lambda *refs: conv_kernel(factor * 2.0 / (2 * seq_len), *r...]
  transfers between devices with their start and end apart: 6 -> 6, of which waited for: 4 -> 4; matrix products, arithmetic and copies ran while one was open for 0% -> 0% of each run, Pallas kernels for 2% -> 1%
where the time goes in v5:
time: 74.9 us; the launch traced here: 74.2 us
  starting transfers between devices  35.6 us (48%)
  waiting for transfers between devices  30.8 us (41%)
  Pallas kernels  5.87 us (8%)
  local copies, waits for them, and re-layouts  0.99 us (1%)
  between operations  0.83 us (1%)
    all_to_all x1, waiting for transfers between devices, on_device(): both = lax.all_to_all(both, 'ctx', 0, 0)  20.8 us
    all_to_all x1, starting transfers between devices, on_device(): both = lax.all_to_all(both, 'ctx', 0, 0)  17.2 us
    ppermute x4, starting transfers between devices, swap(): return lax.ppermute(part, 'dp', [(i, i ^ flip) for i in range(seqs)])  13.7 us
    ppermute x4, waiting for transfers between devices, swap(): return lax.ppermute(part, 'dp', [(i, i ^ flip) for i in range(seqs)])  10 us
    all_to_all x1, starting transfers between devices, on_device(): out = lax.all_to_all(out, 'ctx', 0, 0)  4.65 us
    pallas_call x1, Pallas kernels, on_device(): pl.pallas_call(lambda *refs: conv_kernel(factor * 2.0 / (2 * seq_len), *r...  2.39 us
    pallas_call x1, Pallas kernels, on_device(): pl.pallas_call(mix_kernel, out_shape=jax.ShapeDtypeStruct((groups, 2 * sh...  1.94 us
  transfers between devices with their start and end apart: 6, of which 4 were waited for; matrix products, arithmetic and copies ran while one was open for 0% of the time, Pallas kernels for 1%

profile of v5, /device:TPU:24, one launch (start us, length us, event | category | flops | bytes accessed | tf_op | source)
XLA Modules:
  0.0 74.2 jit_solution(9980031840463516326)
XLA Ops:
  0.6 1.9 %shard_map.155 = bf16[64,16,128]{2,1,0:T(8,128)(2,1)} custom-call(bf16[1,128,512]{2,1,0:T(8,128)(2,1)} %q_ref.1, bf16[1,128,512]{2,1,0:T(8,128)(2,1)} %k_ref.1, bf16[1,128,512]{2,1,0:T(8,128)(2,1)} %v_ref.1, bf16[1,128,512]{2,1,0:T(8,128)(2,1)} %g_ref.1), custom_call_target="tpu_custom_call" | custom-call | tf_op jit(solution)/shard_map/pallas_call | solution.py:200
  2.6 0.0 copy-start.11
  2.6 17.2 %all-to-all-start = ((bf16[64,16,128]{2,1,0:T(8,128)(2,1)}), bf16[64,16,128]{2,1,0:T(8,128)(2,1)S(1)}, u32[]{:S(2)}, u32[]{:S(2)}) async-start(bf16[64,16,128]{2,1,0:T(8,128)(2,1)} %shard_map.155), calls=%async_computation | async-start | bytes 524288 | tf_op jit(solution)/shard_map/all_to_all | solution.py:207
  19.9 0.0 copy-start
  19.9 0.0 copy-start.1
  19.9 0.0 copy-start.6
  19.9 0.0 copy-start.7
  19.9 0.0 copy-start.9
  19.9 0.1 copy.19
  20.0 0.8 %copy-done = bf16[256,256]{1,0:T(8,128)(2,1)S(1)} copy-done((bf16[256,256]{1,0:T(8,128)(2,1)S(1)}, bf16[256,256]{1,0:T(8,128)(2,1)}, u32[]{:S(2)}) %copy-start) | copy-done | bytes 131096
  20.8 0.1 copy-done.1
  20.8 0.0 copy-done.9
  20.9 0.5 shard_map.156.refs_1_
  21.4 20.8 %all-to-all-done.refs_0_ = bf16[64,16,128]{2,1,0:T(8,128)(2,1)S(1)} async-done(((bf16[64,16,128]{2,1,0:T(8,128)(2,1)}), bf16[64,16,128]{2,1,0:T(8,128)(2,1)S(1)}, u32[]{:S(2)}, u32[]{:S(2)}) %all-to-all-start) | async-done | bytes 262176 | tf_op jit(solution)/shard_map/all_to_all | solution.py:207
  42.2 0.0 copy-done.10
  42.2 2.4 %shard_map.157 = (bf16[64,16,128]{2,1,0:T(8,128)(2,1)}, bf16[512,128]{1,0:T(8,128)(2,1)S(1)}) custom-call(bf16[64,16,128]{2,1,0:T(8,128)(2,1)S(1)} %all-to-all-done.refs_0_, f32[512,256]{1,0:T(8,128)S(1)} %shard_map.156.refs_1_, bf16[128,128]{1,0:T(8,128)(2,1)S(1)} %copy-done.10, bf16[128,256]{1,0:T(8,128)(2,1)S(1)} %copy-done.8, f32[64,128]{1,0:T(8,128)S(1)} %copy-done.7, ...), custom_call_target="tpu_custom_call" | custom-call | tf_op jit(solution)/shard_map/pallas_call | solution.py:216
  44.6 4.7 %all-to-all-start.1 = ((bf16[64,16,128]{2,1,0:T(8,128)(2,1)}), bf16[64,16,128]{2,1,0:T(8,128)(2,1)S(1)}, u32[]{:S(2)}, u32[]{:S(2)}) async-start(bf16[64,16,128]{2,1,0:T(8,128)(2,1)} %get-tuple-element.12), calls=%async_computation.1 | async-start | bytes 524288 | tf_op jit(solution)/shard_map/all_to_all | solution.py:232
  49.2 0.0 copy-start.2
  49.2 0.0 copy-start.3
  49.3 0.0 copy-start.4
  49.3 0.0 copy-start.5
  49.3 4.8 %collective-permute-start.2 = (bf16[512,128]{1,0:T(8,128)(2,1)S(1)}, bf16[512,128]{1,0:T(8,128)(2,1)S(1)}, u32[]{:S(2)}, u32[]{:S(2)}) collective-permute-start(bf16[512,128]{1,0:T(8,128)(2,1)S(1)} %get-tuple-element.13), channel_id=1, source_target_pairs={{0,384},{64,448},{128,256},{192,320},{256,128},{320,192},{384,0},{... | collective-permute-start | bytes 393224 | tf_op jit(solution)/shard_map/ppermute | solution.py:235
  54.1 2.1 %collective-permute-start.1 = (bf16[512,128]{1,0:T(8,128)(2,1)S(1)}, bf16[512,128]{1,0:T(8,128)(2,1)S(1)}, u32[]{:S(2)}, u32[]{:S(2)}) collective-permute-start(bf16[512,128]{1,0:T(8,128)(2,1)S(1)} %get-tuple-element.13), channel_id=1, source_target_pairs={{0,128},{64,192},{128,0},{192,64},{256,384},{320,448},{384,256},{4... | collective-permute-start | bytes 393224 | tf_op jit(solution)/shard_map/ppermute | solution.py:235
  56.2 3.6 %collective-permute-start = (bf16[512,128]{1,0:T(8,128)(2,1)S(1)}, bf16[512,128]{1,0:T(8,128)(2,1)S(1)}, u32[]{:S(2)}, u32[]{:S(2)}) collective-permute-start(bf16[512,128]{1,0:T(8,128)(2,1)S(1)} %get-tuple-element.13), channel_id=1, source_target_pairs={{0,256},{64,320},{128,384},{192,448},{256,0},{320,64},{384,128},{4... | collective-permute-start | bytes 393224 | tf_op jit(solution)/shard_map/ppermute | solution.py:235
  59.9 0.0 collective-permute-done.2
  59.9 2.3 %collective-permute-done.1 = bf16[512,128]{1,0:T(8,128)(2,1)S(1)} collective-permute-done((bf16[512,128]{1,0:T(8,128)(2,1)S(1)}, bf16[512,128]{1,0:T(8,128)(2,1)S(1)}, u32[]{:S(2)}, u32[]{:S(2)}) %collective-permute-start.1) | collective-permute-done | bytes 131104 | tf_op jit(solution)/shard_map/ppermute | solution.py:235
  62.2 2.5 %collective-permute-done = bf16[512,128]{1,0:T(8,128)(2,1)S(1)} collective-permute-done((bf16[512,128]{1,0:T(8,128)(2,1)S(1)}, bf16[512,128]{1,0:T(8,128)(2,1)S(1)}, u32[]{:S(2)}, u32[]{:S(2)}) %collective-permute-start) | collective-permute-done | bytes 131104 | tf_op jit(solution)/shard_map/ppermute | solution.py:235
  64.7 0.1 add_convert_fusion.mine_ref
  64.8 3.1 %collective-permute-start.3 = (bf16[512,128]{1,0:T(8,128)(2,1)S(1)}, bf16[512,128]{1,0:T(8,128)(2,1)S(1)}, u32[]{:S(2)}, u32[]{:S(2)}) collective-permute-start(bf16[512,128]{1,0:T(8,128)(2,1)S(1)} %add_convert_fusion.mine_ref), channel_id=1, source_target_pairs={{0,64},{64,0},{128,192},{192,128},{256,320},{320,256},{384,448},{4... | collective-permute-start | bytes 393224 | tf_op jit(solution)/shard_map/ppermute | solution.py:235
  67.9 5.2 %collective-permute-done.3.other_ref = bf16[512,128]{1,0:T(8,128)(2,1)S(1)} collective-permute-done((bf16[512,128]{1,0:T(8,128)(2,1)S(1)}, bf16[512,128]{1,0:T(8,128)(2,1)S(1)}, u32[]{:S(2)}, u32[]{:S(2)}) %collective-permute-start.3) | collective-permute-done | bytes 131104 | tf_op jit(solution)/shard_map/ppermute | solution.py:235
  73.1 0.0 all-to-all-done.1.y_ref
  73.2 1.0 %shard_map.158 = (bf16[1,128,512]{2,1,0:T(8,128)(2,1)}, bf16[1,128,512]{2,1,0:T(8,128)(2,1)}, bf16[1,128,512]{2,1,0:T(8,128)(2,1)}, bf16[1,128,512]{2,1,0:T(8,128)(2,1)}, f32[512,128]{1,0:T(8,128)}) custom-call(bf16[64,16,128]{2,1,0:T(8,128)(2,1)S(1)} %all-to-all-done.1.y_ref, bf16[512,128]{1,0:T(8,128)(2,1)S(1)} %add_convert_fusion.mine_ref, ...), custom_call_target="tpu_custom_call" | custom-call | tf_op jit(solution)/shard_map/pallas_call | solution.py:244
  (10 shorter events, 0.0 us)
Async XLA Ops:
  2.6 17.3 %copy-start.11 = (f32[8192,8]{0,1:T(8,128)S(1)}, f32[8192,8]{0,1:T(8,128)}, u32[]{:S(2)}) copy-start(f32[8192,8]{0,1:T(8,128)} %param.15) | copy-start | bytes 786436
  2.6 39.6 %all-to-all-start = ((bf16[64,16,128]{2,1,0:T(8,128)(2,1)}), bf16[64,16,128]{2,1,0:T(8,128)(2,1)S(1)}, u32[]{:S(2)}, u32[]{:S(2)}) async-start(bf16[64,16,128]{2,1,0:T(8,128)(2,1)} %shard_map.155), calls=%async_computation | async-start | bytes 524288 | tf_op jit(solution)/shard_map/all_to_all | solution.py:207
  19.9 0.9 %copy-start = (bf16[256,256]{1,0:T(8,128)(2,1)S(1)}, bf16[256,256]{1,0:T(8,128)(2,1)}, u32[]{:S(2)}) copy-start(bf16[256,256]{1,0:T(8,128)(2,1)} %constant.18.clone.refs_5_.refs_7_) | copy-start | bytes 393220
  19.9 1.0 %copy-start.1 = (bf16[256,256]{1,0:T(8,128)(2,1)S(1)}, bf16[256,256]{1,0:T(8,128)(2,1)}, u32[]{:S(2)}) copy-start(bf16[256,256]{1,0:T(8,128)(2,1)} %constant.17.clone.refs_4_.refs_6_) | copy-start | bytes 393220
  19.9 1.0 %copy-start.6 = (f32[64,128]{1,0:T(8,128)S(1)}, f32[64,128]{1,0:T(8,128)}, u32[]{:S(2)}) copy-start(f32[64,128]{1,0:T(8,128)} %constant.16.clone.refs_3_.refs_5_) | copy-start | bytes 98308
  19.9 0.9 %copy-start.7 = (f32[64,128]{1,0:T(8,128)S(1)}, f32[64,128]{1,0:T(8,128)}, u32[]{:S(2)}) copy-start(f32[64,128]{1,0:T(8,128)} %constant.15.clone.refs_2_.refs_4_) | copy-start | bytes 98308
  19.9 1.0 %copy-start.9 = (bf16[128,192]{1,0:T(8,128)(2,1)S(1)}, bf16[128,192]{1,0:T(8,128)(2,1)}, u32[]{:S(2)}) copy-start(bf16[128,192]{1,0:T(8,128)(2,1)} %constant.14.clone.refs_1_) | copy-start | bytes 147460
  20.9 21.3 %copy-start.8 = (bf16[128,256]{1,0:T(8,128)(2,1)S(1)}, bf16[128,256]{1,0:T(8,128)(2,1)}, u32[]{:S(2)}) copy-start(bf16[128,256]{1,0:T(8,128)(2,1)} %constant.20.clone.refs_3_) | copy-start | bytes 196612
  20.9 21.3 %copy-start.10 = (bf16[128,128]{1,0:T(8,128)(2,1)S(1)}, bf16[128,128]{1,0:T(8,128)(2,1)}, u32[]{:S(2)}) copy-start(bf16[128,128]{1,0:T(8,128)(2,1)} %constant.19.clone.refs_2_) | copy-start | bytes 98308
  44.6 28.6 %all-to-all-start.1 = ((bf16[64,16,128]{2,1,0:T(8,128)(2,1)}), bf16[64,16,128]{2,1,0:T(8,128)(2,1)S(1)}, u32[]{:S(2)}, u32[]{:S(2)}) async-start(bf16[64,16,128]{2,1,0:T(8,128)(2,1)} %get-tuple-element.12), calls=%async_computation.1 | async-start | bytes 524288 | tf_op jit(solution)/shard_map/all_to_all | solution.py:232
  49.2 23.9 %copy-start.2 = (bf16[1,128,512]{2,1,0:T(8,128)(2,1)S(1)}, bf16[1,128,512]{2,1,0:T(8,128)(2,1)}, u32[]{:S(2)}) copy-start(bf16[1,128,512]{2,1,0:T(8,128)(2,1)} %q_ref.1) | copy-start | bytes 393220
  49.2 23.9 %copy-start.3 = (bf16[1,128,512]{2,1,0:T(8,128)(2,1)S(1)}, bf16[1,128,512]{2,1,0:T(8,128)(2,1)}, u32[]{:S(2)}) copy-start(bf16[1,128,512]{2,1,0:T(8,128)(2,1)} %k_ref.1) | copy-start | bytes 393220
  49.3 23.9 %copy-start.4 = (bf16[1,128,512]{2,1,0:T(8,128)(2,1)S(1)}, bf16[1,128,512]{2,1,0:T(8,128)(2,1)}, u32[]{:S(2)}) copy-start(bf16[1,128,512]{2,1,0:T(8,128)(2,1)} %v_ref.1) | copy-start | bytes 393220
  49.3 23.9 %copy-start.5 = (bf16[1,128,512]{2,1,0:T(8,128)(2,1)S(1)}, bf16[1,128,512]{2,1,0:T(8,128)(2,1)}, u32[]{:S(2)}) copy-start(bf16[1,128,512]{2,1,0:T(8,128)(2,1)} %g_ref.1) | copy-start | bytes 393220
  49.3 10.6 %collective-permute-start.2 = (bf16[512,128]{1,0:T(8,128)(2,1)S(1)}, bf16[512,128]{1,0:T(8,128)(2,1)S(1)}, u32[]{:S(2)}, u32[]{:S(2)}) collective-permute-start(bf16[512,128]{1,0:T(8,128)(2,1)S(1)} %get-tuple-element.13), channel_id=1, source_target_pairs={{0,384},{64,448},{128,256},{192,320},{256,128},{320,192},{384,0},{... | collective-permute-start | bytes 393224 | tf_op jit(solution)/shard_map/ppermute | solution.py:235
  54.1 8.1 %collective-permute-start.1 = (bf16[512,128]{1,0:T(8,128)(2,1)S(1)}, bf16[512,128]{1,0:T(8,128)(2,1)S(1)}, u32[]{:S(2)}, u32[]{:S(2)}) collective-permute-start(bf16[512,128]{1,0:T(8,128)(2,1)S(1)} %get-tuple-element.13), channel_id=1, source_target_pairs={{0,128},{64,192},{128,0},{192,64},{256,384},{320,448},{384,256},{4... | collective-permute-start | bytes 393224 | tf_op jit(solution)/shard_map/ppermute | solution.py:235
  56.2 8.5 %collective-permute-start = (bf16[512,128]{1,0:T(8,128)(2,1)S(1)}, bf16[512,128]{1,0:T(8,128)(2,1)S(1)}, u32[]{:S(2)}, u32[]{:S(2)}) collective-permute-start(bf16[512,128]{1,0:T(8,128)(2,1)S(1)} %get-tuple-element.13), channel_id=1, source_target_pairs={{0,256},{64,320},{128,384},{192,448},{256,0},{320,64},{384,128},{4... | collective-permute-start | bytes 393224 | tf_op jit(solution)/shard_map/ppermute | solution.py:235
  64.8 8.4 %collective-permute-start.3 = (bf16[512,128]{1,0:T(8,128)(2,1)S(1)}, bf16[512,128]{1,0:T(8,128)(2,1)S(1)}, u32[]{:S(2)}, u32[]{:S(2)}) collective-permute-start(bf16[512,128]{1,0:T(8,128)(2,1)S(1)} %add_convert_fusion.mine_ref), channel_id=1, source_target_pairs={{0,64},{64,0},{128,192},{192,128},{256,320},{320,256},{384,448},{4... | collective-permute-start | bytes 393224 | tf_op jit(solution)/shard_map/ppermute | solution.py:235

commit v6 on v5

--- a/solution.py
+++ b/solution.py
@@ -12,6 +12,7 @@
 BF = jnp.bfloat16
 F32 = jnp.float32
 CHUNK = 256
+PLANE = 4
 
 
 def halves(table):
@@ -20,7 +21,15 @@
     return high, low
 
 
+def spread(groups):
+    planes = groups // PLANE
+    bits = planes.bit_length() - 1
+    reverse = [int(format(z, f"0{bits}b")[::-1], 2) for z in range(planes)]
+    return [z * PLANE + one for z in reverse for one in range(PLANE)]
+
+
 def make_tables(blocks, lanes):
+    order = spread(blocks)
     period = 2 * blocks
     total = period * lanes
     n = np.arange(blocks)
@@ -36,7 +45,7 @@
     b_high, b_low = halves(first.T)
     g_high, g_low = halves(second)
     return dict(
-        into=np.concatenate([a_high, a_low], axis=1),
+        into=np.concatenate([a_high, a_low], axis=1)[:, order + [blocks + n for n in order]],
         into3=np.concatenate([a_high, a_high, a_low], axis=1),
         out=np.block([[b_high, b_high], [b_low, np.zeros_like(b_low)]]),
         turn_cos=np.cos(turn).astype(np.float32),
@@ -168,7 +177,9 @@
     mixed = turn(k_ref, v_ref)
     copies[2].wait()
     copies[3].wait()
-    out_ref[...] = jnp.concatenate([mixed, turn(g_ref, q_ref)], axis=1).astype(BF)
+    both = jnp.concatenate([mixed, turn(g_ref, q_ref)], axis=1).astype(BF)
+    for place, group in enumerate(spread(groups)[::PLANE]):
+        out_ref[place * PLANE:(place + 1) * PLANE] = both[group:group + PLANE]
 
 
 def gate_kernel(y_ref, mine_ref, other_ref, q_ref, k_ref, v_ref, g_ref, go_ref, gq_ref, gk_ref, gv_ref, taps_ref):
@@ -204,7 +215,7 @@
         scratch_shapes=[pltpu.VMEM(query_proj.shape, BF)] * 4 + [pltpu.SemaphoreType.DMA((4,))],
         compiler_params=pltpu.CompilerParams(vmem_limit_bytes=60 * 1024 * 1024),
     )(query_proj, key_proj, value_proj, grad_output)
-    both = lax.all_to_all(both, "ctx", 0, 0)
+    both = lax.all_to_all(both, "ctx", 0, 0, axis_index_groups=[spread(groups)])
 
     filt_spec = pl.pallas_call(
         lambda *refs: filter_kernel(2.0 / (2 * seq_len), *refs),

time: 74.9 us -> 74 us (0.988)
  waiting for transfers between devices: 30.8 us -> 26.5 us
  starting transfers between devices: 35.6 us -> 39.1 us
    all_to_all x1, waiting for transfers between devices: 20.8 us -> 16.5 us  [on_device(): both = lax.all_to_all(both, 'ctx', 0, 0, axis_index_groups=[spread(groups)])]
    all_to_all x1, starting transfers between devices: 4.65 us -> 8.15 us  [on_device(): out = lax.all_to_all(out, 'ctx', 0, 0)]
where the time goes in v6:
time: 74 us; the launch traced here: 73.4 us
  starting transfers between devices  39.1 us (53%)
  waiting for transfers between devices  26.5 us (36%)
  Pallas kernels  5.87 us (8%)
  local copies, waits for them, and re-layouts  0.99 us (1%)
  between operations  0.83 us (1%)
    all_to_all x1, starting transfers between devices, on_device(): both = lax.all_to_all(both, 'ctx', 0, 0, axis_index_groups=[spread(groups)])  17.2 us
    all_to_all x1, waiting for transfers between devices, on_device(): both = lax.all_to_all(both, 'ctx', 0, 0, axis_index_groups=[spread(groups)])  16.5 us
    ppermute x4, starting transfers between devices, swap(): return lax.ppermute(part, 'dp', [(i, i ^ flip) for i in range(seqs)])  13.7 us
    ppermute x4, waiting for transfers between devices, swap(): return lax.ppermute(part, 'dp', [(i, i ^ flip) for i in range(seqs)])  10 us
    all_to_all x1, starting transfers between devices, on_device(): out = lax.all_to_all(out, 'ctx', 0, 0)  8.15 us
    pallas_call x1, Pallas kernels, on_device(): pl.pallas_call(lambda *refs: conv_kernel(factor * 2.0 / (2 * seq_len), *r...  2.39 us
    pallas_call x1, Pallas kernels, on_device(): pl.pallas_call(mix_kernel, out_shape=jax.ShapeDtypeStruct((groups, 2 * sh...  1.94 us
  transfers between devices with their start and end apart: 6, of which 4 were waited for; matrix products, arithmetic and copies ran while one was open for 0% of the time, Pallas kernels for 1%

profile of v6, /device:TPU:24, one launch (start us, length us, event | category | flops | bytes accessed | tf_op | source)
XLA Modules:
  0.0 73.4 jit_solution(5237366080544972068)
XLA Ops:
  0.6 1.9 %shard_map.155 = bf16[64,16,128]{2,1,0:T(8,128)(2,1)} custom-call(bf16[1,128,512]{2,1,0:T(8,128)(2,1)} %q_ref.1, bf16[1,128,512]{2,1,0:T(8,128)(2,1)} %k_ref.1, bf16[1,128,512]{2,1,0:T(8,128)(2,1)} %v_ref.1, bf16[1,128,512]{2,1,0:T(8,128)(2,1)} %g_ref.1), custom_call_target="tpu_custom_call" | custom-call | tf_op jit(solution)/shard_map/pallas_call | solution.py:211
  2.6 0.0 copy-start.11
  2.6 17.2 %all-to-all-start = ((bf16[64,16,128]{2,1,0:T(8,128)(2,1)}), bf16[64,16,128]{2,1,0:T(8,128)(2,1)S(1)}, u32[]{:S(2)}, u32[]{:S(2)}) async-start(bf16[64,16,128]{2,1,0:T(8,128)(2,1)} %shard_map.155), calls=%async_computation | async-start | bytes 524288 | tf_op jit(solution)/shard_map/all_to_all | solution.py:218
  19.9 0.0 copy-start
  19.9 0.0 copy-start.1
  19.9 0.0 copy-start.6
  19.9 0.0 copy-start.7
  19.9 0.0 copy-start.9
  19.9 0.1 copy.19
  20.0 0.8 %copy-done = bf16[256,256]{1,0:T(8,128)(2,1)S(1)} copy-done((bf16[256,256]{1,0:T(8,128)(2,1)S(1)}, bf16[256,256]{1,0:T(8,128)(2,1)}, u32[]{:S(2)}) %copy-start) | copy-done | bytes 131096
  20.8 0.1 copy-done.1
  20.8 0.0 copy-done.9
  20.9 0.5 shard_map.156.refs_1_
  21.4 16.5 %all-to-all-done.refs_0_ = bf16[64,16,128]{2,1,0:T(8,128)(2,1)S(1)} async-done(((bf16[64,16,128]{2,1,0:T(8,128)(2,1)}), bf16[64,16,128]{2,1,0:T(8,128)(2,1)S(1)}, u32[]{:S(2)}, u32[]{:S(2)}) %all-to-all-start) | async-done | bytes 262176 | tf_op jit(solution)/shard_map/all_to_all | solution.py:218
  37.9 0.0 copy-done.8
  37.9 2.4 %shard_map.157 = (bf16[64,16,128]{2,1,0:T(8,128)(2,1)}, bf16[512,128]{1,0:T(8,128)(2,1)S(1)}) custom-call(bf16[64,16,128]{2,1,0:T(8,128)(2,1)S(1)} %all-to-all-done.refs_0_, f32[512,256]{1,0:T(8,128)S(1)} %shard_map.156.refs_1_, bf16[128,128]{1,0:T(8,128)(2,1)S(1)} %copy-done.10, bf16[128,256]{1,0:T(8,128)(2,1)S(1)} %copy-done.8, f32[64,128]{1,0:T(8,128)S(1)} %copy-done.7, ...), custom_call_target="tpu_custom_call" | custom-call | tf_op jit(solution)/shard_map/pallas_call | solution.py:227
  40.3 8.1 %all-to-all-start.1 = ((bf16[64,16,128]{2,1,0:T(8,128)(2,1)}), bf16[64,16,128]{2,1,0:T(8,128)(2,1)S(1)}, u32[]{:S(2)}, u32[]{:S(2)}) async-start(bf16[64,16,128]{2,1,0:T(8,128)(2,1)} %get-tuple-element.12), calls=%async_computation.1 | async-start | bytes 524288 | tf_op jit(solution)/shard_map/all_to_all | solution.py:243
  48.4 0.0 copy-start.2
  48.4 0.0 copy-start.3
  48.4 0.0 copy-start.4
  48.5 0.0 copy-start.5
  48.5 4.8 %collective-permute-start.2 = (bf16[512,128]{1,0:T(8,128)(2,1)S(1)}, bf16[512,128]{1,0:T(8,128)(2,1)S(1)}, u32[]{:S(2)}, u32[]{:S(2)}) collective-permute-start(bf16[512,128]{1,0:T(8,128)(2,1)S(1)} %get-tuple-element.13), channel_id=1, source_target_pairs={{0,384},{64,448},{128,256},{192,320},{256,128},{320,192},{384,0},{... | collective-permute-start | bytes 393224 | tf_op jit(solution)/shard_map/ppermute | solution.py:246
  53.3 2.1 %collective-permute-start.1 = (bf16[512,128]{1,0:T(8,128)(2,1)S(1)}, bf16[512,128]{1,0:T(8,128)(2,1)S(1)}, u32[]{:S(2)}, u32[]{:S(2)}) collective-permute-start(bf16[512,128]{1,0:T(8,128)(2,1)S(1)} %get-tuple-element.13), channel_id=1, source_target_pairs={{0,128},{64,192},{128,0},{192,64},{256,384},{320,448},{384,256},{4... | collective-permute-start | bytes 393224 | tf_op jit(solution)/shard_map/ppermute | solution.py:246
  55.4 3.6 %collective-permute-start = (bf16[512,128]{1,0:T(8,128)(2,1)S(1)}, bf16[512,128]{1,0:T(8,128)(2,1)S(1)}, u32[]{:S(2)}, u32[]{:S(2)}) collective-permute-start(bf16[512,128]{1,0:T(8,128)(2,1)S(1)} %get-tuple-element.13), channel_id=1, source_target_pairs={{0,256},{64,320},{128,384},{192,448},{256,0},{320,64},{384,128},{4... | collective-permute-start | bytes 393224 | tf_op jit(solution)/shard_map/ppermute | solution.py:246
  59.1 0.0 collective-permute-done.2
  59.1 2.3 %collective-permute-done.1 = bf16[512,128]{1,0:T(8,128)(2,1)S(1)} collective-permute-done((bf16[512,128]{1,0:T(8,128)(2,1)S(1)}, bf16[512,128]{1,0:T(8,128)(2,1)S(1)}, u32[]{:S(2)}, u32[]{:S(2)}) %collective-permute-start.1) | collective-permute-done | bytes 131104 | tf_op jit(solution)/shard_map/ppermute | solution.py:246
  61.4 2.5 %collective-permute-done = bf16[512,128]{1,0:T(8,128)(2,1)S(1)} collective-permute-done((bf16[512,128]{1,0:T(8,128)(2,1)S(1)}, bf16[512,128]{1,0:T(8,128)(2,1)S(1)}, u32[]{:S(2)}, u32[]{:S(2)}) %collective-permute-start) | collective-permute-done | bytes 131104 | tf_op jit(solution)/shard_map/ppermute | solution.py:246
  63.9 0.1 add_convert_fusion.mine_ref
  64.0 3.1 %collective-permute-start.3 = (bf16[512,128]{1,0:T(8,128)(2,1)S(1)}, bf16[512,128]{1,0:T(8,128)(2,1)S(1)}, u32[]{:S(2)}, u32[]{:S(2)}) collective-permute-start(bf16[512,128]{1,0:T(8,128)(2,1)S(1)} %add_convert_fusion.mine_ref), channel_id=1, source_target_pairs={{0,64},{64,0},{128,192},{192,128},{256,320},{320,256},{384,448},{4... | collective-permute-start | bytes 393224 | tf_op jit(solution)/shard_map/ppermute | solution.py:246
  67.1 5.2 %collective-permute-done.3.other_ref = bf16[512,128]{1,0:T(8,128)(2,1)S(1)} collective-permute-done((bf16[512,128]{1,0:T(8,128)(2,1)S(1)}, bf16[512,128]{1,0:T(8,128)(2,1)S(1)}, u32[]{:S(2)}, u32[]{:S(2)}) %collective-permute-start.3) | collective-permute-done | bytes 131104 | tf_op jit(solution)/shard_map/ppermute | solution.py:246
  72.3 0.0 all-to-all-done.1.y_ref
  72.4 1.0 %shard_map.158 = (bf16[1,128,512]{2,1,0:T(8,128)(2,1)}, bf16[1,128,512]{2,1,0:T(8,128)(2,1)}, bf16[1,128,512]{2,1,0:T(8,128)(2,1)}, bf16[1,128,512]{2,1,0:T(8,128)(2,1)}, f32[512,128]{1,0:T(8,128)}) custom-call(bf16[64,16,128]{2,1,0:T(8,128)(2,1)S(1)} %all-to-all-done.1.y_ref, bf16[512,128]{1,0:T(8,128)(2,1)S(1)} %add_convert_fusion.mine_ref, ...), custom_call_target="tpu_custom_call" | custom-call | tf_op jit(solution)/shard_map/pallas_call | solution.py:255
  (10 shorter events, 0.0 us)
Async XLA Ops:
  2.6 17.3 %copy-start.11 = (f32[8192,8]{0,1:T(8,128)S(1)}, f32[8192,8]{0,1:T(8,128)}, u32[]{:S(2)}) copy-start(f32[8192,8]{0,1:T(8,128)} %param.15) | copy-start | bytes 786436
  2.6 35.3 %all-to-all-start = ((bf16[64,16,128]{2,1,0:T(8,128)(2,1)}), bf16[64,16,128]{2,1,0:T(8,128)(2,1)S(1)}, u32[]{:S(2)}, u32[]{:S(2)}) async-start(bf16[64,16,128]{2,1,0:T(8,128)(2,1)} %shard_map.155), calls=%async_computation | async-start | bytes 524288 | tf_op jit(solution)/shard_map/all_to_all | solution.py:218
  19.9 0.9 %copy-start = (bf16[256,256]{1,0:T(8,128)(2,1)S(1)}, bf16[256,256]{1,0:T(8,128)(2,1)}, u32[]{:S(2)}) copy-start(bf16[256,256]{1,0:T(8,128)(2,1)} %constant.18.clone.refs_5_.refs_7_) | copy-start | bytes 393220
  19.9 1.0 %copy-start.1 = (bf16[256,256]{1,0:T(8,128)(2,1)S(1)}, bf16[256,256]{1,0:T(8,128)(2,1)}, u32[]{:S(2)}) copy-start(bf16[256,256]{1,0:T(8,128)(2,1)} %constant.17.clone.refs_4_.refs_6_) | copy-start | bytes 393220
  19.9 1.0 %copy-start.6 = (f32[64,128]{1,0:T(8,128)S(1)}, f32[64,128]{1,0:T(8,128)}, u32[]{:S(2)}) copy-start(f32[64,128]{1,0:T(8,128)} %constant.16.clone.refs_3_.refs_5_) | copy-start | bytes 98308
  19.9 0.9 %copy-start.7 = (f32[64,128]{1,0:T(8,128)S(1)}, f32[64,128]{1,0:T(8,128)}, u32[]{:S(2)}) copy-start(f32[64,128]{1,0:T(8,128)} %constant.15.clone.refs_2_.refs_4_) | copy-start | bytes 98308
  19.9 1.0 %copy-start.9 = (bf16[128,192]{1,0:T(8,128)(2,1)S(1)}, bf16[128,192]{1,0:T(8,128)(2,1)}, u32[]{:S(2)}) copy-start(bf16[128,192]{1,0:T(8,128)(2,1)} %constant.14.clone.refs_1_) | copy-start | bytes 147460
  20.9 17.0 %copy-start.8 = (bf16[128,256]{1,0:T(8,128)(2,1)S(1)}, bf16[128,256]{1,0:T(8,128)(2,1)}, u32[]{:S(2)}) copy-start(bf16[128,256]{1,0:T(8,128)(2,1)} %constant.20.clone.refs_3_) | copy-start | bytes 196612
  20.9 17.0 %copy-start.10 = (bf16[128,128]{1,0:T(8,128)(2,1)S(1)}, bf16[128,128]{1,0:T(8,128)(2,1)}, u32[]{:S(2)}) copy-start(bf16[128,128]{1,0:T(8,128)(2,1)} %constant.19.clone.refs_2_) | copy-start | bytes 98308
  40.3 32.1 %all-to-all-start.1 = ((bf16[64,16,128]{2,1,0:T(8,128)(2,1)}), bf16[64,16,128]{2,1,0:T(8,128)(2,1)S(1)}, u32[]{:S(2)}, u32[]{:S(2)}) async-start(bf16[64,16,128]{2,1,0:T(8,128)(2,1)} %get-tuple-element.12), calls=%async_computation.1 | async-start | bytes 524288 | tf_op jit(solution)/shard_map/all_to_all | solution.py:243
  48.4 23.9 %copy-start.2 = (bf16[1,128,512]{2,1,0:T(8,128)(2,1)S(1)}, bf16[1,128,512]{2,1,0:T(8,128)(2,1)}, u32[]{:S(2)}) copy-start(bf16[1,128,512]{2,1,0:T(8,128)(2,1)} %q_ref.1) | copy-start | bytes 393220
  48.4 23.9 %copy-start.3 = (bf16[1,128,512]{2,1,0:T(8,128)(2,1)S(1)}, bf16[1,128,512]{2,1,0:T(8,128)(2,1)}, u32[]{:S(2)}) copy-start(bf16[1,128,512]{2,1,0:T(8,128)(2,1)} %k_ref.1) | copy-start | bytes 393220
  48.4 23.9 %copy-start.4 = (bf16[1,128,512]{2,1,0:T(8,128)(2,1)S(1)}, bf16[1,128,512]{2,1,0:T(8,128)(2,1)}, u32[]{:S(2)}) copy-start(bf16[1,128,512]{2,1,0:T(8,128)(2,1)} %v_ref.1) | copy-start | bytes 393220
  48.5 23.9 %copy-start.5 = (bf16[1,128,512]{2,1,0:T(8,128)(2,1)S(1)}, bf16[1,128,512]{2,1,0:T(8,128)(2,1)}, u32[]{:S(2)}) copy-start(bf16[1,128,512]{2,1,0:T(8,128)(2,1)} %g_ref.1) | copy-start | bytes 393220
  48.5 10.6 %collective-permute-start.2 = (bf16[512,128]{1,0:T(8,128)(2,1)S(1)}, bf16[512,128]{1,0:T(8,128)(2,1)S(1)}, u32[]{:S(2)}, u32[]{:S(2)}) collective-permute-start(bf16[512,128]{1,0:T(8,128)(2,1)S(1)} %get-tuple-element.13), channel_id=1, source_target_pairs={{0,384},{64,448},{128,256},{192,320},{256,128},{320,192},{384,0},{... | collective-permute-start | bytes 393224 | tf_op jit(solution)/shard_map/ppermute | solution.py:246
  53.3 8.1 %collective-permute-start.1 = (bf16[512,128]{1,0:T(8,128)(2,1)S(1)}, bf16[512,128]{1,0:T(8,128)(2,1)S(1)}, u32[]{:S(2)}, u32[]{:S(2)}) collective-permute-start(bf16[512,128]{1,0:T(8,128)(2,1)S(1)} %get-tuple-element.13), channel_id=1, source_target_pairs={{0,128},{64,192},{128,0},{192,64},{256,384},{320,448},{384,256},{4... | collective-permute-start | bytes 393224 | tf_op jit(solution)/shard_map/ppermute | solution.py:246
  55.4 8.5 %collective-permute-start = (bf16[512,128]{1,0:T(8,128)(2,1)S(1)}, bf16[512,128]{1,0:T(8,128)(2,1)S(1)}, u32[]{:S(2)}, u32[]{:S(2)}) collective-permute-start(bf16[512,128]{1,0:T(8,128)(2,1)S(1)} %get-tuple-element.13), channel_id=1, source_target_pairs={{0,256},{64,320},{128,384},{192,448},{256,0},{320,64},{384,128},{4... | collective-permute-start | bytes 393224 | tf_op jit(solution)/shard_map/ppermute | solution.py:246
  64.0 8.4 %collective-permute-start.3 = (bf16[512,128]{1,0:T(8,128)(2,1)S(1)}, bf16[512,128]{1,0:T(8,128)(2,1)S(1)}, u32[]{:S(2)}, u32[]{:S(2)}) collective-permute-start(bf16[512,128]{1,0:T(8,128)(2,1)S(1)} %add_convert_fusion.mine_ref), channel_id=1, source_target_pairs={{0,64},{64,0},{128,192},{192,128},{256,320},{320,256},{384,448},{4... | collective-permute-start | bytes 393224 | tf_op jit(solution)/shard_map/ppermute | solution.py:246

commit v7 on v6

--- a/solution.py
+++ b/solution.py
@@ -242,16 +242,19 @@
     )(both, filt_spec, t["into"], t["out"], t["turn_cos"], t["turn_sin"], t["g_high"], t["g_low"])
     out = lax.all_to_all(out, "ctx", 0, 0)
 
-    def swap(part, flip):
-        return lax.ppermute(part, "dp", [(i, i ^ flip) for i in range(seqs)])
+    def swap(part, flips):
+        pairs = [
+            (d * groups + c, (d ^ flips[c % 2]) * groups + c) for d in range(seqs) for c in range(groups)
+        ]
+        return lax.ppermute(part, ("dp", "ctx"), pairs)
 
     def add(a, b):
         return (a.astype(F32) + b.astype(F32)).astype(BF)
 
-    a, b, c = swap(taps, 2), swap(taps, 6), swap(taps, 4)
-    taps = (taps.astype(F32) + c.astype(F32)) + (a.astype(F32) + b.astype(F32))
-    taps = taps.astype(BF)
-    other = swap(taps, 1)
+    taps = add(taps, swap(taps, (2, 6)))
+    taps = add(taps, swap(taps, (6, 1)))
+    other = swap(taps, (1, 2))
+
     *grads, grad_filter = pl.pallas_call(
         gate_kernel,
         out_shape=[jax.ShapeDtypeStruct(query_proj.shape, BF)] * 4 + [jax.ShapeDtypeStruct(taps.shape, F32)],

time: 74 us -> 73.4 us (level)
  starting transfers between devices: 39.1 us -> 36.7 us
  waiting for transfers between devices: 26.5 us -> 28.5 us
    ppermute x4 -> x3, starting transfers between devices: 13.7 us -> 11.3 us  [swap(): return lax.ppermute(part, ('dp', 'ctx'), pairs)]
    ppermute x4 -> x3, waiting for transfers between devices: 10 us -> 12.1 us  [swap(): return lax.ppermute(part, ('dp', 'ctx'), pairs)]
  transfers between devices with their start and end apart: 6 -> 5, of which waited for: 4 -> 4; matrix products, arithmetic and copies ran while one was open for 0% -> 0% of each run, Pallas kernels for 1% -> 1%
where the time goes in v7:
time: 73.4 us; the launch traced here: 73 us
  starting transfers between devices  36.7 us (50%)
  waiting for transfers between devices  28.5 us (39%)
  Pallas kernels  5.87 us (8%)
  local copies, waits for them, and re-layouts  0.99 us (1%)
  between operations  0.81 us (1%)
    all_to_all x1, starting transfers between devices, on_device(): both = lax.all_to_all(both, 'ctx', 0, 0, axis_index_groups=[spread(groups)])  17.2 us
    all_to_all x1, waiting for transfers between devices, on_device(): both = lax.all_to_all(both, 'ctx', 0, 0, axis_index_groups=[spread(groups)])  16.5 us
    ppermute x3, waiting for transfers between devices, swap(): return lax.ppermute(part, ('dp', 'ctx'), pairs)  12.1 us
    ppermute x3, starting transfers between devices, swap(): return lax.ppermute(part, ('dp', 'ctx'), pairs)  11.3 us
    all_to_all x1, starting transfers between devices, on_device(): out = lax.all_to_all(out, 'ctx', 0, 0)  8.15 us
    pallas_call x1, Pallas kernels, on_device(): pl.pallas_call(lambda *refs: conv_kernel(factor * 2.0 / (2 * seq_len), *r...  2.39 us
    pallas_call x1, Pallas kernels, on_device(): pl.pallas_call(mix_kernel, out_shape=jax.ShapeDtypeStruct((groups, 2 * sh...  1.94 us
  transfers between devices with their start and end apart: 5, of which 4 were waited for; matrix products, arithmetic and copies ran while one was open for 0% of the time, Pallas kernels for 1%

profile of v7, /device:TPU:24, one launch (start us, length us, event | category | flops | bytes accessed | tf_op | source)
XLA Modules:
  0.0 73.0 jit_solution(1135723685247187021)
XLA Ops:
  0.6 1.9 %shard_map.155 = bf16[64,16,128]{2,1,0:T(8,128)(2,1)} custom-call(bf16[1,128,512]{2,1,0:T(8,128)(2,1)} %q_ref.1, bf16[1,128,512]{2,1,0:T(8,128)(2,1)} %k_ref.1, bf16[1,128,512]{2,1,0:T(8,128)(2,1)} %v_ref.1, bf16[1,128,512]{2,1,0:T(8,128)(2,1)} %g_ref.1), custom_call_target="tpu_custom_call" | custom-call | tf_op jit(solution)/shard_map/pallas_call | solution.py:211
  2.6 0.0 copy-start.11
  2.6 17.2 %all-to-all-start = ((bf16[64,16,128]{2,1,0:T(8,128)(2,1)}), bf16[64,16,128]{2,1,0:T(8,128)(2,1)S(1)}, u32[]{:S(2)}, u32[]{:S(2)}) async-start(bf16[64,16,128]{2,1,0:T(8,128)(2,1)} %shard_map.155), calls=%async_computation | async-start | bytes 524288 | tf_op jit(solution)/shard_map/all_to_all | solution.py:218
  19.8 0.0 copy-done.11
  19.9 0.0 copy-start
  19.9 0.0 copy-start.1
  19.9 0.0 copy-start.6
  19.9 0.0 copy-start.7
  19.9 0.0 copy-start.9
  19.9 0.1 copy.19
  20.0 0.8 %copy-done = bf16[256,256]{1,0:T(8,128)(2,1)S(1)} copy-done((bf16[256,256]{1,0:T(8,128)(2,1)S(1)}, bf16[256,256]{1,0:T(8,128)(2,1)}, u32[]{:S(2)}) %copy-start) | copy-done | bytes 131096
  20.8 0.1 copy-done.1
  20.8 0.0 copy-done.6
  20.8 0.0 copy-done.7
  20.8 0.0 copy-done.9
  20.9 0.5 shard_map.156.refs_1_
  21.4 16.5 %all-to-all-done.refs_0_ = bf16[64,16,128]{2,1,0:T(8,128)(2,1)S(1)} async-done(((bf16[64,16,128]{2,1,0:T(8,128)(2,1)}), bf16[64,16,128]{2,1,0:T(8,128)(2,1)S(1)}, u32[]{:S(2)}, u32[]{:S(2)}) %all-to-all-start) | async-done | bytes 262176 | tf_op jit(solution)/shard_map/all_to_all | solution.py:218
  37.9 0.0 copy-done.10
  37.9 2.4 %shard_map.157 = (bf16[64,16,128]{2,1,0:T(8,128)(2,1)}, bf16[512,128]{1,0:T(8,128)(2,1)S(1)}) custom-call(bf16[64,16,128]{2,1,0:T(8,128)(2,1)S(1)} %all-to-all-done.refs_0_, f32[512,256]{1,0:T(8,128)S(1)} %shard_map.156.refs_1_, bf16[128,128]{1,0:T(8,128)(2,1)S(1)} %copy-done.10, bf16[128,256]{1,0:T(8,128)(2,1)S(1)} %copy-done.8, f32[64,128]{1,0:T(8,128)S(1)} %copy-done.7, ...), custom_call_target="tpu_custom_call" | custom-call | tf_op jit(solution)/shard_map/pallas_call | solution.py:227
  40.3 8.1 %all-to-all-start.1 = ((bf16[64,16,128]{2,1,0:T(8,128)(2,1)}), bf16[64,16,128]{2,1,0:T(8,128)(2,1)S(1)}, u32[]{:S(2)}, u32[]{:S(2)}) async-start(bf16[64,16,128]{2,1,0:T(8,128)(2,1)} %get-tuple-element.12), calls=%async_computation.1 | async-start | bytes 524288 | tf_op jit(solution)/shard_map/all_to_all | solution.py:243
  48.4 3.4 %collective-permute-start = (bf16[512,128]{1,0:T(8,128)(2,1)S(1)}, bf16[512,128]{1,0:T(8,128)(2,1)S(1)}, u32[]{:S(2)}, u32[]{:S(2)}) collective-permute-start(bf16[512,128]{1,0:T(8,128)(2,1)S(1)} %get-tuple-element.13), channel_id=1, source_target_pairs={{0,128},{1,385},{2,130},{3,387},{4,132},{5,389},{6,134},{7,391},{8... | collective-permute-start | bytes 393224 | tf_op jit(solution)/shard_map/ppermute | solution.py:249
  51.8 3.5 %collective-permute-done = bf16[512,128]{1,0:T(8,128)(2,1)S(1)} collective-permute-done((bf16[512,128]{1,0:T(8,128)(2,1)S(1)}, bf16[512,128]{1,0:T(8,128)(2,1)S(1)}, u32[]{:S(2)}, u32[]{:S(2)}) %collective-permute-start) | collective-permute-done | bytes 131104 | tf_op jit(solution)/shard_map/ppermute | solution.py:249
  55.3 0.0 copy-start.2
  55.3 0.0 copy-start.3
  55.4 0.0 copy-start.4
  55.4 4.8 %collective-permute-start.1 = (bf16[512,128]{1,0:T(8,128)(2,1)S(1)}, bf16[512,128]{1,0:T(8,128)(2,1)S(1)}, u32[]{:S(2)}, u32[]{:S(2)}) collective-permute-start(bf16[512,128]{1,0:T(8,128)(2,1)S(1)} %add_convert_fusion.1), channel_id=1, source_target_pairs={{0,384},{1,65},{2,386},{3,67},{4,388},{5,69},{6,390},{7,71},{8,392... | collective-permute-start | bytes 393224 | tf_op jit(solution)/shard_map/ppermute | solution.py:249
  60.2 3.4 %collective-permute-done.1 = bf16[512,128]{1,0:T(8,128)(2,1)S(1)} collective-permute-done((bf16[512,128]{1,0:T(8,128)(2,1)S(1)}, bf16[512,128]{1,0:T(8,128)(2,1)S(1)}, u32[]{:S(2)}, u32[]{:S(2)}) %collective-permute-start.1) | collective-permute-done | bytes 131104 | tf_op jit(solution)/shard_map/ppermute | solution.py:249
  63.6 3.1 %collective-permute-start.2 = (bf16[512,128]{1,0:T(8,128)(2,1)S(1)}, bf16[512,128]{1,0:T(8,128)(2,1)S(1)}, u32[]{:S(2)}, u32[]{:S(2)}) collective-permute-start(bf16[512,128]{1,0:T(8,128)(2,1)S(1)} %add_convert_fusion.mine_ref), channel_id=1, source_target_pairs={{0,64},{1,129},{2,66},{3,131},{4,68},{5,133},{6,70},{7,135},{8,72}... | collective-permute-start | bytes 393224 | tf_op jit(solution)/shard_map/ppermute | solution.py:249
  66.8 5.2 %collective-permute-done.2.other_ref = bf16[512,128]{1,0:T(8,128)(2,1)S(1)} collective-permute-done((bf16[512,128]{1,0:T(8,128)(2,1)S(1)}, bf16[512,128]{1,0:T(8,128)(2,1)S(1)}, u32[]{:S(2)}, u32[]{:S(2)}) %collective-permute-start.2) | collective-permute-done | bytes 131104 | tf_op jit(solution)/shard_map/ppermute | solution.py:249
  72.0 0.0 all-to-all-done.1.y_ref
  72.0 0.0 copy-done.2
  72.0 1.0 %shard_map.158 = (bf16[1,128,512]{2,1,0:T(8,128)(2,1)}, bf16[1,128,512]{2,1,0:T(8,128)(2,1)}, bf16[1,128,512]{2,1,0:T(8,128)(2,1)}, bf16[1,128,512]{2,1,0:T(8,128)(2,1)}, f32[512,128]{1,0:T(8,128)}) custom-call(bf16[64,16,128]{2,1,0:T(8,128)(2,1)S(1)} %all-to-all-done.1.y_ref, bf16[512,128]{1,0:T(8,128)(2,1)S(1)} %add_convert_fusion.mine_ref, ...), custom_call_target="tpu_custom_call" | custom-call | tf_op jit(solution)/shard_map/pallas_call | solution.py:258
  (9 shorter events, 0.1 us)
Async XLA Ops:
  2.6 17.3 %copy-start.11 = (f32[8192,8]{0,1:T(8,128)S(1)}, f32[8192,8]{0,1:T(8,128)}, u32[]{:S(2)}) copy-start(f32[8192,8]{0,1:T(8,128)} %param.15) | copy-start | bytes 786436
  2.6 35.3 %all-to-all-start = ((bf16[64,16,128]{2,1,0:T(8,128)(2,1)}), bf16[64,16,128]{2,1,0:T(8,128)(2,1)S(1)}, u32[]{:S(2)}, u32[]{:S(2)}) async-start(bf16[64,16,128]{2,1,0:T(8,128)(2,1)} %shard_map.155), calls=%async_computation | async-start | bytes 524288 | tf_op jit(solution)/shard_map/all_to_all | solution.py:218
  19.9 0.9 %copy-start = (bf16[256,256]{1,0:T(8,128)(2,1)S(1)}, bf16[256,256]{1,0:T(8,128)(2,1)}, u32[]{:S(2)}) copy-start(bf16[256,256]{1,0:T(8,128)(2,1)} %constant.18.clone.refs_5_.refs_7_) | copy-start | bytes 393220
  19.9 1.0 %copy-start.1 = (bf16[256,256]{1,0:T(8,128)(2,1)S(1)}, bf16[256,256]{1,0:T(8,128)(2,1)}, u32[]{:S(2)}) copy-start(bf16[256,256]{1,0:T(8,128)(2,1)} %constant.17.clone.refs_4_.refs_6_) | copy-start | bytes 393220
  19.9 1.0 %copy-start.6 = (f32[64,128]{1,0:T(8,128)S(1)}, f32[64,128]{1,0:T(8,128)}, u32[]{:S(2)}) copy-start(f32[64,128]{1,0:T(8,128)} %constant.16.clone.refs_3_.refs_5_) | copy-start | bytes 98308
  19.9 0.9 %copy-start.7 = (f32[64,128]{1,0:T(8,128)S(1)}, f32[64,128]{1,0:T(8,128)}, u32[]{:S(2)}) copy-start(f32[64,128]{1,0:T(8,128)} %constant.15.clone.refs_2_.refs_4_) | copy-start | bytes 98308
  19.9 1.0 %copy-start.9 = (bf16[128,192]{1,0:T(8,128)(2,1)S(1)}, bf16[128,192]{1,0:T(8,128)(2,1)}, u32[]{:S(2)}) copy-start(bf16[128,192]{1,0:T(8,128)(2,1)} %constant.14.clone.refs_1_) | copy-start | bytes 147460
  20.9 17.0 %copy-start.8 = (bf16[128,256]{1,0:T(8,128)(2,1)S(1)}, bf16[128,256]{1,0:T(8,128)(2,1)}, u32[]{:S(2)}) copy-start(bf16[128,256]{1,0:T(8,128)(2,1)} %constant.20.clone.refs_3_) | copy-start | bytes 196612
  20.9 17.0 %copy-start.10 = (bf16[128,128]{1,0:T(8,128)(2,1)S(1)}, bf16[128,128]{1,0:T(8,128)(2,1)}, u32[]{:S(2)}) copy-start(bf16[128,128]{1,0:T(8,128)(2,1)} %constant.19.clone.refs_2_) | copy-start | bytes 98308
  40.3 31.7 %all-to-all-start.1 = ((bf16[64,16,128]{2,1,0:T(8,128)(2,1)}), bf16[64,16,128]{2,1,0:T(8,128)(2,1)S(1)}, u32[]{:S(2)}, u32[]{:S(2)}) async-start(bf16[64,16,128]{2,1,0:T(8,128)(2,1)} %get-tuple-element.12), calls=%async_computation.1 | async-start | bytes 524288 | tf_op jit(solution)/shard_map/all_to_all | solution.py:243
  48.4 6.9 %collective-permute-start = (bf16[512,128]{1,0:T(8,128)(2,1)S(1)}, bf16[512,128]{1,0:T(8,128)(2,1)S(1)}, u32[]{:S(2)}, u32[]{:S(2)}) collective-permute-start(bf16[512,128]{1,0:T(8,128)(2,1)S(1)} %get-tuple-element.13), channel_id=1, source_target_pairs={{0,128},{1,385},{2,130},{3,387},{4,132},{5,389},{6,134},{7,391},{8... | collective-permute-start | bytes 393224 | tf_op jit(solution)/shard_map/ppermute | solution.py:249
  55.3 16.7 %copy-start.5 = (bf16[1,128,512]{2,1,0:T(8,128)(2,1)S(1)}, bf16[1,128,512]{2,1,0:T(8,128)(2,1)}, u32[]{:S(2)}) copy-start(bf16[1,128,512]{2,1,0:T(8,128)(2,1)} %g_ref.1) | copy-start | bytes 393220
  55.3 16.7 %copy-start.2 = (bf16[1,128,512]{2,1,0:T(8,128)(2,1)S(1)}, bf16[1,128,512]{2,1,0:T(8,128)(2,1)}, u32[]{:S(2)}) copy-start(bf16[1,128,512]{2,1,0:T(8,128)(2,1)} %q_ref.1) | copy-start | bytes 393220
  55.3 16.7 %copy-start.3 = (bf16[1,128,512]{2,1,0:T(8,128)(2,1)S(1)}, bf16[1,128,512]{2,1,0:T(8,128)(2,1)}, u32[]{:S(2)}) copy-start(bf16[1,128,512]{2,1,0:T(8,128)(2,1)} %k_ref.1) | copy-start | bytes 393220
  55.4 16.7 %copy-start.4 = (bf16[1,128,512]{2,1,0:T(8,128)(2,1)S(1)}, bf16[1,128,512]{2,1,0:T(8,128)(2,1)}, u32[]{:S(2)}) copy-start(bf16[1,128,512]{2,1,0:T(8,128)(2,1)} %v_ref.1) | copy-start | bytes 393220
  55.4 8.2 %collective-permute-start.1 = (bf16[512,128]{1,0:T(8,128)(2,1)S(1)}, bf16[512,128]{1,0:T(8,128)(2,1)S(1)}, u32[]{:S(2)}, u32[]{:S(2)}) collective-permute-start(bf16[512,128]{1,0:T(8,128)(2,1)S(1)} %add_convert_fusion.1), channel_id=1, source_target_pairs={{0,384},{1,65},{2,386},{3,67},{4,388},{5,69},{6,390},{7,71},{8,392... | collective-permute-start | bytes 393224 | tf_op jit(solution)/shard_map/ppermute | solution.py:249
  63.6 8.4 %collective-permute-start.2 = (bf16[512,128]{1,0:T(8,128)(2,1)S(1)}, bf16[512,128]{1,0:T(8,128)(2,1)S(1)}, u32[]{:S(2)}, u32[]{:S(2)}) collective-permute-start(bf16[512,128]{1,0:T(8,128)(2,1)S(1)} %add_convert_fusion.mine_ref), channel_id=1, source_target_pairs={{0,64},{1,129},{2,66},{3,131},{4,68},{5,133},{6,70},{7,135},{8,72}... | collective-permute-start | bytes 393224 | tf_op jit(solution)/shard_map/ppermute | solution.py:249

commit v8 on v7

--- a/solution.py
+++ b/solution.py
@@ -24,7 +24,7 @@
 def spread(groups):
     planes = groups // PLANE
     bits = planes.bit_length() - 1
-    reverse = [int(format(z, f"0{bits}b")[::-1], 2) for z in range(planes)]
+    reverse = [(int(format(z, f"0{bits}b")[::-1], 2) + planes - 2) % planes for z in range(planes)]
     return [z * PLANE + one for z in reverse for one in range(PLANE)]
 
 

time: 73.4 us -> 73.4 us (level)
  starting transfers between devices: 36.7 us -> 35.9 us
  waiting for transfers between devices: 28.5 us -> 29.3 us
    all_to_all x1, starting transfers between devices: 8.15 us -> 7.3 us  [on_device(): out = lax.all_to_all(out, 'ctx', 0, 0)]
    all_to_all x1, waiting for transfers between devices: 16.5 us -> 17.3 us  [on_device(): both = lax.all_to_all(both, 'ctx', 0, 0, axis_index_groups=[spread(groups)])]
where the time goes in v8:
time: 73.4 us; the launch traced here: 73 us
  starting transfers between devices  35.9 us (49%)
  waiting for transfers between devices  29.3 us (40%)
  Pallas kernels  5.87 us (8%)
  local copies, waits for them, and re-layouts  0.99 us (1%)
  between operations  0.81 us (1%)
    all_to_all x1, waiting for transfers between devices, on_device(): both = lax.all_to_all(both, 'ctx', 0, 0, axis_index_groups=[spread(groups)])  17.3 us
    all_to_all x1, starting transfers between devices, on_device(): both = lax.all_to_all(both, 'ctx', 0, 0, axis_index_groups=[spread(groups)])  17.3 us
    ppermute x3, waiting for transfers between devices, swap(): return lax.ppermute(part, ('dp', 'ctx'), pairs)  12.1 us
    ppermute x3, starting transfers between devices, swap(): return lax.ppermute(part, ('dp', 'ctx'), pairs)  11.3 us
    all_to_all x1, starting transfers between devices, on_device(): out = lax.all_to_all(out, 'ctx', 0, 0)  7.3 us
    pallas_call x1, Pallas kernels, on_device(): pl.pallas_call(lambda *refs: conv_kernel(factor * 2.0 / (2 * seq_len), *r...  2.39 us
    pallas_call x1, Pallas kernels, on_device(): pl.pallas_call(mix_kernel, out_shape=jax.ShapeDtypeStruct((groups, 2 * sh...  1.94 us
  transfers between devices with their start and end apart: 5, of which 4 were waited for; matrix products, arithmetic and copies ran while one was open for 0% of the time, Pallas kernels for 1%

profile of v8, /device:TPU:24, one launch (start us, length us, event | category | flops | bytes accessed | tf_op | source)
XLA Modules:
  0.0 73.0 jit_solution(11812210510934690499)
XLA Ops:
  0.6 1.9 %shard_map.155 = bf16[64,16,128]{2,1,0:T(8,128)(2,1)} custom-call(bf16[1,128,512]{2,1,0:T(8,128)(2,1)} %q_ref.1, bf16[1,128,512]{2,1,0:T(8,128)(2,1)} %k_ref.1, bf16[1,128,512]{2,1,0:T(8,128)(2,1)} %v_ref.1, bf16[1,128,512]{2,1,0:T(8,128)(2,1)} %g_ref.1), custom_call_target="tpu_custom_call" | custom-call | tf_op jit(solution)/shard_map/pallas_call | solution.py:211
  2.6 0.0 copy-start.11
  2.6 17.3 %all-to-all-start = ((bf16[64,16,128]{2,1,0:T(8,128)(2,1)}), bf16[64,16,128]{2,1,0:T(8,128)(2,1)S(1)}, u32[]{:S(2)}, u32[]{:S(2)}) async-start(bf16[64,16,128]{2,1,0:T(8,128)(2,1)} %shard_map.155), calls=%async_computation | async-start | bytes 524288 | tf_op jit(solution)/shard_map/all_to_all | solution.py:218
  19.9 0.0 copy-done.11
  19.9 0.0 copy-start
  19.9 0.0 copy-start.1
  19.9 0.0 copy-start.6
  19.9 0.0 copy-start.7
  19.9 0.0 copy-start.9
  19.9 0.1 copy.19
  20.0 0.8 %copy-done = bf16[256,256]{1,0:T(8,128)(2,1)S(1)} copy-done((bf16[256,256]{1,0:T(8,128)(2,1)S(1)}, bf16[256,256]{1,0:T(8,128)(2,1)}, u32[]{:S(2)}) %copy-start) | copy-done | bytes 131096
  20.8 0.1 copy-done.1
  20.8 0.0 copy-done.6
  20.8 0.0 copy-done.7
  20.8 0.0 copy-done.9
  20.9 0.5 shard_map.156.refs_1_
  21.4 17.3 %all-to-all-done.refs_0_ = bf16[64,16,128]{2,1,0:T(8,128)(2,1)S(1)} async-done(((bf16[64,16,128]{2,1,0:T(8,128)(2,1)}), bf16[64,16,128]{2,1,0:T(8,128)(2,1)S(1)}, u32[]{:S(2)}, u32[]{:S(2)}) %all-to-all-start) | async-done | bytes 262176 | tf_op jit(solution)/shard_map/all_to_all | solution.py:218
  38.7 0.0 copy-done.10
  38.7 2.4 %shard_map.157 = (bf16[64,16,128]{2,1,0:T(8,128)(2,1)}, bf16[512,128]{1,0:T(8,128)(2,1)S(1)}) custom-call(bf16[64,16,128]{2,1,0:T(8,128)(2,1)S(1)} %all-to-all-done.refs_0_, f32[512,256]{1,0:T(8,128)S(1)} %shard_map.156.refs_1_, bf16[128,128]{1,0:T(8,128)(2,1)S(1)} %copy-done.10, bf16[128,256]{1,0:T(8,128)(2,1)S(1)} %copy-done.8, f32[64,128]{1,0:T(8,128)S(1)} %copy-done.7, ...), custom_call_target="tpu_custom_call" | custom-call | tf_op jit(solution)/shard_map/pallas_call | solution.py:227
  41.1 7.3 %all-to-all-start.1 = ((bf16[64,16,128]{2,1,0:T(8,128)(2,1)}), bf16[64,16,128]{2,1,0:T(8,128)(2,1)S(1)}, u32[]{:S(2)}, u32[]{:S(2)}) async-start(bf16[64,16,128]{2,1,0:T(8,128)(2,1)} %get-tuple-element.12), calls=%async_computation.1 | async-start | bytes 524288 | tf_op jit(solution)/shard_map/all_to_all | solution.py:243
  48.4 3.4 %collective-permute-start = (bf16[512,128]{1,0:T(8,128)(2,1)S(1)}, bf16[512,128]{1,0:T(8,128)(2,1)S(1)}, u32[]{:S(2)}, u32[]{:S(2)}) collective-permute-start(bf16[512,128]{1,0:T(8,128)(2,1)S(1)} %get-tuple-element.13), channel_id=1, source_target_pairs={{0,128},{1,385},{2,130},{3,387},{4,132},{5,389},{6,134},{7,391},{8... | collective-permute-start | bytes 393224 | tf_op jit(solution)/shard_map/ppermute | solution.py:249
  51.8 3.5 %collective-permute-done = bf16[512,128]{1,0:T(8,128)(2,1)S(1)} collective-permute-done((bf16[512,128]{1,0:T(8,128)(2,1)S(1)}, bf16[512,128]{1,0:T(8,128)(2,1)S(1)}, u32[]{:S(2)}, u32[]{:S(2)}) %collective-permute-start) | collective-permute-done | bytes 131104 | tf_op jit(solution)/shard_map/ppermute | solution.py:249
  55.3 0.0 copy-start.2
  55.3 0.0 copy-start.3
  55.3 0.0 copy-start.4
  55.3 4.8 %collective-permute-start.1 = (bf16[512,128]{1,0:T(8,128)(2,1)S(1)}, bf16[512,128]{1,0:T(8,128)(2,1)S(1)}, u32[]{:S(2)}, u32[]{:S(2)}) collective-permute-start(bf16[512,128]{1,0:T(8,128)(2,1)S(1)} %add_convert_fusion.1), channel_id=1, source_target_pairs={{0,384},{1,65},{2,386},{3,67},{4,388},{5,69},{6,390},{7,71},{8,392... | collective-permute-start | bytes 393224 | tf_op jit(solution)/shard_map/ppermute | solution.py:249
  60.1 3.4 %collective-permute-done.1 = bf16[512,128]{1,0:T(8,128)(2,1)S(1)} collective-permute-done((bf16[512,128]{1,0:T(8,128)(2,1)S(1)}, bf16[512,128]{1,0:T(8,128)(2,1)S(1)}, u32[]{:S(2)}, u32[]{:S(2)}) %collective-permute-start.1) | collective-permute-done | bytes 131104 | tf_op jit(solution)/shard_map/ppermute | solution.py:249
  63.6 3.1 %collective-permute-start.2 = (bf16[512,128]{1,0:T(8,128)(2,1)S(1)}, bf16[512,128]{1,0:T(8,128)(2,1)S(1)}, u32[]{:S(2)}, u32[]{:S(2)}) collective-permute-start(bf16[512,128]{1,0:T(8,128)(2,1)S(1)} %add_convert_fusion.mine_ref), channel_id=1, source_target_pairs={{0,64},{1,129},{2,66},{3,131},{4,68},{5,133},{6,70},{7,135},{8,72}... | collective-permute-start | bytes 393224 | tf_op jit(solution)/shard_map/ppermute | solution.py:249
  66.7 5.2 %collective-permute-done.2.other_ref = bf16[512,128]{1,0:T(8,128)(2,1)S(1)} collective-permute-done((bf16[512,128]{1,0:T(8,128)(2,1)S(1)}, bf16[512,128]{1,0:T(8,128)(2,1)S(1)}, u32[]{:S(2)}, u32[]{:S(2)}) %collective-permute-start.2) | collective-permute-done | bytes 131104 | tf_op jit(solution)/shard_map/ppermute | solution.py:249
  71.9 0.0 all-to-all-done.1.y_ref
  71.9 0.0 copy-done.2
  72.0 1.0 %shard_map.158 = (bf16[1,128,512]{2,1,0:T(8,128)(2,1)}, bf16[1,128,512]{2,1,0:T(8,128)(2,1)}, bf16[1,128,512]{2,1,0:T(8,128)(2,1)}, bf16[1,128,512]{2,1,0:T(8,128)(2,1)}, f32[512,128]{1,0:T(8,128)}) custom-call(bf16[64,16,128]{2,1,0:T(8,128)(2,1)S(1)} %all-to-all-done.1.y_ref, bf16[512,128]{1,0:T(8,128)(2,1)S(1)} %add_convert_fusion.mine_ref, ...), custom_call_target="tpu_custom_call" | custom-call | tf_op jit(solution)/shard_map/pallas_call | solution.py:258
  (9 shorter events, 0.1 us)
Async XLA Ops:
  2.6 17.3 %copy-start.11 = (f32[8192,8]{0,1:T(8,128)S(1)}, f32[8192,8]{0,1:T(8,128)}, u32[]{:S(2)}) copy-start(f32[8192,8]{0,1:T(8,128)} %param.15) | copy-start | bytes 786436
  2.6 36.1 %all-to-all-start = ((bf16[64,16,128]{2,1,0:T(8,128)(2,1)}), bf16[64,16,128]{2,1,0:T(8,128)(2,1)S(1)}, u32[]{:S(2)}, u32[]{:S(2)}) async-start(bf16[64,16,128]{2,1,0:T(8,128)(2,1)} %shard_map.155), calls=%async_computation | async-start | bytes 524288 | tf_op jit(solution)/shard_map/all_to_all | solution.py:218
  19.9 0.9 %copy-start = (bf16[256,256]{1,0:T(8,128)(2,1)S(1)}, bf16[256,256]{1,0:T(8,128)(2,1)}, u32[]{:S(2)}) copy-start(bf16[256,256]{1,0:T(8,128)(2,1)} %constant.18.clone.refs_5_.refs_7_) | copy-start | bytes 393220
  19.9 1.0 %copy-start.1 = (bf16[256,256]{1,0:T(8,128)(2,1)S(1)}, bf16[256,256]{1,0:T(8,128)(2,1)}, u32[]{:S(2)}) copy-start(bf16[256,256]{1,0:T(8,128)(2,1)} %constant.17.clone.refs_4_.refs_6_) | copy-start | bytes 393220
  19.9 1.0 %copy-start.6 = (f32[64,128]{1,0:T(8,128)S(1)}, f32[64,128]{1,0:T(8,128)}, u32[]{:S(2)}) copy-start(f32[64,128]{1,0:T(8,128)} %constant.16.clone.refs_3_.refs_5_) | copy-start | bytes 98308
  19.9 0.9 %copy-start.7 = (f32[64,128]{1,0:T(8,128)S(1)}, f32[64,128]{1,0:T(8,128)}, u32[]{:S(2)}) copy-start(f32[64,128]{1,0:T(8,128)} %constant.15.clone.refs_2_.refs_4_) | copy-start | bytes 98308
  19.9 1.0 %copy-start.9 = (bf16[128,192]{1,0:T(8,128)(2,1)S(1)}, bf16[128,192]{1,0:T(8,128)(2,1)}, u32[]{:S(2)}) copy-start(bf16[128,192]{1,0:T(8,128)(2,1)} %constant.14.clone.refs_1_) | copy-start | bytes 147460
  20.9 17.8 %copy-start.8 = (bf16[128,256]{1,0:T(8,128)(2,1)S(1)}, bf16[128,256]{1,0:T(8,128)(2,1)}, u32[]{:S(2)}) copy-start(bf16[128,256]{1,0:T(8,128)(2,1)} %constant.20.clone.refs_3_) | copy-start | bytes 196612
  20.9 17.8 %copy-start.10 = (bf16[128,128]{1,0:T(8,128)(2,1)S(1)}, bf16[128,128]{1,0:T(8,128)(2,1)}, u32[]{:S(2)}) copy-start(bf16[128,128]{1,0:T(8,128)(2,1)} %constant.19.clone.refs_2_) | copy-start | bytes 98308
  41.1 30.9 %all-to-all-start.1 = ((bf16[64,16,128]{2,1,0:T(8,128)(2,1)}), bf16[64,16,128]{2,1,0:T(8,128)(2,1)S(1)}, u32[]{:S(2)}, u32[]{:S(2)}) async-start(bf16[64,16,128]{2,1,0:T(8,128)(2,1)} %get-tuple-element.12), calls=%async_computation.1 | async-start | bytes 524288 | tf_op jit(solution)/shard_map/all_to_all | solution.py:243
  48.4 6.9 %collective-permute-start = (bf16[512,128]{1,0:T(8,128)(2,1)S(1)}, bf16[512,128]{1,0:T(8,128)(2,1)S(1)}, u32[]{:S(2)}, u32[]{:S(2)}) collective-permute-start(bf16[512,128]{1,0:T(8,128)(2,1)S(1)} %get-tuple-element.13), channel_id=1, source_target_pairs={{0,128},{1,385},{2,130},{3,387},{4,132},{5,389},{6,134},{7,391},{8... | collective-permute-start | bytes 393224 | tf_op jit(solution)/shard_map/ppermute | solution.py:249
  55.2 16.7 %copy-start.5 = (bf16[1,128,512]{2,1,0:T(8,128)(2,1)S(1)}, bf16[1,128,512]{2,1,0:T(8,128)(2,1)}, u32[]{:S(2)}) copy-start(bf16[1,128,512]{2,1,0:T(8,128)(2,1)} %g_ref.1) | copy-start | bytes 393220
  55.3 16.7 %copy-start.2 = (bf16[1,128,512]{2,1,0:T(8,128)(2,1)S(1)}, bf16[1,128,512]{2,1,0:T(8,128)(2,1)}, u32[]{:S(2)}) copy-start(bf16[1,128,512]{2,1,0:T(8,128)(2,1)} %q_ref.1) | copy-start | bytes 393220
  55.3 16.7 %copy-start.3 = (bf16[1,128,512]{2,1,0:T(8,128)(2,1)S(1)}, bf16[1,128,512]{2,1,0:T(8,128)(2,1)}, u32[]{:S(2)}) copy-start(bf16[1,128,512]{2,1,0:T(8,128)(2,1)} %k_ref.1) | copy-start | bytes 393220
  55.3 16.7 %copy-start.4 = (bf16[1,128,512]{2,1,0:T(8,128)(2,1)S(1)}, bf16[1,128,512]{2,1,0:T(8,128)(2,1)}, u32[]{:S(2)}) copy-start(bf16[1,128,512]{2,1,0:T(8,128)(2,1)} %v_ref.1) | copy-start | bytes 393220
  55.3 8.2 %collective-permute-start.1 = (bf16[512,128]{1,0:T(8,128)(2,1)S(1)}, bf16[512,128]{1,0:T(8,128)(2,1)S(1)}, u32[]{:S(2)}, u32[]{:S(2)}) collective-permute-start(bf16[512,128]{1,0:T(8,128)(2,1)S(1)} %add_convert_fusion.1), channel_id=1, source_target_pairs={{0,384},{1,65},{2,386},{3,67},{4,388},{5,69},{6,390},{7,71},{8,392... | collective-permute-start | bytes 393224 | tf_op jit(solution)/shard_map/ppermute | solution.py:249
  63.6 8.4 %collective-permute-start.2 = (bf16[512,128]{1,0:T(8,128)(2,1)S(1)}, bf16[512,128]{1,0:T(8,128)(2,1)S(1)}, u32[]{:S(2)}, u32[]{:S(2)}) collective-permute-start(bf16[512,128]{1,0:T(8,128)(2,1)S(1)} %add_convert_fusion.mine_ref), channel_id=1, source_target_pairs={{0,64},{1,129},{2,66},{3,131},{4,68},{5,133},{6,70},{7,135},{8,72}... | collective-permute-start | bytes 393224 | tf_op jit(solution)/shard_map/ppermute | solution.py:249

commit v9 on v7

--- a/solution.py
+++ b/solution.py
@@ -152,7 +152,9 @@
                 wide_ref[pl.ds(field, blocks, stride=fields), :] = y
             else:
                 wide_taps_ref[pl.ds(field - fields, blocks, stride=share), :] = y
-    y_ref[...] = wide_ref[...].reshape(blocks, fields, lanes).astype(BF)
+    ys = wide_ref[...].reshape(blocks, fields, lanes).astype(BF)
+    for place, block in enumerate(spread(blocks)[::PLANE]):
+        y_ref[place * PLANE:(place + 1) * PLANE] = ys[block:block + PLANE]
     taps_ref[...] = wide_taps_ref[...].astype(BF)
 
 
@@ -186,7 +188,8 @@
     taps_ref[...] = mine_ref[...].astype(F32) + other_ref[...].astype(F32)
     groups, fields, lanes = y_ref.shape
     share = fields // 2
-    both = y_ref[...].astype(F32)
+    places = np.argsort(spread(groups)[::PLANE]) * PLANE
+    both = jnp.concatenate([y_ref[int(place):int(place) + PLANE] for place in places], axis=0).astype(F32)
     conv = both[:, :share].reshape(groups * share, lanes).T
     back = both[:, share:].reshape(groups * share, lanes).T
     go_ref[0] = (q_ref[0].astype(F32) * conv).astype(BF)
@@ -240,7 +243,7 @@
         ],
         compiler_params=PARAMS,
     )(both, filt_spec, t["into"], t["out"], t["turn_cos"], t["turn_sin"], t["g_high"], t["g_low"])
-    out = lax.all_to_all(out, "ctx", 0, 0)
+    out = lax.all_to_all(out, "ctx", 0, 0, axis_index_groups=[spread(groups)])
 
     def swap(part, flips):
         pairs = [

time: 73.4 us -> 73.4 us (level)
  no operation moved by 1% of the time
where the time goes in v9:
time: 73.4 us; the launch traced here: 73 us
  starting transfers between devices  36.7 us (50%)
  waiting for transfers between devices  28.5 us (39%)
  Pallas kernels  5.87 us (8%)
  local copies, waits for them, and re-layouts  0.99 us (1%)
  between operations  0.81 us (1%)
    all_to_all x1, starting transfers between devices, on_device(): both = lax.all_to_all(both, 'ctx', 0, 0, axis_index_groups=[spread(groups)])  17.2 us
    all_to_all x1, waiting for transfers between devices, on_device(): both = lax.all_to_all(both, 'ctx', 0, 0, axis_index_groups=[spread(groups)])  16.5 us
    ppermute x3, waiting for transfers between devices, swap(): return lax.ppermute(part, ('dp', 'ctx'), pairs)  12.1 us
    ppermute x3, starting transfers between devices, swap(): return lax.ppermute(part, ('dp', 'ctx'), pairs)  11.3 us
    all_to_all x1, starting transfers between devices, on_device(): out = lax.all_to_all(out, 'ctx', 0, 0, axis_index_groups=[spread(groups)])  8.15 us
    pallas_call x1, Pallas kernels, on_device(): pl.pallas_call(lambda *refs: conv_kernel(factor * 2.0 / (2 * seq_len), *r...  2.39 us
    pallas_call x1, Pallas kernels, on_device(): pl.pallas_call(mix_kernel, out_shape=jax.ShapeDtypeStruct((groups, 2 * sh...  1.94 us
  transfers between devices with their start and end apart: 5, of which 4 were waited for; matrix products, arithmetic and copies ran while one was open for 0% of the time, Pallas kernels for 1%

profile of v9, /device:TPU:24, one launch (start us, length us, event | category | flops | bytes accessed | tf_op | source)
XLA Modules:
  0.0 73.0 jit_solution(3476962204465677696)
XLA Ops:
  0.6 1.9 %shard_map.155 = bf16[64,16,128]{2,1,0:T(8,128)(2,1)} custom-call(bf16[1,128,512]{2,1,0:T(8,128)(2,1)} %q_ref.1, bf16[1,128,512]{2,1,0:T(8,128)(2,1)} %k_ref.1, bf16[1,128,512]{2,1,0:T(8,128)(2,1)} %v_ref.1, bf16[1,128,512]{2,1,0:T(8,128)(2,1)} %g_ref.1), custom_call_target="tpu_custom_call" | custom-call | tf_op jit(solution)/shard_map/pallas_call | solution.py:214
  2.6 0.0 copy-start.11
  2.6 17.2 %all-to-all-start = ((bf16[64,16,128]{2,1,0:T(8,128)(2,1)}), bf16[64,16,128]{2,1,0:T(8,128)(2,1)S(1)}, u32[]{:S(2)}, u32[]{:S(2)}) async-start(bf16[64,16,128]{2,1,0:T(8,128)(2,1)} %shard_map.155), calls=%async_computation | async-start | bytes 524288 | tf_op jit(solution)/shard_map/all_to_all | solution.py:221
  19.8 0.0 copy-done.11
  19.9 0.0 copy-start
  19.9 0.0 copy-start.1
  19.9 0.0 copy-start.6
  19.9 0.0 copy-start.7
  19.9 0.0 copy-start.9
  19.9 0.1 copy.19
  20.0 0.8 %copy-done = bf16[256,256]{1,0:T(8,128)(2,1)S(1)} copy-done((bf16[256,256]{1,0:T(8,128)(2,1)S(1)}, bf16[256,256]{1,0:T(8,128)(2,1)}, u32[]{:S(2)}) %copy-start) | copy-done | bytes 131096
  20.8 0.1 copy-done.1
  20.8 0.0 copy-done.6
  20.8 0.0 copy-done.7
  20.8 0.0 copy-done.9
  20.9 0.5 shard_map.156.refs_1_
  21.4 16.5 %all-to-all-done.refs_0_ = bf16[64,16,128]{2,1,0:T(8,128)(2,1)S(1)} async-done(((bf16[64,16,128]{2,1,0:T(8,128)(2,1)}), bf16[64,16,128]{2,1,0:T(8,128)(2,1)S(1)}, u32[]{:S(2)}, u32[]{:S(2)}) %all-to-all-start) | async-done | bytes 262176 | tf_op jit(solution)/shard_map/all_to_all | solution.py:221
  37.9 0.0 copy-done.8
  37.9 0.0 copy-done.10
  37.9 2.4 %shard_map.157 = (bf16[64,16,128]{2,1,0:T(8,128)(2,1)}, bf16[512,128]{1,0:T(8,128)(2,1)S(1)}) custom-call(bf16[64,16,128]{2,1,0:T(8,128)(2,1)S(1)} %all-to-all-done.refs_0_, f32[512,256]{1,0:T(8,128)S(1)} %shard_map.156.refs_1_, bf16[128,128]{1,0:T(8,128)(2,1)S(1)} %copy-done.10, bf16[128,256]{1,0:T(8,128)(2,1)S(1)} %copy-done.8, f32[64,128]{1,0:T(8,128)S(1)} %copy-done.7, ...), custom_call_target="tpu_custom_call" | custom-call | tf_op jit(solution)/shard_map/pallas_call | solution.py:230
  40.3 8.1 %all-to-all-start.1 = ((bf16[64,16,128]{2,1,0:T(8,128)(2,1)}), bf16[64,16,128]{2,1,0:T(8,128)(2,1)S(1)}, u32[]{:S(2)}, u32[]{:S(2)}) async-start(bf16[64,16,128]{2,1,0:T(8,128)(2,1)} %get-tuple-element.12), calls=%async_computation.1 | async-start | bytes 524288 | tf_op jit(solution)/shard_map/all_to_all | solution.py:246
  48.4 3.4 %collective-permute-start = (bf16[512,128]{1,0:T(8,128)(2,1)S(1)}, bf16[512,128]{1,0:T(8,128)(2,1)S(1)}, u32[]{:S(2)}, u32[]{:S(2)}) collective-permute-start(bf16[512,128]{1,0:T(8,128)(2,1)S(1)} %get-tuple-element.13), channel_id=1, source_target_pairs={{0,128},{1,385},{2,130},{3,387},{4,132},{5,389},{6,134},{7,391},{8... | collective-permute-start | bytes 393224 | tf_op jit(solution)/shard_map/ppermute | solution.py:252
  51.8 3.5 %collective-permute-done = bf16[512,128]{1,0:T(8,128)(2,1)S(1)} collective-permute-done((bf16[512,128]{1,0:T(8,128)(2,1)S(1)}, bf16[512,128]{1,0:T(8,128)(2,1)S(1)}, u32[]{:S(2)}, u32[]{:S(2)}) %collective-permute-start) | collective-permute-done | bytes 131104 | tf_op jit(solution)/shard_map/ppermute | solution.py:252
  55.3 0.0 copy-start.2
  55.3 0.0 copy-start.3
  55.4 0.0 copy-start.4
  55.4 4.8 %collective-permute-start.1 = (bf16[512,128]{1,0:T(8,128)(2,1)S(1)}, bf16[512,128]{1,0:T(8,128)(2,1)S(1)}, u32[]{:S(2)}, u32[]{:S(2)}) collective-permute-start(bf16[512,128]{1,0:T(8,128)(2,1)S(1)} %add_convert_fusion.1), channel_id=1, source_target_pairs={{0,384},{1,65},{2,386},{3,67},{4,388},{5,69},{6,390},{7,71},{8,392... | collective-permute-start | bytes 393224 | tf_op jit(solution)/shard_map/ppermute | solution.py:252
  60.2 3.4 %collective-permute-done.1 = bf16[512,128]{1,0:T(8,128)(2,1)S(1)} collective-permute-done((bf16[512,128]{1,0:T(8,128)(2,1)S(1)}, bf16[512,128]{1,0:T(8,128)(2,1)S(1)}, u32[]{:S(2)}, u32[]{:S(2)}) %collective-permute-start.1) | collective-permute-done | bytes 131104 | tf_op jit(solution)/shard_map/ppermute | solution.py:252
  63.6 3.1 %collective-permute-start.2 = (bf16[512,128]{1,0:T(8,128)(2,1)S(1)}, bf16[512,128]{1,0:T(8,128)(2,1)S(1)}, u32[]{:S(2)}, u32[]{:S(2)}) collective-permute-start(bf16[512,128]{1,0:T(8,128)(2,1)S(1)} %add_convert_fusion.mine_ref), channel_id=1, source_target_pairs={{0,64},{1,129},{2,66},{3,131},{4,68},{5,133},{6,70},{7,135},{8,72}... | collective-permute-start | bytes 393224 | tf_op jit(solution)/shard_map/ppermute | solution.py:252
  66.8 5.2 %collective-permute-done.2.other_ref = bf16[512,128]{1,0:T(8,128)(2,1)S(1)} collective-permute-done((bf16[512,128]{1,0:T(8,128)(2,1)S(1)}, bf16[512,128]{1,0:T(8,128)(2,1)S(1)}, u32[]{:S(2)}, u32[]{:S(2)}) %collective-permute-start.2) | collective-permute-done | bytes 131104 | tf_op jit(solution)/shard_map/ppermute | solution.py:252
  72.0 0.0 all-to-all-done.1.y_ref
  72.0 1.0 %shard_map.158 = (bf16[1,128,512]{2,1,0:T(8,128)(2,1)}, bf16[1,128,512]{2,1,0:T(8,128)(2,1)}, bf16[1,128,512]{2,1,0:T(8,128)(2,1)}, bf16[1,128,512]{2,1,0:T(8,128)(2,1)}, f32[512,128]{1,0:T(8,128)}) custom-call(bf16[64,16,128]{2,1,0:T(8,128)(2,1)S(1)} %all-to-all-done.1.y_ref, bf16[512,128]{1,0:T(8,128)(2,1)S(1)} %add_convert_fusion.mine_ref, ...), custom_call_target="tpu_custom_call" | custom-call | tf_op jit(solution)/shard_map/pallas_call | solution.py:261
  (9 shorter events, 0.1 us)
Async XLA Ops:
  2.6 17.3 %copy-start.11 = (f32[8192,8]{0,1:T(8,128)S(1)}, f32[8192,8]{0,1:T(8,128)}, u32[]{:S(2)}) copy-start(f32[8192,8]{0,1:T(8,128)} %param.15) | copy-start | bytes 786436
  2.6 35.3 %all-to-all-start = ((bf16[64,16,128]{2,1,0:T(8,128)(2,1)}), bf16[64,16,128]{2,1,0:T(8,128)(2,1)S(1)}, u32[]{:S(2)}, u32[]{:S(2)}) async-start(bf16[64,16,128]{2,1,0:T(8,128)(2,1)} %shard_map.155), calls=%async_computation | async-start | bytes 524288 | tf_op jit(solution)/shard_map/all_to_all | solution.py:221
  19.9 0.9 %copy-start = (bf16[256,256]{1,0:T(8,128)(2,1)S(1)}, bf16[256,256]{1,0:T(8,128)(2,1)}, u32[]{:S(2)}) copy-start(bf16[256,256]{1,0:T(8,128)(2,1)} %constant.18.clone.refs_5_.refs_7_) | copy-start | bytes 393220
  19.9 1.0 %copy-start.1 = (bf16[256,256]{1,0:T(8,128)(2,1)S(1)}, bf16[256,256]{1,0:T(8,128)(2,1)}, u32[]{:S(2)}) copy-start(bf16[256,256]{1,0:T(8,128)(2,1)} %constant.17.clone.refs_4_.refs_6_) | copy-start | bytes 393220
  19.9 1.0 %copy-start.6 = (f32[64,128]{1,0:T(8,128)S(1)}, f32[64,128]{1,0:T(8,128)}, u32[]{:S(2)}) copy-start(f32[64,128]{1,0:T(8,128)} %constant.16.clone.refs_3_.refs_5_) | copy-start | bytes 98308
  19.9 0.9 %copy-start.7 = (f32[64,128]{1,0:T(8,128)S(1)}, f32[64,128]{1,0:T(8,128)}, u32[]{:S(2)}) copy-start(f32[64,128]{1,0:T(8,128)} %constant.15.clone.refs_2_.refs_4_) | copy-start | bytes 98308
  19.9 1.0 %copy-start.9 = (bf16[128,192]{1,0:T(8,128)(2,1)S(1)}, bf16[128,192]{1,0:T(8,128)(2,1)}, u32[]{:S(2)}) copy-start(bf16[128,192]{1,0:T(8,128)(2,1)} %constant.14.clone.refs_1_) | copy-start | bytes 147460
  20.9 17.0 %copy-start.8 = (bf16[128,256]{1,0:T(8,128)(2,1)S(1)}, bf16[128,256]{1,0:T(8,128)(2,1)}, u32[]{:S(2)}) copy-start(bf16[128,256]{1,0:T(8,128)(2,1)} %constant.20.clone.refs_3_) | copy-start | bytes 196612
  20.9 17.0 %copy-start.10 = (bf16[128,128]{1,0:T(8,128)(2,1)S(1)}, bf16[128,128]{1,0:T(8,128)(2,1)}, u32[]{:S(2)}) copy-start(bf16[128,128]{1,0:T(8,128)(2,1)} %constant.19.clone.refs_2_) | copy-start | bytes 98308
  40.3 31.7 %all-to-all-start.1 = ((bf16[64,16,128]{2,1,0:T(8,128)(2,1)}), bf16[64,16,128]{2,1,0:T(8,128)(2,1)S(1)}, u32[]{:S(2)}, u32[]{:S(2)}) async-start(bf16[64,16,128]{2,1,0:T(8,128)(2,1)} %get-tuple-element.12), calls=%async_computation.1 | async-start | bytes 524288 | tf_op jit(solution)/shard_map/all_to_all | solution.py:246
  48.4 6.9 %collective-permute-start = (bf16[512,128]{1,0:T(8,128)(2,1)S(1)}, bf16[512,128]{1,0:T(8,128)(2,1)S(1)}, u32[]{:S(2)}, u32[]{:S(2)}) collective-permute-start(bf16[512,128]{1,0:T(8,128)(2,1)S(1)} %get-tuple-element.13), channel_id=1, source_target_pairs={{0,128},{1,385},{2,130},{3,387},{4,132},{5,389},{6,134},{7,391},{8... | collective-permute-start | bytes 393224 | tf_op jit(solution)/shard_map/ppermute | solution.py:252
  55.3 16.7 %copy-start.5 = (bf16[1,128,512]{2,1,0:T(8,128)(2,1)S(1)}, bf16[1,128,512]{2,1,0:T(8,128)(2,1)}, u32[]{:S(2)}) copy-start(bf16[1,128,512]{2,1,0:T(8,128)(2,1)} %g_ref.1) | copy-start | bytes 393220
  55.3 16.7 %copy-start.2 = (bf16[1,128,512]{2,1,0:T(8,128)(2,1)S(1)}, bf16[1,128,512]{2,1,0:T(8,128)(2,1)}, u32[]{:S(2)}) copy-start(bf16[1,128,512]{2,1,0:T(8,128)(2,1)} %q_ref.1) | copy-start | bytes 393220
  55.3 16.6 %copy-start.3 = (bf16[1,128,512]{2,1,0:T(8,128)(2,1)S(1)}, bf16[1,128,512]{2,1,0:T(8,128)(2,1)}, u32[]{:S(2)}) copy-start(bf16[1,128,512]{2,1,0:T(8,128)(2,1)} %k_ref.1) | copy-start | bytes 393220
  55.4 16.6 %copy-start.4 = (bf16[1,128,512]{2,1,0:T(8,128)(2,1)S(1)}, bf16[1,128,512]{2,1,0:T(8,128)(2,1)}, u32[]{:S(2)}) copy-start(bf16[1,128,512]{2,1,0:T(8,128)(2,1)} %v_ref.1) | copy-start | bytes 393220
  55.4 8.2 %collective-permute-start.1 = (bf16[512,128]{1,0:T(8,128)(2,1)S(1)}, bf16[512,128]{1,0:T(8,128)(2,1)S(1)}, u32[]{:S(2)}, u32[]{:S(2)}) collective-permute-start(bf16[512,128]{1,0:T(8,128)(2,1)S(1)} %add_convert_fusion.1), channel_id=1, source_target_pairs={{0,384},{1,65},{2,386},{3,67},{4,388},{5,69},{6,390},{7,71},{8,392... | collective-permute-start | bytes 393224 | tf_op jit(solution)/shard_map/ppermute | solution.py:252
  63.6 8.4 %collective-permute-start.2 = (bf16[512,128]{1,0:T(8,128)(2,1)S(1)}, bf16[512,128]{1,0:T(8,128)(2,1)S(1)}, u32[]{:S(2)}, u32[]{:S(2)}) collective-permute-start(bf16[512,128]{1,0:T(8,128)(2,1)S(1)} %add_convert_fusion.mine_ref), channel_id=1, source_target_pairs={{0,64},{1,129},{2,66},{3,131},{4,68},{5,133},{6,70},{7,135},{8,72}... | collective-permute-start | bytes 393224 | tf_op jit(solution)/shard_map/ppermute | solution.py:252
